TPU v7x, 128 devices: a whole 4x4x4 slice. The times are simulated.
128 devices in a mesh: rows: 8 (over z, y_hi), heads: 16 (over y_lo, x, core).
Axes of the slice: x: 4, y: 4 (y_hi: 2, y_lo: 2; y = y_hi * 2 + y_lo), z: 4, core: 2. Of those that a mesh axis runs over, the one named last changes fastest.
Arguments:
- x_forward: bfloat16 [128, 256, 1152], P('rows', 'heads'), may hold values from -24 to 24
- x_backward: bfloat16 [128, 256, 1152], P('rows', 'heads'), may hold values from -24 to 24
- grad_out: bfloat16 [128, 256, 1152], P('rows', 'heads'), may hold values from -6 to 6
- w_qkv: bfloat16 [1152, 3456], replicated, may hold values from -0.1875 to 0.1875
- w_out: bfloat16 [1152, 1152], replicated, may hold values from -0.1875 to 0.1875
Outputs:
- y_forward: bfloat16 [128, 256, 1152], P('rows', 'heads')
- dx_backward: bfloat16 [128, 256, 1152], P('rows', 'heads')
All inputs are finite; a program needn't handle non-finite values.
Results may differ from a plain program's by a relative error of at most 0.015.
The roundings to bfloat16 on the way count: a program that leaves them out, or rounds other values in their place, can miss the bound.
Values may be sent and summed in bfloat16 or wider, within the bound.
No kernel may reach another device: no remote copies, remote signals or barrier semaphores. Data moves between devices by JAX's collectives and lax.ppermute only.
A program may use at most 192 MiB of HBM per device.

v0:
```python
import functools
import math

import jax
import jax.numpy as jnp
from jax import lax
from jax.experimental import pallas as pl
from jax.experimental.pallas import tpu as pltpu
from jax.sharding import PartitionSpec as P

RADIUS = 7
SIDE = 16
LANES = 256
GROUP = 256
HALF = 128
SPAN = 3 * GROUP
KEYS = 4 * GROUP
NEG = -1e30
CHUNK = 16
LIMIT = 40 * 2**20


def shifted(value, axis, step):
    count = lax.axis_size(axis)
    return lax.ppermute(value, axis, [(i, (i + step) % count) for i in range(count)])


def row_halos(x):
    return shifted(x[SIDE - RADIUS :], "rows", 1), x, shifted(x[:RADIUS], "rows", -1)


def column_sends(parts):
    zeros = jnp.zeros((2, 8) + parts[0].shape[2:], parts[0].dtype)
    return [jnp.concatenate([part[:, side] for part in parts] + [zeros], 0) for side in (slice(8, 16), slice(0, 8))]


def side_columns(sends):
    return jnp.concatenate([shifted(sends[0], "heads", 1), shifted(sends[1], "heads", -1)], 1)


def window_bias():
    row_start = lax.axis_index("rows") * SIDE
    col_start = lax.axis_index("heads") * SIDE
    rows_total = lax.axis_size("rows") * SIDE
    cols_total = lax.axis_size("heads") * SIDE
    query = lax.broadcasted_iota(jnp.int32, (2 * HALF, SPAN), 0)
    place = lax.broadcasted_iota(jnp.int32, (2 * HALF, SPAN), 1)
    half = query // HALF
    query_row, query_col = query // SIDE, query % SIDE
    group, rest = place // GROUP + half, place % GROUP
    side, inner = rest // HALF, rest % HALF
    key_row, column = group * 8 + inner // SIDE, inner % SIDE
    key_col = jnp.where(side == 0, column, jnp.where(column < 8, column - 8, column + 8))
    image_row = row_start + key_row - RADIUS
    image_col = col_start + key_col
    row_gap, col_gap = key_row - query_row, key_col - query_col
    valid = (row_gap >= 0) & (row_gap <= 2 * RADIUS) & (col_gap >= -RADIUS) & (col_gap <= RADIUS)
    valid &= (image_row >= 0) & (image_row < rows_total) & (image_col >= 0) & (image_col < cols_total)
    return jnp.where(valid, 0.0, NEG).astype(jnp.float32)


def head_lanes(head, head_dim, width):
    tile = jnp.clip(head * head_dim // 128, 0, (width - LANES) // 128)
    offset = head * head_dim - tile * 128
    lane = lax.broadcasted_iota(jnp.int32, (1, LANES), 1)
    return tile * 128, (lane >= offset) & (lane < offset + head_dim)


def at_lanes(start):
    return pl.ds(pl.multiple_of(start, 128), LANES)


def own_keys_kernel(above, own, below, weights, out_ref):
    skip = weights.shape[1] - out_ref.shape[1]
    for start in range(0, out_ref.shape[1], GROUP):
        low = 0
        for x_ref in (above, own, below):
            part = jnp.dot(
                x_ref[...], weights[:, skip + start : skip + start + GROUP], preferred_element_type=jnp.float32
            )
            out_ref[low : low + x_ref.shape[0], start : start + GROUP] = part.astype(out_ref.dtype)
            low += x_ref.shape[0]
        out_ref[low:, start : start + GROUP] = jnp.zeros((out_ref.shape[0] - low, GROUP), out_ref.dtype)


def own_gradient_kernel(dkv, dq, weights, out_ref):
    width = dq.shape[1]
    for start in range(0, out_ref.shape[0], GROUP):
        part = jnp.dot(weights[:, width:], dkv[:, start : start + GROUP], preferred_element_type=jnp.float32)
        out_ref[start : start + GROUP, :] = jnp.transpose(part)
    mine = slice(RADIUS * SIDE, RADIUS * SIDE + dq.shape[0])
    out_ref[mine, :] += lax.dot_general(
        dq[...], weights[:, :width], (((1,), (1,)), ((), ())), preferred_element_type=jnp.float32
    )


def fill_keys(kv_own, x_side, weights, kv):
    skip = weights.shape[1] - kv.shape[1]
    for group in range(4):
        kv[GROUP * group : GROUP * group + HALF, :] = kv_own[HALF * group : HALF * (group + 1), :]
    for start in range(0, kv.shape[1], GROUP):
        part = jnp.dot(
            x_side[...], weights[:, skip + start : skip + start + GROUP], preferred_element_type=jnp.float32
        ).astype(kv.dtype)
        for group in range(4):
            low = GROUP * group + HALF
            kv[low : low + HALF, start : start + GROUP] = part[HALF * group : HALF * (group + 1)]


def turned(source, target):
    heads, head_dim, _ = target.shape
    flipped = jnp.transpose(source[...].astype(jnp.float32))
    for head in range(heads):
        target[head] = flipped[head * head_dim : (head + 1) * head_dim].astype(target.dtype)


def span_products(rows, kv, start, out_ref):
    def one(group):
        low = 0 if group < 3 else HALF
        high = 2 * HALF if group > 0 else HALF
        keys = kv[GROUP * group : GROUP * (group + 1), at_lanes(start)]
        part = lax.dot_general(
            rows[low:high], keys, (((1,), (1,)), ((), ())), preferred_element_type=jnp.float32
        )
        if group < 3:
            out_ref[:HALF, GROUP * group : GROUP * (group + 1)] = part[:HALF]
        if group > 0:
            out_ref[HALF:, GROUP * (group - 1) : GROUP * group] = part[-HALF:]

    return [functools.partial(one, group) for group in range(4)]


def interleave(*streams):
    marks = [((i + 0.5) / len(stream), n, step) for n, stream in enumerate(streams) for i, step in enumerate(stream)]
    for _, _, step in sorted(marks, key=lambda mark: mark[:2]):
        step()


def softmax_rows(scores, bias, factor):
    scores = scores + bias
    top = jnp.max(scores, axis=1, keepdims=True)
    terms = jnp.exp2((scores - top) * factor)
    return terms * (1.0 / jnp.sum(terms, axis=1, keepdims=True))


def span_of(rows):
    start = 0 if rows < HALF else GROUP
    return slice(start, start + SPAN)


def forward_kernel(
    head_dim, kv_own, x_side, weights, w_out, queries, bias, out_ref, kv, acc, scores0, scores1, probs0, probs1
):
    width = queries.shape[1]
    heads = width // head_dim
    factor = head_dim**-0.5 * math.log2(math.e)
    scores, probs = (scores0, scores1), (probs0, probs1)
    for ref in probs + (acc,):
        ref[...] = jnp.zeros_like(ref)
    fill_keys(kv_own, x_side, weights, kv)

    def scored(head, u):
        start, mask = head_lanes(head, head_dim, width)
        return span_products(jnp.where(mask, queries[:, at_lanes(start)], 0), kv, start, scores[u])

    def weighted(u):
        def one(rows):
            part = slice(rows, rows + CHUNK)
            attention = softmax_rows(scores[u][part, :], bias[part, :], factor)
            probs[u][part, span_of(rows)] = attention.astype(jnp.bfloat16)

        return [functools.partial(one, rows) for rows in range(0, 2 * HALF, CHUNK)]

    def mixed(head, u):
        start, mask = head_lanes(head, head_dim, width)

        def one():
            mix = jnp.dot(probs[u][...], kv[:, at_lanes(start + width)], preferred_element_type=jnp.float32)
            acc[:, at_lanes(start)] += jnp.where(mask & (head >= 0), mix, 0.0)

        return [one]

    interleave(scored(0, 0))

    def pair(index, carry):
        head = 2 * index
        interleave(scored(head + 1, 1), weighted(0), mixed(head - 1, 1))
        interleave(scored(jnp.minimum(head + 2, heads - 1), 0), weighted(1), mixed(head, 0))
        return carry

    lax.fori_loop(0, heads // 2, pair, 0)
    interleave(mixed(heads - 1, 1))
    attended = acc[...].astype(jnp.bfloat16)
    out_ref[...] = jnp.dot(attended, w_out[...], preferred_element_type=jnp.float32).astype(out_ref.dtype)


def backward_kernel(
    head_dim, kv_own, x_side, weights, queries, cotangents, bias, down_ref, dq_ref, dside_ref,
    queries_t, cotangents_t, kv, dkv, acc,
    scores0, scores1, grads0, grads1, probs0, probs1, dscores0, dscores1, held0, held1
):
    width = queries.shape[1]
    heads = width // head_dim
    scaling = head_dim**-0.5
    factor = scaling * math.log2(math.e)
    scores, grads, held = (scores0, scores1), (grads0, grads1), (held0, held1)
    probs, dscores = (probs0, probs1), (dscores0, dscores1)
    for ref in probs + dscores + held + (acc,):
        ref[...] = jnp.zeros_like(ref)
    turned(queries, queries_t)
    turned(cotangents, cotangents_t)
    fill_keys(kv_own, x_side, weights, kv)

    def scored(head, u):
        start, mask = head_lanes(head, head_dim, width)
        one = span_products(jnp.where(mask, queries[:, at_lanes(start)], 0), kv, start, scores[u])
        other = span_products(jnp.where(mask, cotangents[:, at_lanes(start)], 0), kv, start + width, grads[u])
        return [step for both in zip(one, other) for step in both]

    def weighted(u):
        def one(rows):
            part = slice(rows, rows + CHUNK)
            attention = softmax_rows(scores[u][part, :], bias[part, :], factor)
            grad = grads[u][part, :]
            centre = jnp.sum(attention * grad, axis=1, keepdims=True)
            probs[u][part, span_of(rows)] = attention.astype(jnp.bfloat16)
            dscores[u][part, span_of(rows)] = (attention * (grad - centre) * scaling).astype(jnp.bfloat16)

        return [functools.partial(one, rows) for rows in range(0, 2 * HALF, CHUNK)]

    def spread(head, u):
        start, mask = head_lanes(head, head_dim, width)
        row = jnp.maximum(head, 0)
        base = jnp.maximum(head - 1, 0) * head_dim

        def query_part():
            dq = jnp.dot(dscores[u][...], kv[:, at_lanes(start)], preferred_element_type=jnp.float32)
            acc[:, at_lanes(start)] += jnp.where(mask & (head >= 0), dq, 0.0)

        def key_part(index, group):
            source, spans = ((queries_t, dscores), (cotangents_t, probs))[index]
            place = slice(GROUP * group, GROUP * (group + 1))
            part = jnp.dot(source[row], spans[u][:, place], preferred_element_type=jnp.float32)
            if u == 0:
                held[index][:, place] = part
            else:
                both = jnp.concatenate([held[index][:, place], part], 0).astype(jnp.bfloat16)
                rows = pl.ds(pl.multiple_of(base + index * width, 16), 2 * head_dim)
                place = slice(HALF * group, HALF * (group + 1))
                down_ref[rows, place] = both[:, :HALF]
                dkv[rows, place] = both[:, HALF:]

        parts = [functools.partial(key_part, index, group) for index in range(2) for group in range(4)]
        return parts[:4] + [query_part] + parts[4:]

    interleave(scored(0, 0))

    def pair(index, carry):
        head = 2 * index
        interleave(scored(head + 1, 1), weighted(0), spread(head - 1, 1))
        interleave(scored(jnp.minimum(head + 2, heads - 1), 0), weighted(1), spread(head, 0))
        return carry

    lax.fori_loop(0, heads // 2, pair, 0)
    interleave(spread(heads - 1, 1))

    dq_ref[...] = acc[...].astype(dq_ref.dtype)
    for start in range(0, dside_ref.shape[0], GROUP):
        part = jnp.dot(weights[:, width:], dkv[:, start : start + GROUP], preferred_element_type=jnp.float32)
        dside_ref[start : start + GROUP, :] = jnp.transpose(part).astype(dside_ref.dtype)


def call_kernel(kernel, args, out_shape, scratch, flops, name):
    return pl.pallas_call(
        kernel,
        out_shape=out_shape,
        scratch_shapes=scratch,
        compiler_params=pltpu.CompilerParams(vmem_limit_bytes=LIMIT),
        cost_estimate=pl.CostEstimate(flops=flops, bytes_accessed=16 * 2**20, transcendentals=2**22),
        name=name,
    )(*args)


def own_keys(x_parts, w_qkv):
    width, columns = w_qkv.shape
    out_shape = jax.ShapeDtypeStruct((KEYS // 2, columns - width), jnp.bfloat16)
    return call_kernel(own_keys_kernel, [*x_parts, w_qkv], out_shape, [], 2 * KEYS * width * width, "own_keys")


def own_gradient(dkv, dq, w_qkv):
    out_shape = jax.ShapeDtypeStruct((KEYS // 2, dq.shape[1]), jnp.float32)
    flops = 2 * KEYS * dq.shape[1] ** 2
    return call_kernel(own_gradient_kernel, [dkv, dq, w_qkv], out_shape, [], flops, "own_gradient")


def attention_forward(kv_own, x_side, w_qkv, w_out, queries, bias, heads):
    tokens, width = queries.shape
    half, full = jnp.bfloat16, jnp.float32
    square = (tokens, SPAN)
    scratch = [pltpu.VMEM((KEYS, 2 * width), half), pltpu.VMEM((tokens, width), full)]
    scratch += [pltpu.VMEM(square, full)] * 2 + [pltpu.VMEM((tokens, KEYS), half)] * 2
    return call_kernel(
        functools.partial(forward_kernel, width // heads),
        [kv_own, x_side, w_qkv, w_out, queries, bias],
        jax.ShapeDtypeStruct(queries.shape, half),
        scratch,
        2 * KEYS * width * width + 4 * heads * tokens * KEYS * LANES,
        "attention_forward",
    )


def attention_backward(kv_own, x_side, w_qkv, queries, cotangents, bias, heads):
    tokens, width = queries.shape
    head_dim = width // heads
    square = (tokens, SPAN)
    half, full = jnp.bfloat16, jnp.float32
    by_head = (heads, head_dim, tokens)
    scratch = [
        pltpu.VMEM(by_head, half),
        pltpu.VMEM(by_head, half),
        pltpu.VMEM((KEYS, 2 * width), half),
        pltpu.VMEM((2 * width, KEYS // 2), half),
        pltpu.VMEM((tokens, width), full),
    ]
    scratch += [pltpu.VMEM(square, full)] * 4 + [pltpu.VMEM((tokens, KEYS), half)] * 4
    scratch += [pltpu.VMEM((head_dim, KEYS), full)] * 2
    return call_kernel(
        functools.partial(backward_kernel, head_dim),
        [kv_own, x_side, w_qkv, queries, cotangents, bias],
        [
            jax.ShapeDtypeStruct((2 * width, KEYS // 2), half),
            jax.ShapeDtypeStruct(queries.shape, half),
            jax.ShapeDtypeStruct((KEYS // 2, width), half),
        ],
        scratch,
        4 * KEYS * width * width + 10 * heads * tokens * KEYS * LANES,
        "attention_backward",
    )


def project(x, w):
    return jnp.dot(x, w, preferred_element_type=jnp.float32).astype(jnp.bfloat16)


def body(x_forward, x_backward, grad_out, w_qkv, w_out):
    rows, cols, width = x_forward.shape
    heads = lax.axis_size("heads")
    w_q = w_qkv[:, :width]
    flat = lambda x: x.reshape(-1, width)
    bias = window_bias()

    parts_backward = row_halos(x_backward)
    q_backward = project(flat(x_backward), w_q)
    q_forward = project(flat(x_forward), w_q)
    grad_heads = lax.dot_general(
        flat(grad_out), w_out, (((1,), (1,)), ((), ())), preferred_element_type=jnp.float32
    ).astype(jnp.bfloat16)
    sends_backward, q_backward, q_forward, grad_heads, bias = lax.optimization_barrier(
        (column_sends(parts_backward), q_backward, q_forward, grad_heads, bias)
    )
    side_backward = flat(side_columns(sends_backward))
    x_forward, _ = lax.optimization_barrier((x_forward, sends_backward))
    parts_forward = row_halos(x_forward)
    parts_backward, _ = lax.optimization_barrier((parts_backward, sends_backward))
    own_backward = own_keys([flat(part) for part in parts_backward], w_qkv)

    dkv_own, dq, dx_side = attention_backward(
        own_backward, side_backward, w_qkv, q_backward, grad_heads, bias, heads
    )
    dx_side = dx_side.reshape(2 * SIDE, SIDE, width)
    from_right = shifted(dx_side[:, :8], "heads", -1)
    from_left = shifted(dx_side[:, 8:], "heads", 1)
    dx_own = own_gradient(dkv_own, dq, w_qkv).reshape(2 * SIDE, SIDE, width)
    parts_forward, _ = lax.optimization_barrier((parts_forward, dx_own))
    sends_forward = column_sends(parts_forward)
    side_forward = flat(side_columns(sends_forward))
    parts_forward, _ = lax.optimization_barrier((parts_forward, sends_forward))
    own_forward = own_keys([flat(part) for part in parts_forward], w_qkv)
    from_left, from_right, own_forward = lax.optimization_barrier((from_left, from_right, own_forward))
    total = dx_own + jnp.concatenate([from_left, from_right], 1).astype(jnp.float32)
    from_below = shifted(total[:RADIUS].astype(jnp.bfloat16), "rows", -1)
    from_above = shifted(total[RADIUS + SIDE : 2 * RADIUS + SIDE].astype(jnp.bfloat16), "rows", 1)
    side_forward, middle = lax.optimization_barrier((side_forward, total[RADIUS : RADIUS + SIDE]))
    y_forward = attention_forward(own_forward, side_forward, w_qkv, w_out, q_forward, bias, heads)

    gap = jnp.zeros((rows - RADIUS, cols, width), jnp.float32)
    dx = (
        middle
        + jnp.concatenate([from_above.astype(jnp.float32), gap], 0)
        + jnp.concatenate([gap, from_below.astype(jnp.float32)], 0)
    )
    return (y_forward.reshape(rows, cols, width), dx.astype(jnp.bfloat16))


def solution(mesh):
    spec = P("rows", "heads", None)
    return jax.shard_map(
        body, mesh=mesh, in_specs=(spec, spec, spec, P(), P()), out_specs=(spec, spec), check_vma=False
    )
```

profile of v0, /device:TPU:7, one launch (start us, length us, event | category | flops | bytes accessed | tf_op | source)
XLA Modules:
  0.0 100.3 jit_solution(13053664077978177681)
XLA Ops:
  0.6 0.0 copy-start
  0.6 1.2 %fusion.25 = (bf16[7,16,1152]{2,1,0:T(8,128)(2,1)S(1)}, bf16[7,16,1152]{2,1,0:T(8,128)(2,1)S(1)}) fusion(bf16[16,16,1152]{2,1,0:T(8,128)(2,1)} %param.6), kind=kLoop, calls=%fused_computation.68 | loop fusion | bytes 1032192 | tf_op jit(solution)/shard_map/slice | solution.py:29
  1.8 6.5 %collective-permute-start.1 = (bf16[7,16,1152]{2,1,0:T(8,128)(2,1)S(1)}, bf16[7,16,1152]{2,1,0:T(8,128)(2,1)S(1)}, u32[]{:S(2)}, u32[]{:S(2)}) collective-permute-start(bf16[7,16,1152]{2,1,0:T(8,128)(2,1)S(1)} %get-tuple-element.62), channel_id=1, source_target_pairs={{0,112},{16,0},{32,16},{48,32},{64,48},{80,64},{96,80},{112,96},{1... | collective-permute-start | bytes 774152 | tf_op jit(solution)/shard_map/ppermute | solution.py:25
  8.3 0.0 collective-permute-start
  8.4 1.1 %fusion.24 = (bf16[16,8,1152]{2,1,0:T(8,128)(2,1)S(1)}, bf16[16,8,1152]{2,1,0:T(8,128)(2,1)S(1)}) fusion(bf16[16,16,1152]{2,1,0:T(8,128)(2,1)} %param.6), kind=kLoop, calls=%fused_computation.67 | loop fusion | bytes 1179648 | tf_op jit(solution)/shard_map/slice | solution.py:34
  9.5 0.0 copy-start.2
  9.5 0.0 copy-start.3
  9.5 3.1 %convolution_convert_fusion.2.queries = bf16[256,1152]{1,0:T(8,128)(2,1)S(1)} fusion(bf16[256,1152]{1,0:T(8,128)(2,1)} %bitcast.24, bf16[1152,3456]{1,0:T(8,128)(2,1)} %weights.9), kind=kOutput, calls=%fused_computation.2 | convolution fusion | flops 679772160 | bytes 3833856 | tf_op jit(solution)/shard_map/dot_general | solution.py:342
  12.6 0.0 slice-start
  12.6 2.9 %convolution_convert_fusion.1.queries = bf16[256,1152]{1,0:T(8,128)(2,1)S(1)} fusion(bf16[256,1152]{1,0:T(8,128)(2,1)S(1)} %bitcast.26, bf16[1152,3456]{1,0:T(8,128)(2,1)} %weights.9), kind=kOutput, calls=%fused_computation.1 | convolution fusion | flops 679772160 | bytes 3833856 | tf_op jit(solution)/shard_map/dot_general | solution.py:342
  15.5 0.1 pad.25.clone
  15.6 0.7 and_select_fusion.bias
  16.4 0.0 slice-start.1
  16.4 1.1 %convolution_convert_fusion.cotangents = bf16[256,1152]{1,0:T(8,128)(2,1)S(1)} fusion(bf16[256,1152]{1,0:T(8,128)(2,1)S(1)} %bitcast.18, bf16[1152,1152]{1,0:T(8,128)(2,1)S(1)} %copy-done.3), kind=kOutput, calls=%fused_computation | convolution fusion | flops 679772160 | bytes 3833856 | tf_op jit(solution)/shard_map/dot_general | solution.py:355
  17.5 0.0 copy-start.1
  17.5 0.0 collective-permute-done.1
  17.5 2.2 %collective-permute-done = bf16[7,16,1152]{2,1,0:T(8,128)(2,1)S(1)} collective-permute-done((bf16[7,16,1152]{2,1,0:T(8,128)(2,1)S(1)}, bf16[7,16,1152]{2,1,0:T(8,128)(2,1)S(1)}, u32[]{:S(2)}, u32[]{:S(2)}) %collective-permute-start) | collective-permute-done | bytes 258080 | tf_op jit(solution)/shard_map/ppermute | solution.py:25
  19.7 0.2 maximum_maximum_fusion.1
  19.9 2.5 %collective-permute-start.2 = (bf16[32,8,1152]{2,1,0:T(8,128)(2,1)S(1)}, bf16[32,8,1152]{2,1,0:T(8,128)(2,1)S(1)}, u32[]{:S(2)}, u32[]{:S(2)}) collective-permute-start(bf16[32,8,1152]{2,1,0:T(8,128)(2,1)S(1)} %get-tuple-element.26), channel_id=1, source_target_pairs={{0,1},{1,2},{2,3},{3,4},{4,5},{5,6},{6,7},{7,8},{8,9},{9,10},{10,1... | collective-permute-start | bytes 1769480 | tf_op jit(solution)/shard_map/ppermute | solution.py:25
  22.5 2.6 %collective-permute-start.7 = (bf16[7,16,1152]{2,1,0:T(8,128)(2,1)S(1)}, bf16[7,16,1152]{2,1,0:T(8,128)(2,1)S(1)}, u32[]{:S(2)}, u32[]{:S(2)}) collective-permute-start(bf16[7,16,1152]{2,1,0:T(8,128)(2,1)S(1)} %get-tuple-element.58), channel_id=1, source_target_pairs={{0,112},{16,0},{32,16},{48,32},{64,48},{80,64},{96,80},{112,96},{1... | collective-permute-start | bytes 774152 | tf_op jit(solution)/shard_map/ppermute | solution.py:25
  25.1 0.5 collective-permute-start.6
  25.6 3.2 %own_keys.2.kv_own = bf16[512,2304]{1,0:T(8,128)(2,1)S(1)} custom-call(bf16[112,1152]{1,0:T(8,128)(2,1)S(1)} %bitcast.32, bf16[256,1152]{1,0:T(8,128)(2,1)S(1)} %bitcast.25, bf16[112,1152]{1,0:T(8,128)(2,1)S(1)} %bitcast.31, bf16[1152,3456]{1,0:T(8,128)(2,1)S(1)} %bitcast.20), custom_call_target="tpu_custom_call" | custom-call | flops 2717908992 | bytes 16777216 | tf_op jit(solution)/shard_map/own_keys/pallas_call | solution.py:274
  28.8 0.5 collective-permute-done.2
  29.3 4.9 %collective-permute-done.3 = bf16[32,8,1152]{2,1,0:T(8,128)(2,1)S(1)} collective-permute-done((bf16[32,8,1152]{2,1,0:T(8,128)(2,1)S(1)}, bf16[32,8,1152]{2,1,0:T(8,128)(2,1)S(1)}, u32[]{:S(2)}, u32[]{:S(2)}) %collective-permute-start.3) | collective-permute-done | bytes 589856 | tf_op jit(solution)/shard_map/ppermute | solution.py:25
  34.2 0.1 pad_maximum_fusion
  34.3 0.0 slice-start.2
  34.3 25.8 %attention_backward.1 = (bf16[2304,512]{1,0:T(8,128)(2,1)S(1)}, bf16[256,1152]{1,0:T(8,128)(2,1)S(1)}, bf16[512,1152]{1,0:T(8,128)(2,1)S(1)}) custom-call(bf16[512,2304]{1,0:T(8,128)(2,1)S(1)} %own_keys.2.kv_own, bf16[512,1152]{1,0:T(8,128)(2,1)S(1)} %bitcast.29, bf16[1152,3456]{1,0:T(8,128)(2,1)} %weights.9, ...), custom_call_target="tpu_custom_call" | custom-call | flops 16173236224 | bytes 16777216 | tf_op jit(solution)/shard_map/attention_backward/pallas_call | solution.py:274
  60.1 0.1 fusion.21
  60.2 0.1 collective-permute-start.5
  60.3 3.8 %collective-permute-start.4 = (bf16[32,8,1152]{2,1,0:T(8,128)(2,1)S(1)}, bf16[32,8,1152]{2,1,0:T(8,128)(2,1)S(1)}, u32[]{:S(2)}, u32[]{:S(2)}) collective-permute-start(bf16[32,8,1152]{2,1,0:T(8,128)(2,1)S(1)} %get-tuple-element.55), channel_id=1, source_target_pairs={{0,1},{1,2},{2,3},{3,4},{4,5},{5,6},{6,7},{7,8},{8,9},{9,10},{10,1... | collective-permute-start | bytes 1769480 | tf_op jit(solution)/shard_map/ppermute | solution.py:25
  64.2 3.8 %own_gradient.1 = f32[512,1152]{1,0:T(8,128)S(1)} custom-call(bf16[2304,512]{1,0:T(8,128)(2,1)S(1)} %get-tuple-element.36.dkv, bf16[256,1152]{1,0:T(8,128)(2,1)S(1)} %get-tuple-element.37.dq, bf16[1152,3456]{1,0:T(8,128)(2,1)S(1)} %bitcast.22), custom_call_target="tpu_custom_call" | custom-call | flops 2717908992 | bytes 16777216 | tf_op jit(solution)/shard_map/own_gradient/pallas_call | solution.py:274
  67.9 0.0 collective-permute-done.6
  68.1 0.2 maximum_maximum_fusion.3
  68.3 0.1 collective-permute-start.9
  68.4 3.8 %collective-permute-start.8 = (bf16[32,8,1152]{2,1,0:T(8,128)(2,1)S(1)}, bf16[32,8,1152]{2,1,0:T(8,128)(2,1)S(1)}, u32[]{:S(2)}, u32[]{:S(2)}) collective-permute-start(bf16[32,8,1152]{2,1,0:T(8,128)(2,1)S(1)} %get-tuple-element.73), channel_id=1, source_target_pairs={{0,1},{1,2},{2,3},{3,4},{4,5},{5,6},{6,7},{7,8},{8,9},{9,10},{10,1... | collective-permute-start | bytes 1769480 | tf_op jit(solution)/shard_map/ppermute | solution.py:25
  72.2 3.3 %own_keys.3.kv_own = bf16[512,2304]{1,0:T(8,128)(2,1)S(1)} custom-call(bf16[112,1152]{1,0:T(8,128)(2,1)S(1)} %bitcast.34, bf16[256,1152]{1,0:T(8,128)(2,1)S(1)} %bitcast.27, bf16[112,1152]{1,0:T(8,128)(2,1)S(1)} %bitcast.33, bf16[1152,3456]{1,0:T(8,128)(2,1)S(1)} %bitcast.22), custom_call_target="tpu_custom_call" | custom-call | flops 2717908992 | bytes 16777216 | tf_op jit(solution)/shard_map/own_keys/pallas_call | solution.py:274
  75.5 0.0 collective-permute-done.5
  75.5 0.3 fusion.19
  75.9 2.5 %collective-permute-start.10 = (bf16[7,16,1152]{2,1,0:T(8,128)(2,1)S(1)}, bf16[7,16,1152]{2,1,0:T(8,128)(2,1)S(1)}, u32[]{:S(2)}, u32[]{:S(2)}) collective-permute-start(bf16[7,16,1152]{2,1,0:T(8,128)(2,1)S(1)} %get-tuple-element.52), channel_id=1, source_target_pairs={{0,16},{16,32},{32,48},{48,64},{64,80},{80,96},{96,112},{112,0},{1... | collective-permute-start | bytes 774152 | tf_op jit(solution)/shard_map/ppermute | solution.py:25
  78.4 2.6 %collective-permute-start.11 = (bf16[7,16,1152]{2,1,0:T(8,128)(2,1)S(1)}, bf16[7,16,1152]{2,1,0:T(8,128)(2,1)S(1)}, u32[]{:S(2)}, u32[]{:S(2)}) collective-permute-start(bf16[7,16,1152]{2,1,0:T(8,128)(2,1)S(1)} %get-tuple-element.53), channel_id=1, source_target_pairs={{0,112},{16,0},{32,16},{48,32},{64,48},{80,64},{96,80},{112,96},{1... | collective-permute-start | bytes 774152 | tf_op jit(solution)/shard_map/ppermute | solution.py:25
  81.1 0.1 slice.96
  81.1 0.0 collective-permute-done.9
  81.2 0.1 pad_maximum_fusion.1
  81.3 1.5 %copy-done.4 = bf16[1152,1152]{1,0:T(8,128)(2,1)S(1)} copy-done((bf16[1152,1152]{1,0:T(8,128)(2,1)S(1)}, bf16[1152,1152]{1,0:T(8,128)(2,1)}, u32[]{:S(2)}) %copy-start.4) | copy-done | bytes 2654232
  82.8 16.5 %attention_forward.1 = bf16[256,1152]{1,0:T(8,128)(2,1)} custom-call(bf16[512,2304]{1,0:T(8,128)(2,1)S(1)} %own_keys.3.kv_own, bf16[512,1152]{1,0:T(8,128)(2,1)S(1)} %bitcast.30, bf16[1152,3456]{1,0:T(8,128)(2,1)} %weights.9, bf16[1152,1152]{1,0:T(8,128)(2,1)S(1)} %copy-done.4, bf16[256,1152]{1,0:T(8,128)(2,1)S(1)} %convolution_convert_fusion.1.queries, ...), custom_call_target="tpu_custom_call" | custom-call | flops 7012876288 | bytes 16777216 | tf_op jit(solution)/shard_map/attention_forward/pallas_call | solution.py:274
  99.3 0.0 collective-permute-done.10
  99.3 0.0 collective-permute-done.11
  99.3 0.9 add_convert_fusion
  (32 shorter events, 0.3 us)
Async XLA Ops:
  0.6 15.7 %copy-start = (bf16[16,16,1152]{2,1,0:T(8,128)(2,1)S(1)}, bf16[16,16,1152]{2,1,0:T(8,128)(2,1)}, u32[]{:S(2)}) copy-start(bf16[16,16,1152]{2,1,0:T(8,128)(2,1)} %param.7) | copy-start | bytes 1769476
  1.8 15.6 %collective-permute-start.1 = (bf16[7,16,1152]{2,1,0:T(8,128)(2,1)S(1)}, bf16[7,16,1152]{2,1,0:T(8,128)(2,1)S(1)}, u32[]{:S(2)}, u32[]{:S(2)}) collective-permute-start(bf16[7,16,1152]{2,1,0:T(8,128)(2,1)S(1)} %get-tuple-element.62), channel_id=1, source_target_pairs={{0,112},{16,0},{32,16},{48,32},{64,48},{80,64},{96,80},{112,96},{1... | collective-permute-start | bytes 774152 | tf_op jit(solution)/shard_map/ppermute | solution.py:25
  8.3 11.4 %collective-permute-start = (bf16[7,16,1152]{2,1,0:T(8,128)(2,1)S(1)}, bf16[7,16,1152]{2,1,0:T(8,128)(2,1)S(1)}, u32[]{:S(2)}, u32[]{:S(2)}) collective-permute-start(bf16[7,16,1152]{2,1,0:T(8,128)(2,1)S(1)} %get-tuple-element.63), channel_id=1, source_target_pairs={{0,16},{16,32},{32,48},{48,64},{64,80},{80,96},{96,112},{112,0},{1... | collective-permute-start | bytes 774152 | tf_op jit(solution)/shard_map/ppermute | solution.py:25
  9.5 3.1 %copy-start.2 = (bf16[16,16,1152]{2,1,0:T(8,128)(2,1)S(1)}, bf16[16,16,1152]{2,1,0:T(8,128)(2,1)}, u32[]{:S(2)}) copy-start(bf16[16,16,1152]{2,1,0:T(8,128)(2,1)} %param.5) | copy-start | bytes 1769476
  9.5 6.9 %copy-start.3 = (bf16[1152,1152]{1,0:T(8,128)(2,1)S(1)}, bf16[1152,1152]{1,0:T(8,128)(2,1)}, u32[]{:S(2)}) copy-start(bf16[1152,1152]{1,0:T(8,128)(2,1)} %w_out.1) | copy-start | bytes 7962628
  12.6 12.9 %slice-start = ((s8[7962624]{0:T(1024)(128)(4,1)}), s8[4194304]{0:T(1024)(128)(4,1)S(1)}, s32[]{:S(2)}) async-start(s8[7962624]{0:T(1024)(128)(4,1)} %bitcast.19), calls=%async_computation | async-start | bytes 8388608
  16.4 9.2 %slice-start.1 = ((s8[7962624]{0:T(1024)(128)(4,1)}), s8[3768320]{0:T(1024)(128)(4,1)S(1)}, s32[]{:S(2)}) async-start(s8[7962624]{0:T(1024)(128)(4,1)} %bitcast.19), calls=%async_computation.1 | async-start | bytes 7536640
  17.5 8.1 %copy-start.1 = (bf16[16,16,1152]{2,1,0:T(8,128)(2,1)S(1)}, bf16[16,16,1152]{2,1,0:T(8,128)(2,1)}, u32[]{:S(2)}) copy-start(bf16[16,16,1152]{2,1,0:T(8,128)(2,1)} %param.6) | copy-start | bytes 1769476
  19.9 9.4 %collective-permute-start.2 = (bf16[32,8,1152]{2,1,0:T(8,128)(2,1)S(1)}, bf16[32,8,1152]{2,1,0:T(8,128)(2,1)S(1)}, u32[]{:S(2)}, u32[]{:S(2)}) collective-permute-start(bf16[32,8,1152]{2,1,0:T(8,128)(2,1)S(1)} %get-tuple-element.26), channel_id=1, source_target_pairs={{0,1},{1,2},{2,3},{3,4},{4,5},{5,6},{6,7},{7,8},{8,9},{9,10},{10,1... | collective-permute-start | bytes 1769480 | tf_op jit(solution)/shard_map/ppermute | solution.py:25
  22.5 11.8 %collective-permute-start.3 = (bf16[32,8,1152]{2,1,0:T(8,128)(2,1)S(1)}, bf16[32,8,1152]{2,1,0:T(8,128)(2,1)S(1)}, u32[]{:S(2)}, u32[]{:S(2)}) collective-permute-start(bf16[32,8,1152]{2,1,0:T(8,128)(2,1)S(1)} %get-tuple-element.27), channel_id=1, source_target_pairs={{0,15},{1,0},{2,1},{3,2},{4,3},{5,4},{6,5},{7,6},{8,7},{9,8},{10,9... | collective-permute-start | bytes 1769480 | tf_op jit(solution)/shard_map/ppermute | solution.py:25
  22.5 45.4 %collective-permute-start.7 = (bf16[7,16,1152]{2,1,0:T(8,128)(2,1)S(1)}, bf16[7,16,1152]{2,1,0:T(8,128)(2,1)S(1)}, u32[]{:S(2)}, u32[]{:S(2)}) collective-permute-start(bf16[7,16,1152]{2,1,0:T(8,128)(2,1)S(1)} %get-tuple-element.58), channel_id=1, source_target_pairs={{0,112},{16,0},{32,16},{48,32},{64,48},{80,64},{96,80},{112,96},{1... | collective-permute-start | bytes 774152 | tf_op jit(solution)/shard_map/ppermute | solution.py:25
  25.1 42.9 %collective-permute-start.6 = (bf16[7,16,1152]{2,1,0:T(8,128)(2,1)S(1)}, bf16[7,16,1152]{2,1,0:T(8,128)(2,1)S(1)}, u32[]{:S(2)}, u32[]{:S(2)}) collective-permute-start(bf16[7,16,1152]{2,1,0:T(8,128)(2,1)S(1)} %get-tuple-element.59), channel_id=1, source_target_pairs={{0,16},{16,32},{32,48},{48,64},{64,80},{80,96},{96,112},{112,0},{1... | collective-permute-start | bytes 774152 | tf_op jit(solution)/shard_map/ppermute | solution.py:25
  34.3 29.9 %slice-start.2 = ((s8[7962624]{0:T(1024)(128)(4,1)}), s8[4194304]{0:T(1024)(128)(4,1)S(1)}, s32[]{:S(2)}) async-start(s8[7962624]{0:T(1024)(128)(4,1)} %bitcast.21), calls=%async_computation.2 | async-start | bytes 8388608
  34.3 29.8 %slice-start.3 = ((s8[7962624]{0:T(1024)(128)(4,1)}), s8[3768320]{0:T(1024)(128)(4,1)S(1)}, s32[]{:S(2)}) async-start(s8[7962624]{0:T(1024)(128)(4,1)} %bitcast.21), calls=%async_computation.3 | async-start | bytes 7536640
  60.2 15.3 %collective-permute-start.5 = (bf16[32,8,1152]{2,1,0:T(8,128)(2,1)S(1)}, bf16[32,8,1152]{2,1,0:T(8,128)(2,1)S(1)}, u32[]{:S(2)}, u32[]{:S(2)}) collective-permute-start(bf16[32,8,1152]{2,1,0:T(8,128)(2,1)S(1)} %get-tuple-element.54), channel_id=1, source_target_pairs={{0,15},{1,0},{2,1},{3,2},{4,3},{5,4},{6,5},{7,6},{8,7},{9,8},{10,9... | collective-permute-start | bytes 1769480 | tf_op jit(solution)/shard_map/ppermute | solution.py:25
  60.3 15.2 %collective-permute-start.4 = (bf16[32,8,1152]{2,1,0:T(8,128)(2,1)S(1)}, bf16[32,8,1152]{2,1,0:T(8,128)(2,1)S(1)}, u32[]{:S(2)}, u32[]{:S(2)}) collective-permute-start(bf16[32,8,1152]{2,1,0:T(8,128)(2,1)S(1)} %get-tuple-element.55), channel_id=1, source_target_pairs={{0,1},{1,2},{2,3},{3,4},{4,5},{5,6},{6,7},{7,8},{8,9},{9,10},{10,1... | collective-permute-start | bytes 1769480 | tf_op jit(solution)/shard_map/ppermute | solution.py:25
  68.3 12.8 %collective-permute-start.9 = (bf16[32,8,1152]{2,1,0:T(8,128)(2,1)S(1)}, bf16[32,8,1152]{2,1,0:T(8,128)(2,1)S(1)}, u32[]{:S(2)}, u32[]{:S(2)}) collective-permute-start(bf16[32,8,1152]{2,1,0:T(8,128)(2,1)S(1)} %get-tuple-element.72), channel_id=1, source_target_pairs={{0,15},{1,0},{2,1},{3,2},{4,3},{5,4},{6,5},{7,6},{8,7},{9,8},{10,9... | collective-permute-start | bytes 1769480 | tf_op jit(solution)/shard_map/ppermute | solution.py:25
  68.4 12.8 %collective-permute-start.8 = (bf16[32,8,1152]{2,1,0:T(8,128)(2,1)S(1)}, bf16[32,8,1152]{2,1,0:T(8,128)(2,1)S(1)}, u32[]{:S(2)}, u32[]{:S(2)}) collective-permute-start(bf16[32,8,1152]{2,1,0:T(8,128)(2,1)S(1)} %get-tuple-element.73), channel_id=1, source_target_pairs={{0,1},{1,2},{2,3},{3,4},{4,5},{5,6},{6,7},{7,8},{8,9},{9,10},{10,1... | collective-permute-start | bytes 1769480 | tf_op jit(solution)/shard_map/ppermute | solution.py:25
  75.9 23.4 %collective-permute-start.10 = (bf16[7,16,1152]{2,1,0:T(8,128)(2,1)S(1)}, bf16[7,16,1152]{2,1,0:T(8,128)(2,1)S(1)}, u32[]{:S(2)}, u32[]{:S(2)}) collective-permute-start(bf16[7,16,1152]{2,1,0:T(8,128)(2,1)S(1)} %get-tuple-element.52), channel_id=1, source_target_pairs={{0,16},{16,32},{32,48},{48,64},{64,80},{80,96},{96,112},{112,0},{1... | collective-permute-start | bytes 774152 | tf_op jit(solution)/shard_map/ppermute | solution.py:25
  78.4 20.9 %collective-permute-start.11 = (bf16[7,16,1152]{2,1,0:T(8,128)(2,1)S(1)}, bf16[7,16,1152]{2,1,0:T(8,128)(2,1)S(1)}, u32[]{:S(2)}, u32[]{:S(2)}) collective-permute-start(bf16[7,16,1152]{2,1,0:T(8,128)(2,1)S(1)} %get-tuple-element.53), channel_id=1, source_target_pairs={{0,112},{16,0},{32,16},{48,32},{64,48},{80,64},{96,80},{112,96},{1... | collective-permute-start | bytes 774152 | tf_op jit(solution)/shard_map/ppermute | solution.py:25
  81.1 1.7 %copy-start.4 = (bf16[1152,1152]{1,0:T(8,128)(2,1)S(1)}, bf16[1152,1152]{1,0:T(8,128)(2,1)}, u32[]{:S(2)}) copy-start(bf16[1152,1152]{1,0:T(8,128)(2,1)} %w_out.1) | copy-start | bytes 7962628
where the time goes:
time: 100 us
  Pallas kernels  52.6 us (53%)
  starting transfers between devices  25 us (25%)
  waiting for transfers between devices  7.61 us (8%)
  matrix products  7.04 us (7%)
  local copies, waits for them, and re-layouts  4.34 us (4%)
  other arithmetic  2.64 us (3%)
  between operations  1.01 us (1%)
    pallas_call x5, Pallas kernels, call_kernel(): pl.pallas_call(kernel, out_shape=out_shape, scratch_shapes=scratch, compi...  52.6 us
    ppermute x12, starting transfers between devices, shifted(): lax.ppermute(value, axis, [(i, (i + step) % count) for i in range(count)])  25 us
    ppermute x12, waiting for transfers between devices, shifted(): lax.ppermute(value, axis, [(i, (i + step) % count) for i in range(count)])  7.61 us
    dot_general x2, matrix products, project(): jnp.dot(x, w, preferred_element_type=jnp.float32).astype(jnp.bfloat16)  5.99 us
  transfers between devices with their start and end apart: 12, of which 3 were waited for; matrix products, arithmetic and copies ran while one was open for 10% of the time, Pallas kernels for 52%

commit v1 on v0

--- a/solution.py
+++ b/solution.py
@@ -16,7 +16,7 @@
 SPAN = 3 * GROUP
 KEYS = 4 * GROUP
 NEG = -1e30
-CHUNK = 16
+CHUNK = 32
 LIMIT = 40 * 2**20
 
 
@@ -59,11 +59,32 @@
     return jnp.where(valid, 0.0, NEG).astype(jnp.float32)
 
 
-def head_lanes(head, head_dim, width):
-    tile = jnp.clip(head * head_dim // 128, 0, (width - LANES) // 128)
-    offset = head * head_dim - tile * 128
+def pair_lanes(pair, head_dim, width):
+    tile = jnp.clip(2 * pair * head_dim // 128, 0, (width - LANES) // 128)
+    offset = 2 * pair * head_dim - tile * 128
     lane = lax.broadcasted_iota(jnp.int32, (1, LANES), 1)
-    return tile * 128, (lane >= offset) & (lane < offset + head_dim)
+    live = pair >= 0
+    first = (lane >= offset) & (lane < offset + head_dim) & live
+    second = (lane >= offset + head_dim) & (lane < offset + 2 * head_dim) & live
+    return tile * 128, (first, second)
+
+
+def stacked(ref, start, masks):
+    block = ref[:, at_lanes(start)]
+    halves = (block[:HALF], block[HALF:])
+    return jnp.concatenate([jnp.where(mask, half, 0) for half in halves for mask in masks], 0)
+
+
+def add_heads(acc, start, masks, parts):
+    for half, part in enumerate(parts):
+        rows = slice(HALF * half, HALF * (half + 1))
+        acc[rows, at_lanes(start)] += jnp.where(masks[0], part[:HALF], jnp.where(masks[1], part[HALF:], 0.0))
+
+
+def span_mix(weights, kv, start):
+    low = jnp.dot(weights[: 2 * HALF, :], kv[:SPAN, at_lanes(start)], preferred_element_type=jnp.float32)
+    high = jnp.dot(weights[2 * HALF :, :], kv[GROUP:, at_lanes(start)], preferred_element_type=jnp.float32)
+    return low, high
 
 
 def at_lanes(start):
@@ -116,16 +137,16 @@
 
 def span_products(rows, kv, start, out_ref):
     def one(group):
-        low = 0 if group < 3 else HALF
-        high = 2 * HALF if group > 0 else HALF
+        low = 0 if group < 3 else 2 * HALF
+        high = 4 * HALF if group > 0 else 2 * HALF
         keys = kv[GROUP * group : GROUP * (group + 1), at_lanes(start)]
         part = lax.dot_general(
             rows[low:high], keys, (((1,), (1,)), ((), ())), preferred_element_type=jnp.float32
         )
         if group < 3:
-            out_ref[:HALF, GROUP * group : GROUP * (group + 1)] = part[:HALF]
+            out_ref[: 2 * HALF, GROUP * group : GROUP * (group + 1)] = part[: 2 * HALF]
         if group > 0:
-            out_ref[HALF:, GROUP * (group - 1) : GROUP * group] = part[-HALF:]
+            out_ref[2 * HALF :, GROUP * (group - 1) : GROUP * group] = part[-2 * HALF :]
 
     return [functools.partial(one, group) for group in range(4)]
 
@@ -143,126 +164,118 @@
     return terms * (1.0 / jnp.sum(terms, axis=1, keepdims=True))
 
 
-def span_of(rows):
-    start = 0 if rows < HALF else GROUP
-    return slice(start, start + SPAN)
+def bias_rows(rows):
+    start = rows // (2 * HALF) * HALF + rows % HALF
+    return slice(start, start + CHUNK)
+
+
+def run_pairs(pairs, scored, weighted, spread):
+    interleave(scored(0, 0))
+
+    def two(index, carry):
+        pair = 2 * index
+        interleave(scored(pair + 1, 1), weighted(0), spread(pair - 1, 1))
+        interleave(scored(jnp.minimum(pair + 2, pairs - 1), 0), weighted(1), spread(pair, 0))
+        return carry
+
+    lax.fori_loop(0, pairs // 2, two, 0)
+    interleave(spread(pairs - 1, 1))
 
 
 def forward_kernel(
     head_dim, kv_own, x_side, weights, w_out, queries, bias, out_ref, kv, acc, scores0, scores1, probs0, probs1
 ):
     width = queries.shape[1]
-    heads = width // head_dim
     factor = head_dim**-0.5 * math.log2(math.e)
     scores, probs = (scores0, scores1), (probs0, probs1)
-    for ref in probs + (acc,):
-        ref[...] = jnp.zeros_like(ref)
+    acc[...] = jnp.zeros_like(acc)
     fill_keys(kv_own, x_side, weights, kv)
 
-    def scored(head, u):
-        start, mask = head_lanes(head, head_dim, width)
-        return span_products(jnp.where(mask, queries[:, at_lanes(start)], 0), kv, start, scores[u])
+    def scored(pair, u):
+        start, masks = pair_lanes(pair, head_dim, width)
+        return span_products(stacked(queries, start, masks), kv, start, scores[u])
 
     def weighted(u):
         def one(rows):
             part = slice(rows, rows + CHUNK)
-            attention = softmax_rows(scores[u][part, :], bias[part, :], factor)
-            probs[u][part, span_of(rows)] = attention.astype(jnp.bfloat16)
-
-        return [functools.partial(one, rows) for rows in range(0, 2 * HALF, CHUNK)]
-
-    def mixed(head, u):
-        start, mask = head_lanes(head, head_dim, width)
-
-        def one():
-            mix = jnp.dot(probs[u][...], kv[:, at_lanes(start + width)], preferred_element_type=jnp.float32)
-            acc[:, at_lanes(start)] += jnp.where(mask & (head >= 0), mix, 0.0)
-
-        return [one]
-
-    interleave(scored(0, 0))
-
-    def pair(index, carry):
-        head = 2 * index
-        interleave(scored(head + 1, 1), weighted(0), mixed(head - 1, 1))
-        interleave(scored(jnp.minimum(head + 2, heads - 1), 0), weighted(1), mixed(head, 0))
-        return carry
-
-    lax.fori_loop(0, heads // 2, pair, 0)
-    interleave(mixed(heads - 1, 1))
+            attention = softmax_rows(scores[u][part, :], bias[bias_rows(rows), :], factor)
+            probs[u][part, :] = attention.astype(jnp.bfloat16)
+
+        return [functools.partial(one, rows) for rows in range(0, 4 * HALF, CHUNK)]
+
+    def spread(pair, u):
+        start, masks = pair_lanes(pair, head_dim, width)
+        return [lambda: add_heads(acc, start, masks, span_mix(probs[u], kv, start + width))]
+
+    run_pairs(width // head_dim // 2, scored, weighted, spread)
     attended = acc[...].astype(jnp.bfloat16)
     out_ref[...] = jnp.dot(attended, w_out[...], preferred_element_type=jnp.float32).astype(out_ref.dtype)
 
 
 def backward_kernel(
     head_dim, kv_own, x_side, weights, queries, cotangents, bias, down_ref, dq_ref, dside_ref,
-    queries_t, cotangents_t, kv, dkv, acc,
-    scores0, scores1, grads0, grads1, probs0, probs1, dscores0, dscores1, held0, held1
+    queries_t, cotangents_t, kv, dkv, acc, scores0, scores1, grads0, grads1, probs0, probs1, dscores0, dscores1
 ):
     width = queries.shape[1]
-    heads = width // head_dim
     scaling = head_dim**-0.5
     factor = scaling * math.log2(math.e)
-    scores, grads, held = (scores0, scores1), (grads0, grads1), (held0, held1)
+    scores, grads = (scores0, scores1), (grads0, grads1)
     probs, dscores = (probs0, probs1), (dscores0, dscores1)
-    for ref in probs + dscores + held + (acc,):
-        ref[...] = jnp.zeros_like(ref)
+    acc[...] = jnp.zeros_like(acc)
     turned(queries, queries_t)
     turned(cotangents, cotangents_t)
     fill_keys(kv_own, x_side, weights, kv)
 
-    def scored(head, u):
-        start, mask = head_lanes(head, head_dim, width)
-        one = span_products(jnp.where(mask, queries[:, at_lanes(start)], 0), kv, start, scores[u])
-        other = span_products(jnp.where(mask, cotangents[:, at_lanes(start)], 0), kv, start + width, grads[u])
+    def scored(pair, u):
+        start, masks = pair_lanes(pair, head_dim, width)
+        one = span_products(stacked(queries, start, masks), kv, start, scores[u])
+        other = span_products(stacked(cotangents, start, masks), kv, start + width, grads[u])
         return [step for both in zip(one, other) for step in both]
 
     def weighted(u):
         def one(rows):
             part = slice(rows, rows + CHUNK)
-            attention = softmax_rows(scores[u][part, :], bias[part, :], factor)
+            attention = softmax_rows(scores[u][part, :], bias[bias_rows(rows), :], factor)
             grad = grads[u][part, :]
             centre = jnp.sum(attention * grad, axis=1, keepdims=True)
-            probs[u][part, span_of(rows)] = attention.astype(jnp.bfloat16)
-            dscores[u][part, span_of(rows)] = (attention * (grad - centre) * scaling).astype(jnp.bfloat16)
-
-        return [functools.partial(one, rows) for rows in range(0, 2 * HALF, CHUNK)]
-
-    def spread(head, u):
-        start, mask = head_lanes(head, head_dim, width)
-        row = jnp.maximum(head, 0)
-        base = jnp.maximum(head - 1, 0) * head_dim
+            probs[u][part, :] = attention.astype(jnp.bfloat16)
+            dscores[u][part, :] = (attention * (grad - centre) * scaling).astype(jnp.bfloat16)
+
+        return [functools.partial(one, rows) for rows in range(0, 4 * HALF, CHUNK)]
+
+    def spread(pair, u):
+        start, masks = pair_lanes(pair, head_dim, width)
+        here = jnp.maximum(pair, 0)
 
         def query_part():
-            dq = jnp.dot(dscores[u][...], kv[:, at_lanes(start)], preferred_element_type=jnp.float32)
-            acc[:, at_lanes(start)] += jnp.where(mask & (head >= 0), dq, 0.0)
+            add_heads(acc, start, masks, span_mix(dscores[u], kv, start))
+
+        def head_part(source, spans, head, group):
+            low = spans[HALF * head : HALF * (head + 1), GROUP * group : GROUP * (group + 1)] if group < 3 else None
+            place = slice(GROUP * (group - 1), GROUP * group)
+            high = spans[HALF * (head + 2) : HALF * (head + 3), place] if group > 0 else None
+            features = source[2 * here + head]
+            if group == 0:
+                features, span = features[:, :HALF], low
+            elif group == 3:
+                features, span = features[:, HALF:], high
+            else:
+                span = jnp.concatenate([low, high], 0)
+            return jnp.dot(features, span, preferred_element_type=jnp.float32)
 
         def key_part(index, group):
-            source, spans = ((queries_t, dscores), (cotangents_t, probs))[index]
-            place = slice(GROUP * group, GROUP * (group + 1))
-            part = jnp.dot(source[row], spans[u][:, place], preferred_element_type=jnp.float32)
-            if u == 0:
-                held[index][:, place] = part
-            else:
-                both = jnp.concatenate([held[index][:, place], part], 0).astype(jnp.bfloat16)
-                rows = pl.ds(pl.multiple_of(base + index * width, 16), 2 * head_dim)
-                place = slice(HALF * group, HALF * (group + 1))
-                down_ref[rows, place] = both[:, :HALF]
-                dkv[rows, place] = both[:, HALF:]
+            source, spans = ((queries_t, dscores[u]), (cotangents_t, probs[u]))[index]
+            both = jnp.concatenate([head_part(source, spans, head, group) for head in range(2)], 0)
+            both = both.astype(jnp.bfloat16)
+            rows = pl.ds(pl.multiple_of(2 * head_dim * here + index * width, 16), 2 * head_dim)
+            place = slice(HALF * group, HALF * (group + 1))
+            down_ref[rows, place] = both[:, :HALF]
+            dkv[rows, place] = both[:, HALF:]
 
         parts = [functools.partial(key_part, index, group) for index in range(2) for group in range(4)]
         return parts[:4] + [query_part] + parts[4:]
 
-    interleave(scored(0, 0))
-
-    def pair(index, carry):
-        head = 2 * index
-        interleave(scored(head + 1, 1), weighted(0), spread(head - 1, 1))
-        interleave(scored(jnp.minimum(head + 2, heads - 1), 0), weighted(1), spread(head, 0))
-        return carry
-
-    lax.fori_loop(0, heads // 2, pair, 0)
-    interleave(spread(heads - 1, 1))
+    run_pairs(width // head_dim // 2, scored, weighted, spread)
 
     dq_ref[...] = acc[...].astype(dq_ref.dtype)
     for start in range(0, dside_ref.shape[0], GROUP):
@@ -296,9 +309,9 @@
 def attention_forward(kv_own, x_side, w_qkv, w_out, queries, bias, heads):
     tokens, width = queries.shape
     half, full = jnp.bfloat16, jnp.float32
-    square = (tokens, SPAN)
+    square = (2 * tokens, SPAN)
     scratch = [pltpu.VMEM((KEYS, 2 * width), half), pltpu.VMEM((tokens, width), full)]
-    scratch += [pltpu.VMEM(square, full)] * 2 + [pltpu.VMEM((tokens, KEYS), half)] * 2
+    scratch += [pltpu.VMEM(square, full)] * 2 + [pltpu.VMEM(square, half)] * 2
     return call_kernel(
         functools.partial(forward_kernel, width // heads),
         [kv_own, x_side, w_qkv, w_out, queries, bias],
@@ -312,7 +325,7 @@
 def attention_backward(kv_own, x_side, w_qkv, queries, cotangents, bias, heads):
     tokens, width = queries.shape
     head_dim = width // heads
-    square = (tokens, SPAN)
+    square = (2 * tokens, SPAN)
     half, full = jnp.bfloat16, jnp.float32
     by_head = (heads, head_dim, tokens)
     scratch = [
@@ -322,8 +335,7 @@
         pltpu.VMEM((2 * width, KEYS // 2), half),
         pltpu.VMEM((tokens, width), full),
     ]
-    scratch += [pltpu.VMEM(square, full)] * 4 + [pltpu.VMEM((tokens, KEYS), half)] * 4
-    scratch += [pltpu.VMEM((head_dim, KEYS), full)] * 2
+    scratch += [pltpu.VMEM(square, full)] * 4 + [pltpu.VMEM(square, half)] * 4
     return call_kernel(
         functools.partial(backward_kernel, head_dim),
         [kv_own, x_side, w_qkv, queries, cotangents, bias],

time: 100 us -> 97.1 us (0.971)
  Pallas kernels: 52.6 us -> 49.3 us
    pallas_call x5, Pallas kernels: 52.6 us -> 49.3 us  [call_kernel(): pl.pallas_call(kernel, out_shape=out_shape, scratch_shapes=scratch, compi...]
  transfers between devices with their start and end apart: 12 -> 12, of which waited for: 3 -> 3; matrix products, arithmetic and copies ran while one was open for 10% -> 10% of each run, Pallas kernels for 52% -> 51%
where the time goes in v1:
time: 97.1 us; the launch traced here: 96.9 us
  Pallas kernels  49.3 us (51%)
  starting transfers between devices  25 us (26%)
  waiting for transfers between devices  7.61 us (8%)
  matrix products  7.04 us (7%)
  local copies, waits for them, and re-layouts  4.34 us (4%)
  other arithmetic  2.64 us (3%)
  between operations  1.01 us (1%)
    pallas_call x5, Pallas kernels, call_kernel(): pl.pallas_call(kernel, out_shape=out_shape, scratch_shapes=scratch, compi...  49.3 us
    ppermute x12, starting transfers between devices, shifted(): lax.ppermute(value, axis, [(i, (i + step) % count) for i in range(count)])  25 us
    ppermute x12, waiting for transfers between devices, shifted(): lax.ppermute(value, axis, [(i, (i + step) % count) for i in range(count)])  7.61 us
    dot_general x2, matrix products, project(): jnp.dot(x, w, preferred_element_type=jnp.float32).astype(jnp.bfloat16)  5.99 us
  transfers between devices with their start and end apart: 12, of which 3 were waited for; matrix products, arithmetic and copies ran while one was open for 10% of the time, Pallas kernels for 51%

profile of v1, /device:TPU:7, one launch (start us, length us, event | category | flops | bytes accessed | tf_op | source)
XLA Modules:
  0.0 96.9 jit_solution(10553845134042988643)
XLA Ops:
  0.6 0.0 copy-start
  0.6 1.2 %fusion.25 = (bf16[7,16,1152]{2,1,0:T(8,128)(2,1)S(1)}, bf16[7,16,1152]{2,1,0:T(8,128)(2,1)S(1)}) fusion(bf16[16,16,1152]{2,1,0:T(8,128)(2,1)} %param.6), kind=kLoop, calls=%fused_computation.68 | loop fusion | bytes 1032192 | tf_op jit(solution)/shard_map/slice | solution.py:29
  1.8 6.5 %collective-permute-start.1 = (bf16[7,16,1152]{2,1,0:T(8,128)(2,1)S(1)}, bf16[7,16,1152]{2,1,0:T(8,128)(2,1)S(1)}, u32[]{:S(2)}, u32[]{:S(2)}) collective-permute-start(bf16[7,16,1152]{2,1,0:T(8,128)(2,1)S(1)} %get-tuple-element.62), channel_id=1, source_target_pairs={{0,112},{16,0},{32,16},{48,32},{64,48},{80,64},{96,80},{112,96},{1... | collective-permute-start | bytes 774152 | tf_op jit(solution)/shard_map/ppermute | solution.py:25
  8.3 0.0 collective-permute-start
  8.4 1.1 %fusion.24 = (bf16[16,8,1152]{2,1,0:T(8,128)(2,1)S(1)}, bf16[16,8,1152]{2,1,0:T(8,128)(2,1)S(1)}) fusion(bf16[16,16,1152]{2,1,0:T(8,128)(2,1)} %param.6), kind=kLoop, calls=%fused_computation.67 | loop fusion | bytes 1179648 | tf_op jit(solution)/shard_map/slice | solution.py:34
  9.5 0.0 copy-start.2
  9.5 0.0 copy-start.3
  9.5 3.1 %convolution_convert_fusion.2.queries = bf16[256,1152]{1,0:T(8,128)(2,1)S(1)} fusion(bf16[256,1152]{1,0:T(8,128)(2,1)} %bitcast.24, bf16[1152,3456]{1,0:T(8,128)(2,1)} %weights.9), kind=kOutput, calls=%fused_computation.2 | convolution fusion | flops 679772160 | bytes 3833856 | tf_op jit(solution)/shard_map/dot_general | solution.py:354
  12.6 0.0 slice-start
  12.6 2.9 %convolution_convert_fusion.1.queries = bf16[256,1152]{1,0:T(8,128)(2,1)S(1)} fusion(bf16[256,1152]{1,0:T(8,128)(2,1)S(1)} %bitcast.26, bf16[1152,3456]{1,0:T(8,128)(2,1)} %weights.9), kind=kOutput, calls=%fused_computation.1 | convolution fusion | flops 679772160 | bytes 3833856 | tf_op jit(solution)/shard_map/dot_general | solution.py:354
  15.5 0.1 pad.25.clone
  15.6 0.7 and_select_fusion.bias
  16.4 0.0 slice-start.1
  16.4 1.1 %convolution_convert_fusion.cotangents = bf16[256,1152]{1,0:T(8,128)(2,1)S(1)} fusion(bf16[256,1152]{1,0:T(8,128)(2,1)S(1)} %bitcast.18, bf16[1152,1152]{1,0:T(8,128)(2,1)S(1)} %copy-done.3), kind=kOutput, calls=%fused_computation | convolution fusion | flops 679772160 | bytes 3833856 | tf_op jit(solution)/shard_map/dot_general | solution.py:367
  17.5 0.0 copy-start.1
  17.5 0.0 collective-permute-done.1
  17.5 2.2 %collective-permute-done = bf16[7,16,1152]{2,1,0:T(8,128)(2,1)S(1)} collective-permute-done((bf16[7,16,1152]{2,1,0:T(8,128)(2,1)S(1)}, bf16[7,16,1152]{2,1,0:T(8,128)(2,1)S(1)}, u32[]{:S(2)}, u32[]{:S(2)}) %collective-permute-start) | collective-permute-done | bytes 258080 | tf_op jit(solution)/shard_map/ppermute | solution.py:25
  19.7 0.2 maximum_maximum_fusion.1
  19.9 2.5 %collective-permute-start.2 = (bf16[32,8,1152]{2,1,0:T(8,128)(2,1)S(1)}, bf16[32,8,1152]{2,1,0:T(8,128)(2,1)S(1)}, u32[]{:S(2)}, u32[]{:S(2)}) collective-permute-start(bf16[32,8,1152]{2,1,0:T(8,128)(2,1)S(1)} %get-tuple-element.26), channel_id=1, source_target_pairs={{0,1},{1,2},{2,3},{3,4},{4,5},{5,6},{6,7},{7,8},{8,9},{9,10},{10,1... | collective-permute-start | bytes 1769480 | tf_op jit(solution)/shard_map/ppermute | solution.py:25
  22.5 0.0 collective-permute-start.3
  22.5 2.6 %collective-permute-start.7 = (bf16[7,16,1152]{2,1,0:T(8,128)(2,1)S(1)}, bf16[7,16,1152]{2,1,0:T(8,128)(2,1)S(1)}, u32[]{:S(2)}, u32[]{:S(2)}) collective-permute-start(bf16[7,16,1152]{2,1,0:T(8,128)(2,1)S(1)} %get-tuple-element.58), channel_id=1, source_target_pairs={{0,112},{16,0},{32,16},{48,32},{64,48},{80,64},{96,80},{112,96},{1... | collective-permute-start | bytes 774152 | tf_op jit(solution)/shard_map/ppermute | solution.py:25
  25.1 0.5 collective-permute-start.6
  25.6 3.2 %own_keys.2.kv_own = bf16[512,2304]{1,0:T(8,128)(2,1)S(1)} custom-call(bf16[112,1152]{1,0:T(8,128)(2,1)S(1)} %bitcast.32, bf16[256,1152]{1,0:T(8,128)(2,1)S(1)} %bitcast.25, bf16[112,1152]{1,0:T(8,128)(2,1)S(1)} %bitcast.31, bf16[1152,3456]{1,0:T(8,128)(2,1)S(1)} %bitcast.20), custom_call_target="tpu_custom_call" | custom-call | flops 2717908992 | bytes 16777216 | tf_op jit(solution)/shard_map/own_keys/pallas_call | solution.py:287
  28.8 0.5 collective-permute-done.2
  29.3 4.9 %collective-permute-done.3 = bf16[32,8,1152]{2,1,0:T(8,128)(2,1)S(1)} collective-permute-done((bf16[32,8,1152]{2,1,0:T(8,128)(2,1)S(1)}, bf16[32,8,1152]{2,1,0:T(8,128)(2,1)S(1)}, u32[]{:S(2)}, u32[]{:S(2)}) %collective-permute-start.3) | collective-permute-done | bytes 589856 | tf_op jit(solution)/shard_map/ppermute | solution.py:25
  34.2 0.1 pad_maximum_fusion
  34.3 0.0 slice-start.2
  34.3 23.5 %attention_backward.1 = (bf16[2304,512]{1,0:T(8,128)(2,1)S(1)}, bf16[256,1152]{1,0:T(8,128)(2,1)S(1)}, bf16[512,1152]{1,0:T(8,128)(2,1)S(1)}) custom-call(bf16[512,2304]{1,0:T(8,128)(2,1)S(1)} %own_keys.2.kv_own, bf16[512,1152]{1,0:T(8,128)(2,1)S(1)} %bitcast.29, bf16[1152,3456]{1,0:T(8,128)(2,1)} %weights.9, ...), custom_call_target="tpu_custom_call" | custom-call | flops 16173236224 | bytes 16777216 | tf_op jit(solution)/shard_map/attention_backward/pallas_call | solution.py:287
  57.9 0.1 fusion.21
  58.0 0.1 collective-permute-start.5
  58.0 3.8 %collective-permute-start.4 = (bf16[32,8,1152]{2,1,0:T(8,128)(2,1)S(1)}, bf16[32,8,1152]{2,1,0:T(8,128)(2,1)S(1)}, u32[]{:S(2)}, u32[]{:S(2)}) collective-permute-start(bf16[32,8,1152]{2,1,0:T(8,128)(2,1)S(1)} %get-tuple-element.55), channel_id=1, source_target_pairs={{0,1},{1,2},{2,3},{3,4},{4,5},{5,6},{6,7},{7,8},{8,9},{9,10},{10,1... | collective-permute-start | bytes 1769480 | tf_op jit(solution)/shard_map/ppermute | solution.py:25
  61.9 3.8 %own_gradient.1 = f32[512,1152]{1,0:T(8,128)S(1)} custom-call(bf16[2304,512]{1,0:T(8,128)(2,1)S(1)} %get-tuple-element.36.dkv, bf16[256,1152]{1,0:T(8,128)(2,1)S(1)} %get-tuple-element.37.dq, bf16[1152,3456]{1,0:T(8,128)(2,1)S(1)} %bitcast.22), custom_call_target="tpu_custom_call" | custom-call | flops 2717908992 | bytes 16777216 | tf_op jit(solution)/shard_map/own_gradient/pallas_call | solution.py:287
  65.6 0.0 collective-permute-done.7
  65.8 0.2 maximum_maximum_fusion.3
  66.0 0.1 collective-permute-start.9
  66.1 3.8 %collective-permute-start.8 = (bf16[32,8,1152]{2,1,0:T(8,128)(2,1)S(1)}, bf16[32,8,1152]{2,1,0:T(8,128)(2,1)S(1)}, u32[]{:S(2)}, u32[]{:S(2)}) collective-permute-start(bf16[32,8,1152]{2,1,0:T(8,128)(2,1)S(1)} %get-tuple-element.73), channel_id=1, source_target_pairs={{0,1},{1,2},{2,3},{3,4},{4,5},{5,6},{6,7},{7,8},{8,9},{9,10},{10,1... | collective-permute-start | bytes 1769480 | tf_op jit(solution)/shard_map/ppermute | solution.py:25
  69.9 3.3 %own_keys.3.kv_own = bf16[512,2304]{1,0:T(8,128)(2,1)S(1)} custom-call(bf16[112,1152]{1,0:T(8,128)(2,1)S(1)} %bitcast.34, bf16[256,1152]{1,0:T(8,128)(2,1)S(1)} %bitcast.27, bf16[112,1152]{1,0:T(8,128)(2,1)S(1)} %bitcast.33, bf16[1152,3456]{1,0:T(8,128)(2,1)S(1)} %bitcast.22), custom_call_target="tpu_custom_call" | custom-call | flops 2717908992 | bytes 16777216 | tf_op jit(solution)/shard_map/own_keys/pallas_call | solution.py:287
  73.2 0.0 collective-permute-done.5
  73.2 0.0 collective-permute-done.4
  73.3 0.3 fusion.19
  73.6 2.5 %collective-permute-start.10 = (bf16[7,16,1152]{2,1,0:T(8,128)(2,1)S(1)}, bf16[7,16,1152]{2,1,0:T(8,128)(2,1)S(1)}, u32[]{:S(2)}, u32[]{:S(2)}) collective-permute-start(bf16[7,16,1152]{2,1,0:T(8,128)(2,1)S(1)} %get-tuple-element.52), channel_id=1, source_target_pairs={{0,16},{16,32},{32,48},{48,64},{64,80},{80,96},{96,112},{112,0},{1... | collective-permute-start | bytes 774152 | tf_op jit(solution)/shard_map/ppermute | solution.py:25
  76.1 2.6 %collective-permute-start.11 = (bf16[7,16,1152]{2,1,0:T(8,128)(2,1)S(1)}, bf16[7,16,1152]{2,1,0:T(8,128)(2,1)S(1)}, u32[]{:S(2)}, u32[]{:S(2)}) collective-permute-start(bf16[7,16,1152]{2,1,0:T(8,128)(2,1)S(1)} %get-tuple-element.53), channel_id=1, source_target_pairs={{0,112},{16,0},{32,16},{48,32},{64,48},{80,64},{96,80},{112,96},{1... | collective-permute-start | bytes 774152 | tf_op jit(solution)/shard_map/ppermute | solution.py:25
  78.8 0.1 slice.96
  78.9 0.0 collective-permute-done.8
  78.9 0.1 pad_maximum_fusion.1
  79.0 1.5 %copy-done.4 = bf16[1152,1152]{1,0:T(8,128)(2,1)S(1)} copy-done((bf16[1152,1152]{1,0:T(8,128)(2,1)S(1)}, bf16[1152,1152]{1,0:T(8,128)(2,1)}, u32[]{:S(2)}) %copy-start.4) | copy-done | bytes 2654232
  80.5 15.5 %attention_forward.1 = bf16[256,1152]{1,0:T(8,128)(2,1)} custom-call(bf16[512,2304]{1,0:T(8,128)(2,1)S(1)} %own_keys.3.kv_own, bf16[512,1152]{1,0:T(8,128)(2,1)S(1)} %bitcast.30, bf16[1152,3456]{1,0:T(8,128)(2,1)} %weights.9, bf16[1152,1152]{1,0:T(8,128)(2,1)S(1)} %copy-done.4, bf16[256,1152]{1,0:T(8,128)(2,1)S(1)} %convolution_convert_fusion.1.queries, ...), custom_call_target="tpu_custom_call" | custom-call | flops 7012876288 | bytes 16777216 | tf_op jit(solution)/shard_map/attention_forward/pallas_call | solution.py:287
  96.0 0.9 add_convert_fusion
  (32 shorter events, 0.3 us)
Async XLA Ops:
  0.6 15.7 %copy-start = (bf16[16,16,1152]{2,1,0:T(8,128)(2,1)S(1)}, bf16[16,16,1152]{2,1,0:T(8,128)(2,1)}, u32[]{:S(2)}) copy-start(bf16[16,16,1152]{2,1,0:T(8,128)(2,1)} %param.7) | copy-start | bytes 1769476
  1.8 15.6 %collective-permute-start.1 = (bf16[7,16,1152]{2,1,0:T(8,128)(2,1)S(1)}, bf16[7,16,1152]{2,1,0:T(8,128)(2,1)S(1)}, u32[]{:S(2)}, u32[]{:S(2)}) collective-permute-start(bf16[7,16,1152]{2,1,0:T(8,128)(2,1)S(1)} %get-tuple-element.62), channel_id=1, source_target_pairs={{0,112},{16,0},{32,16},{48,32},{64,48},{80,64},{96,80},{112,96},{1... | collective-permute-start | bytes 774152 | tf_op jit(solution)/shard_map/ppermute | solution.py:25
  8.3 11.4 %collective-permute-start = (bf16[7,16,1152]{2,1,0:T(8,128)(2,1)S(1)}, bf16[7,16,1152]{2,1,0:T(8,128)(2,1)S(1)}, u32[]{:S(2)}, u32[]{:S(2)}) collective-permute-start(bf16[7,16,1152]{2,1,0:T(8,128)(2,1)S(1)} %get-tuple-element.63), channel_id=1, source_target_pairs={{0,16},{16,32},{32,48},{48,64},{64,80},{80,96},{96,112},{112,0},{1... | collective-permute-start | bytes 774152 | tf_op jit(solution)/shard_map/ppermute | solution.py:25
  9.5 3.1 %copy-start.2 = (bf16[16,16,1152]{2,1,0:T(8,128)(2,1)S(1)}, bf16[16,16,1152]{2,1,0:T(8,128)(2,1)}, u32[]{:S(2)}) copy-start(bf16[16,16,1152]{2,1,0:T(8,128)(2,1)} %param.5) | copy-start | bytes 1769476
  9.5 6.9 %copy-start.3 = (bf16[1152,1152]{1,0:T(8,128)(2,1)S(1)}, bf16[1152,1152]{1,0:T(8,128)(2,1)}, u32[]{:S(2)}) copy-start(bf16[1152,1152]{1,0:T(8,128)(2,1)} %w_out.1) | copy-start | bytes 7962628
  12.6 12.9 %slice-start = ((s8[7962624]{0:T(1024)(128)(4,1)}), s8[4194304]{0:T(1024)(128)(4,1)S(1)}, s32[]{:S(2)}) async-start(s8[7962624]{0:T(1024)(128)(4,1)} %bitcast.19), calls=%async_computation | async-start | bytes 8388608
  16.4 9.2 %slice-start.1 = ((s8[7962624]{0:T(1024)(128)(4,1)}), s8[3768320]{0:T(1024)(128)(4,1)S(1)}, s32[]{:S(2)}) async-start(s8[7962624]{0:T(1024)(128)(4,1)} %bitcast.19), calls=%async_computation.1 | async-start | bytes 7536640
  17.5 8.1 %copy-start.1 = (bf16[16,16,1152]{2,1,0:T(8,128)(2,1)S(1)}, bf16[16,16,1152]{2,1,0:T(8,128)(2,1)}, u32[]{:S(2)}) copy-start(bf16[16,16,1152]{2,1,0:T(8,128)(2,1)} %param.6) | copy-start | bytes 1769476
  19.9 9.4 %collective-permute-start.2 = (bf16[32,8,1152]{2,1,0:T(8,128)(2,1)S(1)}, bf16[32,8,1152]{2,1,0:T(8,128)(2,1)S(1)}, u32[]{:S(2)}, u32[]{:S(2)}) collective-permute-start(bf16[32,8,1152]{2,1,0:T(8,128)(2,1)S(1)} %get-tuple-element.26), channel_id=1, source_target_pairs={{0,1},{1,2},{2,3},{3,4},{4,5},{5,6},{6,7},{7,8},{8,9},{9,10},{10,1... | collective-permute-start | bytes 1769480 | tf_op jit(solution)/shard_map/ppermute | solution.py:25
  22.5 11.8 %collective-permute-start.3 = (bf16[32,8,1152]{2,1,0:T(8,128)(2,1)S(1)}, bf16[32,8,1152]{2,1,0:T(8,128)(2,1)S(1)}, u32[]{:S(2)}, u32[]{:S(2)}) collective-permute-start(bf16[32,8,1152]{2,1,0:T(8,128)(2,1)S(1)} %get-tuple-element.27), channel_id=1, source_target_pairs={{0,15},{1,0},{2,1},{3,2},{4,3},{5,4},{6,5},{7,6},{8,7},{9,8},{10,9... | collective-permute-start | bytes 1769480 | tf_op jit(solution)/shard_map/ppermute | solution.py:25
  22.5 43.1 %collective-permute-start.7 = (bf16[7,16,1152]{2,1,0:T(8,128)(2,1)S(1)}, bf16[7,16,1152]{2,1,0:T(8,128)(2,1)S(1)}, u32[]{:S(2)}, u32[]{:S(2)}) collective-permute-start(bf16[7,16,1152]{2,1,0:T(8,128)(2,1)S(1)} %get-tuple-element.58), channel_id=1, source_target_pairs={{0,112},{16,0},{32,16},{48,32},{64,48},{80,64},{96,80},{112,96},{1... | collective-permute-start | bytes 774152 | tf_op jit(solution)/shard_map/ppermute | solution.py:25
  25.1 40.6 %collective-permute-start.6 = (bf16[7,16,1152]{2,1,0:T(8,128)(2,1)S(1)}, bf16[7,16,1152]{2,1,0:T(8,128)(2,1)S(1)}, u32[]{:S(2)}, u32[]{:S(2)}) collective-permute-start(bf16[7,16,1152]{2,1,0:T(8,128)(2,1)S(1)} %get-tuple-element.59), channel_id=1, source_target_pairs={{0,16},{16,32},{32,48},{48,64},{64,80},{80,96},{96,112},{112,0},{1... | collective-permute-start | bytes 774152 | tf_op jit(solution)/shard_map/ppermute | solution.py:25
  34.3 27.6 %slice-start.2 = ((s8[7962624]{0:T(1024)(128)(4,1)}), s8[4194304]{0:T(1024)(128)(4,1)S(1)}, s32[]{:S(2)}) async-start(s8[7962624]{0:T(1024)(128)(4,1)} %bitcast.21), calls=%async_computation.2 | async-start | bytes 8388608
  34.3 27.6 %slice-start.3 = ((s8[7962624]{0:T(1024)(128)(4,1)}), s8[3768320]{0:T(1024)(128)(4,1)S(1)}, s32[]{:S(2)}) async-start(s8[7962624]{0:T(1024)(128)(4,1)} %bitcast.21), calls=%async_computation.3 | async-start | bytes 7536640
  58.0 15.3 %collective-permute-start.5 = (bf16[32,8,1152]{2,1,0:T(8,128)(2,1)S(1)}, bf16[32,8,1152]{2,1,0:T(8,128)(2,1)S(1)}, u32[]{:S(2)}, u32[]{:S(2)}) collective-permute-start(bf16[32,8,1152]{2,1,0:T(8,128)(2,1)S(1)} %get-tuple-element.54), channel_id=1, source_target_pairs={{0,15},{1,0},{2,1},{3,2},{4,3},{5,4},{6,5},{7,6},{8,7},{9,8},{10,9... | collective-permute-start | bytes 1769480 | tf_op jit(solution)/shard_map/ppermute | solution.py:25
  58.0 15.2 %collective-permute-start.4 = (bf16[32,8,1152]{2,1,0:T(8,128)(2,1)S(1)}, bf16[32,8,1152]{2,1,0:T(8,128)(2,1)S(1)}, u32[]{:S(2)}, u32[]{:S(2)}) collective-permute-start(bf16[32,8,1152]{2,1,0:T(8,128)(2,1)S(1)} %get-tuple-element.55), channel_id=1, source_target_pairs={{0,1},{1,2},{2,3},{3,4},{4,5},{5,6},{6,7},{7,8},{8,9},{9,10},{10,1... | collective-permute-start | bytes 1769480 | tf_op jit(solution)/shard_map/ppermute | solution.py:25
  66.0 12.8 %collective-permute-start.9 = (bf16[32,8,1152]{2,1,0:T(8,128)(2,1)S(1)}, bf16[32,8,1152]{2,1,0:T(8,128)(2,1)S(1)}, u32[]{:S(2)}, u32[]{:S(2)}) collective-permute-start(bf16[32,8,1152]{2,1,0:T(8,128)(2,1)S(1)} %get-tuple-element.72), channel_id=1, source_target_pairs={{0,15},{1,0},{2,1},{3,2},{4,3},{5,4},{6,5},{7,6},{8,7},{9,8},{10,9... | collective-permute-start | bytes 1769480 | tf_op jit(solution)/shard_map/ppermute | solution.py:25
  66.1 12.8 %collective-permute-start.8 = (bf16[32,8,1152]{2,1,0:T(8,128)(2,1)S(1)}, bf16[32,8,1152]{2,1,0:T(8,128)(2,1)S(1)}, u32[]{:S(2)}, u32[]{:S(2)}) collective-permute-start(bf16[32,8,1152]{2,1,0:T(8,128)(2,1)S(1)} %get-tuple-element.73), channel_id=1, source_target_pairs={{0,1},{1,2},{2,3},{3,4},{4,5},{5,6},{6,7},{7,8},{8,9},{9,10},{10,1... | collective-permute-start | bytes 1769480 | tf_op jit(solution)/shard_map/ppermute | solution.py:25
  73.6 22.4 %collective-permute-start.10 = (bf16[7,16,1152]{2,1,0:T(8,128)(2,1)S(1)}, bf16[7,16,1152]{2,1,0:T(8,128)(2,1)S(1)}, u32[]{:S(2)}, u32[]{:S(2)}) collective-permute-start(bf16[7,16,1152]{2,1,0:T(8,128)(2,1)S(1)} %get-tuple-element.52), channel_id=1, source_target_pairs={{0,16},{16,32},{32,48},{48,64},{64,80},{80,96},{96,112},{112,0},{1... | collective-permute-start | bytes 774152 | tf_op jit(solution)/shard_map/ppermute | solution.py:25
  76.1 19.9 %collective-permute-start.11 = (bf16[7,16,1152]{2,1,0:T(8,128)(2,1)S(1)}, bf16[7,16,1152]{2,1,0:T(8,128)(2,1)S(1)}, u32[]{:S(2)}, u32[]{:S(2)}) collective-permute-start(bf16[7,16,1152]{2,1,0:T(8,128)(2,1)S(1)} %get-tuple-element.53), channel_id=1, source_target_pairs={{0,112},{16,0},{32,16},{48,32},{64,48},{80,64},{96,80},{112,96},{1... | collective-permute-start | bytes 774152 | tf_op jit(solution)/shard_map/ppermute | solution.py:25
  78.8 1.7 %copy-start.4 = (bf16[1152,1152]{1,0:T(8,128)(2,1)S(1)}, bf16[1152,1152]{1,0:T(8,128)(2,1)}, u32[]{:S(2)}) copy-start(bf16[1152,1152]{1,0:T(8,128)(2,1)} %w_out.1) | copy-start | bytes 7962628

commit v2 on v1

--- a/solution.py
+++ b/solution.py
@@ -115,14 +115,28 @@
     )
 
 
-def fill_keys(kv_own, x_side, weights, kv):
-    skip = weights.shape[1] - kv.shape[1]
+def fetch(pairs, sems):
+    copies = [pltpu.make_async_copy(source, target, sems.at[i]) for i, (source, target) in enumerate(pairs)]
+    for copy in copies:
+        copy.start()
+    return copies
+
+
+def key_weights(w_ref, w_kv):
+    skip, columns = w_ref.shape[1] - w_kv.shape[1], w_kv.shape[1]
+    return [
+        (w_ref.at[:, pl.ds(skip + start, SPAN)], w_kv.at[:, pl.ds(start, SPAN)]) for start in range(0, columns, SPAN)
+    ]
+
+
+def fill_keys(kv_own, x_side, w_kv, copies, kv):
     for group in range(4):
         kv[GROUP * group : GROUP * group + HALF, :] = kv_own[HALF * group : HALF * (group + 1), :]
     for start in range(0, kv.shape[1], GROUP):
-        part = jnp.dot(
-            x_side[...], weights[:, skip + start : skip + start + GROUP], preferred_element_type=jnp.float32
-        ).astype(kv.dtype)
+        if start % SPAN == 0:
+            copies[start // SPAN].wait()
+        part = jnp.dot(x_side[...], w_kv[:, start : start + GROUP], preferred_element_type=jnp.float32)
+        part = part.astype(kv.dtype)
         for group in range(4):
             low = GROUP * group + HALF
             kv[low : low + HALF, start : start + GROUP] = part[HALF * group : HALF * (group + 1)]
@@ -183,13 +197,15 @@
 
 
 def forward_kernel(
-    head_dim, kv_own, x_side, weights, w_out, queries, bias, out_ref, kv, acc, scores0, scores1, probs0, probs1
+    head_dim, kv_own, x_side, w_ref, wo_ref, queries, bias, out_ref,
+    w_kv, w_out, kv, acc, scores0, scores1, probs0, probs1, sems
 ):
     width = queries.shape[1]
     factor = head_dim**-0.5 * math.log2(math.e)
     scores, probs = (scores0, scores1), (probs0, probs1)
+    copies = fetch(key_weights(w_ref, w_kv) + [(wo_ref, w_out)], sems)
     acc[...] = jnp.zeros_like(acc)
-    fill_keys(kv_own, x_side, weights, kv)
+    fill_keys(kv_own, x_side, w_kv, copies, kv)
 
     def scored(pair, u):
         start, masks = pair_lanes(pair, head_dim, width)
@@ -209,22 +225,25 @@
 
     run_pairs(width // head_dim // 2, scored, weighted, spread)
     attended = acc[...].astype(jnp.bfloat16)
+    copies[-1].wait()
     out_ref[...] = jnp.dot(attended, w_out[...], preferred_element_type=jnp.float32).astype(out_ref.dtype)
 
 
 def backward_kernel(
-    head_dim, kv_own, x_side, weights, queries, cotangents, bias, down_ref, dq_ref, dside_ref,
-    queries_t, cotangents_t, kv, dkv, acc, scores0, scores1, grads0, grads1, probs0, probs1, dscores0, dscores1
+    head_dim, kv_own, x_side, w_ref, queries, cotangents, bias, down_ref, dq_ref, dside_ref,
+    w_kv, queries_t, cotangents_t, kv, dkv, acc,
+    scores0, scores1, grads0, grads1, probs0, probs1, dscores0, dscores1, sems
 ):
     width = queries.shape[1]
     scaling = head_dim**-0.5
     factor = scaling * math.log2(math.e)
     scores, grads = (scores0, scores1), (grads0, grads1)
     probs, dscores = (probs0, probs1), (dscores0, dscores1)
+    copies = fetch(key_weights(w_ref, w_kv), sems)
     acc[...] = jnp.zeros_like(acc)
     turned(queries, queries_t)
     turned(cotangents, cotangents_t)
-    fill_keys(kv_own, x_side, weights, kv)
+    fill_keys(kv_own, x_side, w_kv, copies, kv)
 
     def scored(pair, u):
         start, masks = pair_lanes(pair, head_dim, width)
@@ -279,13 +298,15 @@
 
     dq_ref[...] = acc[...].astype(dq_ref.dtype)
     for start in range(0, dside_ref.shape[0], GROUP):
-        part = jnp.dot(weights[:, width:], dkv[:, start : start + GROUP], preferred_element_type=jnp.float32)
+        part = jnp.dot(w_kv[...], dkv[:, start : start + GROUP], preferred_element_type=jnp.float32)
         dside_ref[start : start + GROUP, :] = jnp.transpose(part).astype(dside_ref.dtype)
 
 
-def call_kernel(kernel, args, out_shape, scratch, flops, name):
+def call_kernel(kernel, args, out_shape, scratch, flops, name, fetched=()):
+    spaces = [pl.ANY if i in fetched else pltpu.VMEM for i in range(len(args))]
     return pl.pallas_call(
         kernel,
+        in_specs=[pl.BlockSpec(memory_space=space) for space in spaces],
         out_shape=out_shape,
         scratch_shapes=scratch,
         compiler_params=pltpu.CompilerParams(vmem_limit_bytes=LIMIT),
@@ -310,8 +331,14 @@
     tokens, width = queries.shape
     half, full = jnp.bfloat16, jnp.float32
     square = (2 * tokens, SPAN)
-    scratch = [pltpu.VMEM((KEYS, 2 * width), half), pltpu.VMEM((tokens, width), full)]
+    scratch = [
+        pltpu.VMEM((width, 2 * width), half),
+        pltpu.VMEM(w_out.shape, half),
+        pltpu.VMEM((KEYS, 2 * width), half),
+        pltpu.VMEM((tokens, width), full),
+    ]
     scratch += [pltpu.VMEM(square, full)] * 2 + [pltpu.VMEM(square, half)] * 2
+    scratch += [pltpu.SemaphoreType.DMA((2 * width // SPAN + 1,))]
     return call_kernel(
         functools.partial(forward_kernel, width // heads),
         [kv_own, x_side, w_qkv, w_out, queries, bias],
@@ -319,6 +346,7 @@
         scratch,
         2 * KEYS * width * width + 4 * heads * tokens * KEYS * LANES,
         "attention_forward",
+        fetched=(2, 3),
     )
 
 
@@ -329,6 +357,7 @@
     half, full = jnp.bfloat16, jnp.float32
     by_head = (heads, head_dim, tokens)
     scratch = [
+        pltpu.VMEM((width, 2 * width), half),
         pltpu.VMEM(by_head, half),
         pltpu.VMEM(by_head, half),
         pltpu.VMEM((KEYS, 2 * width), half),
@@ -336,6 +365,7 @@
         pltpu.VMEM((tokens, width), full),
     ]
     scratch += [pltpu.VMEM(square, full)] * 4 + [pltpu.VMEM(square, half)] * 4
+    scratch += [pltpu.SemaphoreType.DMA((2 * width // SPAN,))]
     return call_kernel(
         functools.partial(backward_kernel, head_dim),
         [kv_own, x_side, w_qkv, queries, cotangents, bias],
@@ -347,6 +377,7 @@
         scratch,
         4 * KEYS * width * width + 10 * heads * tokens * KEYS * LANES,
         "attention_backward",
+        fetched=(2,),
     )
 
 

time: 97.1 us -> 95.6 us (0.985)
  Pallas kernels: 49.3 us -> 47.6 us
    pallas_call x5, Pallas kernels: 49.3 us -> 47.6 us  [call_kernel(): pl.pallas_call(kernel, in_specs=[pl.BlockSpec(memory_space=space) for spa...]
  transfers between devices with their start and end apart: 12 -> 12, of which waited for: 3 -> 3; matrix products, arithmetic and copies ran while one was open for 10% -> 11% of each run, Pallas kernels for 51% -> 50%
where the time goes in v2:
time: 95.6 us; the launch traced here: 95.5 us
  Pallas kernels  47.6 us (50%)
  starting transfers between devices  25.2 us (26%)
  waiting for transfers between devices  7.61 us (8%)
  matrix products  7.04 us (7%)
  local copies, waits for them, and re-layouts  4.34 us (5%)
  other arithmetic  2.64 us (3%)
  between operations  1.03 us (1%)
    pallas_call x5, Pallas kernels, call_kernel(): pl.pallas_call(kernel, in_specs=[pl.BlockSpec(memory_space=space) for spa...  47.6 us
    ppermute x12, starting transfers between devices, shifted(): lax.ppermute(value, axis, [(i, (i + step) % count) for i in range(count)])  25.2 us
    ppermute x12, waiting for transfers between devices, shifted(): lax.ppermute(value, axis, [(i, (i + step) % count) for i in range(count)])  7.61 us
    dot_general x2, matrix products, project(): jnp.dot(x, w, preferred_element_type=jnp.float32).astype(jnp.bfloat16)  5.99 us
  transfers between devices with their start and end apart: 12, of which 3 were waited for; matrix products, arithmetic and copies ran while one was open for 11% of the time, Pallas kernels for 50%

profile of v2, /device:TPU:7, one launch (start us, length us, event | category | flops | bytes accessed | tf_op | source)
XLA Modules:
  0.0 95.5 jit_solution(15084957896170351051)
XLA Ops:
  0.6 0.0 copy-start
  0.6 1.2 %fusion.25 = (bf16[7,16,1152]{2,1,0:T(8,128)(2,1)S(1)}, bf16[7,16,1152]{2,1,0:T(8,128)(2,1)S(1)}) fusion(bf16[16,16,1152]{2,1,0:T(8,128)(2,1)} %param.6), kind=kLoop, calls=%fused_computation.68 | loop fusion | bytes 1032192 | tf_op jit(solution)/shard_map/slice | solution.py:29
  1.8 6.5 %collective-permute-start.1 = (bf16[7,16,1152]{2,1,0:T(8,128)(2,1)S(1)}, bf16[7,16,1152]{2,1,0:T(8,128)(2,1)S(1)}, u32[]{:S(2)}, u32[]{:S(2)}) collective-permute-start(bf16[7,16,1152]{2,1,0:T(8,128)(2,1)S(1)} %get-tuple-element.62), channel_id=1, source_target_pairs={{0,112},{16,0},{32,16},{48,32},{64,48},{80,64},{96,80},{112,96},{1... | collective-permute-start | bytes 774152 | tf_op jit(solution)/shard_map/ppermute | solution.py:25
  8.3 0.0 collective-permute-start
  8.4 1.1 %fusion.24 = (bf16[16,8,1152]{2,1,0:T(8,128)(2,1)S(1)}, bf16[16,8,1152]{2,1,0:T(8,128)(2,1)S(1)}) fusion(bf16[16,16,1152]{2,1,0:T(8,128)(2,1)} %param.6), kind=kLoop, calls=%fused_computation.67 | loop fusion | bytes 1179648 | tf_op jit(solution)/shard_map/slice | solution.py:34
  9.5 0.0 copy-start.2
  9.5 0.0 copy-start.3
  9.5 3.1 %convolution_convert_fusion.2.queries = bf16[256,1152]{1,0:T(8,128)(2,1)S(1)} fusion(bf16[256,1152]{1,0:T(8,128)(2,1)} %bitcast.24, bf16[1152,3456]{1,0:T(8,128)(2,1)} %w_ref.3), kind=kOutput, calls=%fused_computation.2 | convolution fusion | flops 679772160 | bytes 3833856 | tf_op jit(solution)/shard_map/dot_general | solution.py:385
  12.6 0.0 slice-start
  12.6 2.9 %convolution_convert_fusion.1.queries = bf16[256,1152]{1,0:T(8,128)(2,1)S(1)} fusion(bf16[256,1152]{1,0:T(8,128)(2,1)S(1)} %bitcast.26, bf16[1152,3456]{1,0:T(8,128)(2,1)} %w_ref.3), kind=kOutput, calls=%fused_computation.1 | convolution fusion | flops 679772160 | bytes 3833856 | tf_op jit(solution)/shard_map/dot_general | solution.py:385
  15.5 0.1 pad.25.clone
  15.6 0.7 and_select_fusion.bias
  16.4 0.0 slice-start.1
  16.4 1.1 %convolution_convert_fusion.cotangents = bf16[256,1152]{1,0:T(8,128)(2,1)S(1)} fusion(bf16[256,1152]{1,0:T(8,128)(2,1)S(1)} %bitcast.18, bf16[1152,1152]{1,0:T(8,128)(2,1)S(1)} %copy-done.3), kind=kOutput, calls=%fused_computation | convolution fusion | flops 679772160 | bytes 3833856 | tf_op jit(solution)/shard_map/dot_general | solution.py:398
  17.5 0.0 copy-start.1
  17.5 0.0 collective-permute-done.1
  17.5 2.2 %collective-permute-done = bf16[7,16,1152]{2,1,0:T(8,128)(2,1)S(1)} collective-permute-done((bf16[7,16,1152]{2,1,0:T(8,128)(2,1)S(1)}, bf16[7,16,1152]{2,1,0:T(8,128)(2,1)S(1)}, u32[]{:S(2)}, u32[]{:S(2)}) %collective-permute-start) | collective-permute-done | bytes 258080 | tf_op jit(solution)/shard_map/ppermute | solution.py:25
  19.7 0.2 maximum_maximum_fusion.1
  19.9 2.5 %collective-permute-start.2 = (bf16[32,8,1152]{2,1,0:T(8,128)(2,1)S(1)}, bf16[32,8,1152]{2,1,0:T(8,128)(2,1)S(1)}, u32[]{:S(2)}, u32[]{:S(2)}) collective-permute-start(bf16[32,8,1152]{2,1,0:T(8,128)(2,1)S(1)} %get-tuple-element.26), channel_id=1, source_target_pairs={{0,1},{1,2},{2,3},{3,4},{4,5},{5,6},{6,7},{7,8},{8,9},{9,10},{10,1... | collective-permute-start | bytes 1769480 | tf_op jit(solution)/shard_map/ppermute | solution.py:25
  22.5 0.0 collective-permute-start.3
  22.5 2.6 %collective-permute-start.7 = (bf16[7,16,1152]{2,1,0:T(8,128)(2,1)S(1)}, bf16[7,16,1152]{2,1,0:T(8,128)(2,1)S(1)}, u32[]{:S(2)}, u32[]{:S(2)}) collective-permute-start(bf16[7,16,1152]{2,1,0:T(8,128)(2,1)S(1)} %get-tuple-element.58), channel_id=1, source_target_pairs={{0,112},{16,0},{32,16},{48,32},{64,48},{80,64},{96,80},{112,96},{1... | collective-permute-start | bytes 774152 | tf_op jit(solution)/shard_map/ppermute | solution.py:25
  25.1 0.5 collective-permute-start.6
  25.6 3.2 %own_keys.2.kv_own = bf16[512,2304]{1,0:T(8,128)(2,1)S(1)} custom-call(bf16[112,1152]{1,0:T(8,128)(2,1)S(1)} %bitcast.32, bf16[256,1152]{1,0:T(8,128)(2,1)S(1)} %bitcast.25, bf16[112,1152]{1,0:T(8,128)(2,1)S(1)} %bitcast.31, bf16[1152,3456]{1,0:T(8,128)(2,1)S(1)} %bitcast.20), custom_call_target="tpu_custom_call" | custom-call | flops 2717908992 | bytes 16777216 | tf_op jit(solution)/shard_map/own_keys/pallas_call | solution.py:307
  28.8 0.5 collective-permute-done.2
  29.3 4.9 %collective-permute-done.3 = bf16[32,8,1152]{2,1,0:T(8,128)(2,1)S(1)} collective-permute-done((bf16[32,8,1152]{2,1,0:T(8,128)(2,1)S(1)}, bf16[32,8,1152]{2,1,0:T(8,128)(2,1)S(1)}, u32[]{:S(2)}, u32[]{:S(2)}) %collective-permute-start.3) | collective-permute-done | bytes 589856 | tf_op jit(solution)/shard_map/ppermute | solution.py:25
  34.2 0.1 pad_maximum_fusion
  34.3 0.0 slice-start.2
  34.3 22.6 %attention_backward.1 = (bf16[2304,512]{1,0:T(8,128)(2,1)S(1)}, bf16[256,1152]{1,0:T(8,128)(2,1)S(1)}, bf16[512,1152]{1,0:T(8,128)(2,1)S(1)}) custom-call(bf16[512,2304]{1,0:T(8,128)(2,1)S(1)} %own_keys.2.kv_own, bf16[512,1152]{1,0:T(8,128)(2,1)S(1)} %bitcast.29, bf16[1152,3456]{1,0:T(8,128)(2,1)} %w_ref.3, ...), custom_call_target="tpu_custom_call" | custom-call | flops 16173236224 | bytes 16777216 | tf_op jit(solution)/shard_map/attention_backward/pallas_call | solution.py:307
  56.9 0.1 fusion.21
  57.0 0.3 collective-permute-start.5
  57.3 3.8 %collective-permute-start.4 = (bf16[32,8,1152]{2,1,0:T(8,128)(2,1)S(1)}, bf16[32,8,1152]{2,1,0:T(8,128)(2,1)S(1)}, u32[]{:S(2)}, u32[]{:S(2)}) collective-permute-start(bf16[32,8,1152]{2,1,0:T(8,128)(2,1)S(1)} %get-tuple-element.55), channel_id=1, source_target_pairs={{0,1},{1,2},{2,3},{3,4},{4,5},{5,6},{6,7},{7,8},{8,9},{9,10},{10,1... | collective-permute-start | bytes 1769480 | tf_op jit(solution)/shard_map/ppermute | solution.py:25
  61.2 3.8 %own_gradient.1 = f32[512,1152]{1,0:T(8,128)S(1)} custom-call(bf16[2304,512]{1,0:T(8,128)(2,1)S(1)} %get-tuple-element.36.dkv, bf16[256,1152]{1,0:T(8,128)(2,1)S(1)} %get-tuple-element.37.dq, bf16[1152,3456]{1,0:T(8,128)(2,1)S(1)} %bitcast.22), custom_call_target="tpu_custom_call" | custom-call | flops 2717908992 | bytes 16777216 | tf_op jit(solution)/shard_map/own_gradient/pallas_call | solution.py:307
  64.9 0.0 collective-permute-done.7
  65.1 0.2 maximum_maximum_fusion.3
  65.3 0.1 collective-permute-start.9
  65.4 3.8 %collective-permute-start.8 = (bf16[32,8,1152]{2,1,0:T(8,128)(2,1)S(1)}, bf16[32,8,1152]{2,1,0:T(8,128)(2,1)S(1)}, u32[]{:S(2)}, u32[]{:S(2)}) collective-permute-start(bf16[32,8,1152]{2,1,0:T(8,128)(2,1)S(1)} %get-tuple-element.73), channel_id=1, source_target_pairs={{0,1},{1,2},{2,3},{3,4},{4,5},{5,6},{6,7},{7,8},{8,9},{9,10},{10,1... | collective-permute-start | bytes 1769480 | tf_op jit(solution)/shard_map/ppermute | solution.py:25
  69.2 3.3 %own_keys.3.kv_own = bf16[512,2304]{1,0:T(8,128)(2,1)S(1)} custom-call(bf16[112,1152]{1,0:T(8,128)(2,1)S(1)} %bitcast.34, bf16[256,1152]{1,0:T(8,128)(2,1)S(1)} %bitcast.27, bf16[112,1152]{1,0:T(8,128)(2,1)S(1)} %bitcast.33, bf16[1152,3456]{1,0:T(8,128)(2,1)S(1)} %bitcast.22), custom_call_target="tpu_custom_call" | custom-call | flops 2717908992 | bytes 16777216 | tf_op jit(solution)/shard_map/own_keys/pallas_call | solution.py:307
  72.6 0.0 collective-permute-done.4
  72.6 0.3 fusion.19
  72.9 2.5 %collective-permute-start.10 = (bf16[7,16,1152]{2,1,0:T(8,128)(2,1)S(1)}, bf16[7,16,1152]{2,1,0:T(8,128)(2,1)S(1)}, u32[]{:S(2)}, u32[]{:S(2)}) collective-permute-start(bf16[7,16,1152]{2,1,0:T(8,128)(2,1)S(1)} %get-tuple-element.52), channel_id=1, source_target_pairs={{0,16},{16,32},{32,48},{48,64},{64,80},{80,96},{96,112},{112,0},{1... | collective-permute-start | bytes 774152 | tf_op jit(solution)/shard_map/ppermute | solution.py:25
  75.5 2.6 %collective-permute-start.11 = (bf16[7,16,1152]{2,1,0:T(8,128)(2,1)S(1)}, bf16[7,16,1152]{2,1,0:T(8,128)(2,1)S(1)}, u32[]{:S(2)}, u32[]{:S(2)}) collective-permute-start(bf16[7,16,1152]{2,1,0:T(8,128)(2,1)S(1)} %get-tuple-element.53), channel_id=1, source_target_pairs={{0,112},{16,0},{32,16},{48,32},{64,48},{80,64},{96,80},{112,96},{1... | collective-permute-start | bytes 774152 | tf_op jit(solution)/shard_map/ppermute | solution.py:25
  78.1 0.1 slice.96
  78.2 0.0 collective-permute-done.8
  78.2 0.1 pad_maximum_fusion.1
  78.3 1.5 %copy-done.4 = bf16[1152,1152]{1,0:T(8,128)(2,1)S(1)} copy-done((bf16[1152,1152]{1,0:T(8,128)(2,1)S(1)}, bf16[1152,1152]{1,0:T(8,128)(2,1)}, u32[]{:S(2)}) %copy-start.4) | copy-done | bytes 2654232
  79.8 14.7 %attention_forward.1 = bf16[256,1152]{1,0:T(8,128)(2,1)} custom-call(bf16[512,2304]{1,0:T(8,128)(2,1)S(1)} %own_keys.3.kv_own, bf16[512,1152]{1,0:T(8,128)(2,1)S(1)} %bitcast.30, bf16[1152,3456]{1,0:T(8,128)(2,1)} %w_ref.3, bf16[1152,1152]{1,0:T(8,128)(2,1)S(1)} %copy-done.4, bf16[256,1152]{1,0:T(8,128)(2,1)S(1)} %convolution_convert_fusion.1.queries, ...), custom_call_target="tpu_custom_call" | custom-call | flops 7012876288 | bytes 16777216 | tf_op jit(solution)/shard_map/attention_forward/pallas_call | solution.py:307
  94.5 0.0 collective-permute-done.11
  94.5 0.9 add_convert_fusion
  (32 shorter events, 0.3 us)
Async XLA Ops:
  0.6 15.7 %copy-start = (bf16[16,16,1152]{2,1,0:T(8,128)(2,1)S(1)}, bf16[16,16,1152]{2,1,0:T(8,128)(2,1)}, u32[]{:S(2)}) copy-start(bf16[16,16,1152]{2,1,0:T(8,128)(2,1)} %param.7) | copy-start | bytes 1769476
  1.8 15.6 %collective-permute-start.1 = (bf16[7,16,1152]{2,1,0:T(8,128)(2,1)S(1)}, bf16[7,16,1152]{2,1,0:T(8,128)(2,1)S(1)}, u32[]{:S(2)}, u32[]{:S(2)}) collective-permute-start(bf16[7,16,1152]{2,1,0:T(8,128)(2,1)S(1)} %get-tuple-element.62), channel_id=1, source_target_pairs={{0,112},{16,0},{32,16},{48,32},{64,48},{80,64},{96,80},{112,96},{1... | collective-permute-start | bytes 774152 | tf_op jit(solution)/shard_map/ppermute | solution.py:25
  8.3 11.4 %collective-permute-start = (bf16[7,16,1152]{2,1,0:T(8,128)(2,1)S(1)}, bf16[7,16,1152]{2,1,0:T(8,128)(2,1)S(1)}, u32[]{:S(2)}, u32[]{:S(2)}) collective-permute-start(bf16[7,16,1152]{2,1,0:T(8,128)(2,1)S(1)} %get-tuple-element.63), channel_id=1, source_target_pairs={{0,16},{16,32},{32,48},{48,64},{64,80},{80,96},{96,112},{112,0},{1... | collective-permute-start | bytes 774152 | tf_op jit(solution)/shard_map/ppermute | solution.py:25
  9.5 3.1 %copy-start.2 = (bf16[16,16,1152]{2,1,0:T(8,128)(2,1)S(1)}, bf16[16,16,1152]{2,1,0:T(8,128)(2,1)}, u32[]{:S(2)}) copy-start(bf16[16,16,1152]{2,1,0:T(8,128)(2,1)} %param.5) | copy-start | bytes 1769476
  9.5 6.9 %copy-start.3 = (bf16[1152,1152]{1,0:T(8,128)(2,1)S(1)}, bf16[1152,1152]{1,0:T(8,128)(2,1)}, u32[]{:S(2)}) copy-start(bf16[1152,1152]{1,0:T(8,128)(2,1)} %wo_ref.1) | copy-start | bytes 7962628
  12.6 12.9 %slice-start = ((s8[7962624]{0:T(1024)(128)(4,1)}), s8[4194304]{0:T(1024)(128)(4,1)S(1)}, s32[]{:S(2)}) async-start(s8[7962624]{0:T(1024)(128)(4,1)} %bitcast.19), calls=%async_computation | async-start | bytes 8388608
  16.4 9.2 %slice-start.1 = ((s8[7962624]{0:T(1024)(128)(4,1)}), s8[3768320]{0:T(1024)(128)(4,1)S(1)}, s32[]{:S(2)}) async-start(s8[7962624]{0:T(1024)(128)(4,1)} %bitcast.19), calls=%async_computation.1 | async-start | bytes 7536640
  17.5 8.1 %copy-start.1 = (bf16[16,16,1152]{2,1,0:T(8,128)(2,1)S(1)}, bf16[16,16,1152]{2,1,0:T(8,128)(2,1)}, u32[]{:S(2)}) copy-start(bf16[16,16,1152]{2,1,0:T(8,128)(2,1)} %param.6) | copy-start | bytes 1769476
  19.9 9.4 %collective-permute-start.2 = (bf16[32,8,1152]{2,1,0:T(8,128)(2,1)S(1)}, bf16[32,8,1152]{2,1,0:T(8,128)(2,1)S(1)}, u32[]{:S(2)}, u32[]{:S(2)}) collective-permute-start(bf16[32,8,1152]{2,1,0:T(8,128)(2,1)S(1)} %get-tuple-element.26), channel_id=1, source_target_pairs={{0,1},{1,2},{2,3},{3,4},{4,5},{5,6},{6,7},{7,8},{8,9},{9,10},{10,1... | collective-permute-start | bytes 1769480 | tf_op jit(solution)/shard_map/ppermute | solution.py:25
  22.5 11.8 %collective-permute-start.3 = (bf16[32,8,1152]{2,1,0:T(8,128)(2,1)S(1)}, bf16[32,8,1152]{2,1,0:T(8,128)(2,1)S(1)}, u32[]{:S(2)}, u32[]{:S(2)}) collective-permute-start(bf16[32,8,1152]{2,1,0:T(8,128)(2,1)S(1)} %get-tuple-element.27), channel_id=1, source_target_pairs={{0,15},{1,0},{2,1},{3,2},{4,3},{5,4},{6,5},{7,6},{8,7},{9,8},{10,9... | collective-permute-start | bytes 1769480 | tf_op jit(solution)/shard_map/ppermute | solution.py:25
  22.5 42.4 %collective-permute-start.7 = (bf16[7,16,1152]{2,1,0:T(8,128)(2,1)S(1)}, bf16[7,16,1152]{2,1,0:T(8,128)(2,1)S(1)}, u32[]{:S(2)}, u32[]{:S(2)}) collective-permute-start(bf16[7,16,1152]{2,1,0:T(8,128)(2,1)S(1)} %get-tuple-element.58), channel_id=1, source_target_pairs={{0,112},{16,0},{32,16},{48,32},{64,48},{80,64},{96,80},{112,96},{1... | collective-permute-start | bytes 774152 | tf_op jit(solution)/shard_map/ppermute | solution.py:25
  25.1 39.9 %collective-permute-start.6 = (bf16[7,16,1152]{2,1,0:T(8,128)(2,1)S(1)}, bf16[7,16,1152]{2,1,0:T(8,128)(2,1)S(1)}, u32[]{:S(2)}, u32[]{:S(2)}) collective-permute-start(bf16[7,16,1152]{2,1,0:T(8,128)(2,1)S(1)} %get-tuple-element.59), channel_id=1, source_target_pairs={{0,16},{16,32},{32,48},{48,64},{64,80},{80,96},{96,112},{112,0},{1... | collective-permute-start | bytes 774152 | tf_op jit(solution)/shard_map/ppermute | solution.py:25
  34.3 26.9 %slice-start.2 = ((s8[7962624]{0:T(1024)(128)(4,1)}), s8[4194304]{0:T(1024)(128)(4,1)S(1)}, s32[]{:S(2)}) async-start(s8[7962624]{0:T(1024)(128)(4,1)} %bitcast.21), calls=%async_computation.2 | async-start | bytes 8388608
  34.3 26.9 %slice-start.3 = ((s8[7962624]{0:T(1024)(128)(4,1)}), s8[3768320]{0:T(1024)(128)(4,1)S(1)}, s32[]{:S(2)}) async-start(s8[7962624]{0:T(1024)(128)(4,1)} %bitcast.21), calls=%async_computation.3 | async-start | bytes 7536640
  57.0 15.5 %collective-permute-start.5 = (bf16[32,8,1152]{2,1,0:T(8,128)(2,1)S(1)}, bf16[32,8,1152]{2,1,0:T(8,128)(2,1)S(1)}, u32[]{:S(2)}, u32[]{:S(2)}) collective-permute-start(bf16[32,8,1152]{2,1,0:T(8,128)(2,1)S(1)} %get-tuple-element.54), channel_id=1, source_target_pairs={{0,15},{1,0},{2,1},{3,2},{4,3},{5,4},{6,5},{7,6},{8,7},{9,8},{10,9... | collective-permute-start | bytes 1769480 | tf_op jit(solution)/shard_map/ppermute | solution.py:25
  57.3 15.2 %collective-permute-start.4 = (bf16[32,8,1152]{2,1,0:T(8,128)(2,1)S(1)}, bf16[32,8,1152]{2,1,0:T(8,128)(2,1)S(1)}, u32[]{:S(2)}, u32[]{:S(2)}) collective-permute-start(bf16[32,8,1152]{2,1,0:T(8,128)(2,1)S(1)} %get-tuple-element.55), channel_id=1, source_target_pairs={{0,1},{1,2},{2,3},{3,4},{4,5},{5,6},{6,7},{7,8},{8,9},{9,10},{10,1... | collective-permute-start | bytes 1769480 | tf_op jit(solution)/shard_map/ppermute | solution.py:25
  65.3 12.8 %collective-permute-start.9 = (bf16[32,8,1152]{2,1,0:T(8,128)(2,1)S(1)}, bf16[32,8,1152]{2,1,0:T(8,128)(2,1)S(1)}, u32[]{:S(2)}, u32[]{:S(2)}) collective-permute-start(bf16[32,8,1152]{2,1,0:T(8,128)(2,1)S(1)} %get-tuple-element.72), channel_id=1, source_target_pairs={{0,15},{1,0},{2,1},{3,2},{4,3},{5,4},{6,5},{7,6},{8,7},{9,8},{10,9... | collective-permute-start | bytes 1769480 | tf_op jit(solution)/shard_map/ppermute | solution.py:25
  65.4 12.8 %collective-permute-start.8 = (bf16[32,8,1152]{2,1,0:T(8,128)(2,1)S(1)}, bf16[32,8,1152]{2,1,0:T(8,128)(2,1)S(1)}, u32[]{:S(2)}, u32[]{:S(2)}) collective-permute-start(bf16[32,8,1152]{2,1,0:T(8,128)(2,1)S(1)} %get-tuple-element.73), channel_id=1, source_target_pairs={{0,1},{1,2},{2,3},{3,4},{4,5},{5,6},{6,7},{7,8},{8,9},{9,10},{10,1... | collective-permute-start | bytes 1769480 | tf_op jit(solution)/shard_map/ppermute | solution.py:25
  72.9 21.6 %collective-permute-start.10 = (bf16[7,16,1152]{2,1,0:T(8,128)(2,1)S(1)}, bf16[7,16,1152]{2,1,0:T(8,128)(2,1)S(1)}, u32[]{:S(2)}, u32[]{:S(2)}) collective-permute-start(bf16[7,16,1152]{2,1,0:T(8,128)(2,1)S(1)} %get-tuple-element.52), channel_id=1, source_target_pairs={{0,16},{16,32},{32,48},{48,64},{64,80},{80,96},{96,112},{112,0},{1... | collective-permute-start | bytes 774152 | tf_op jit(solution)/shard_map/ppermute | solution.py:25
  75.5 19.1 %collective-permute-start.11 = (bf16[7,16,1152]{2,1,0:T(8,128)(2,1)S(1)}, bf16[7,16,1152]{2,1,0:T(8,128)(2,1)S(1)}, u32[]{:S(2)}, u32[]{:S(2)}) collective-permute-start(bf16[7,16,1152]{2,1,0:T(8,128)(2,1)S(1)} %get-tuple-element.53), channel_id=1, source_target_pairs={{0,112},{16,0},{32,16},{48,32},{64,48},{80,64},{96,80},{112,96},{1... | collective-permute-start | bytes 774152 | tf_op jit(solution)/shard_map/ppermute | solution.py:25
  78.1 1.7 %copy-start.4 = (bf16[1152,1152]{1,0:T(8,128)(2,1)S(1)}, bf16[1152,1152]{1,0:T(8,128)(2,1)}, u32[]{:S(2)}) copy-start(bf16[1152,1152]{1,0:T(8,128)(2,1)} %wo_ref.1) | copy-start | bytes 7962628

commit v3 on v2

--- a/solution.py
+++ b/solution.py
@@ -411,15 +411,15 @@
         own_backward, side_backward, w_qkv, q_backward, grad_heads, bias, heads
     )
     dx_side = dx_side.reshape(2 * SIDE, SIDE, width)
-    from_right = shifted(dx_side[:, :8], "heads", -1)
-    from_left = shifted(dx_side[:, 8:], "heads", 1)
+    parts_forward, _ = lax.optimization_barrier((parts_forward, dx_side))
+    to_right, to_left = column_sends(parts_forward)
+    from_left = shifted(jnp.concatenate([dx_side[:, 8:], to_right], 0), "heads", 1)
+    from_right = shifted(jnp.concatenate([dx_side[:, :8], to_left], 0), "heads", -1)
+    own_forward = own_keys([flat(part) for part in parts_forward], w_qkv)
     dx_own = own_gradient(dkv_own, dq, w_qkv).reshape(2 * SIDE, SIDE, width)
-    parts_forward, _ = lax.optimization_barrier((parts_forward, dx_own))
-    sends_forward = column_sends(parts_forward)
-    side_forward = flat(side_columns(sends_forward))
-    parts_forward, _ = lax.optimization_barrier((parts_forward, sends_forward))
-    own_forward = own_keys([flat(part) for part in parts_forward], w_qkv)
     from_left, from_right, own_forward = lax.optimization_barrier((from_left, from_right, own_forward))
+    side_forward = flat(jnp.concatenate([from_left[2 * SIDE :], from_right[2 * SIDE :]], 1))
+    from_left, from_right = from_left[: 2 * SIDE], from_right[: 2 * SIDE]
     total = dx_own + jnp.concatenate([from_left, from_right], 1).astype(jnp.float32)
     from_below = shifted(total[:RADIUS].astype(jnp.bfloat16), "rows", -1)
     from_above = shifted(total[RADIUS + SIDE : 2 * RADIUS + SIDE].astype(jnp.bfloat16), "rows", 1)

time: 95.6 us -> 98.1 us (1.026)
  waiting for transfers between devices: 7.61 us -> 19.4 us
  starting transfers between devices: 25.2 us -> 17.7 us
    ppermute x12 -> x10, waiting for transfers between devices: 7.61 us -> 19.4 us  [shifted(): lax.ppermute(value, axis, [(i, (i + step) % count) for i in range(count)])]
    ppermute x12 -> x10, starting transfers between devices: 25.2 us -> 17.7 us  [shifted(): lax.ppermute(value, axis, [(i, (i + step) % count) for i in range(count)])]
    slice x6 -> x3, local copies, waits for them, and re-layouts: 1.23 us -> 0.09 us  [column_sends(): part[:, side]]
  transfers between devices with their start and end apart: 12 -> 10, of which waited for: 3 -> 5; matrix products, arithmetic and copies ran while one was open for 11% -> 8% of each run, Pallas kernels for 50% -> 48%
where the time goes in v3:
time: 98.1 us; the launch traced here: 97.9 us
  Pallas kernels  46.9 us (48%)
  waiting for transfers between devices  19.4 us (20%)
  starting transfers between devices  17.7 us (18%)
  matrix products  6.87 us (7%)
  local copies, waits for them, and re-layouts  3.51 us (4%)
  other arithmetic  2.42 us (2%)
  between operations  1.02 us (1%)
    pallas_call x5, Pallas kernels, call_kernel(): pl.pallas_call(kernel, in_specs=[pl.BlockSpec(memory_space=space) for spa...  46.9 us
    ppermute x10, waiting for transfers between devices, shifted(): lax.ppermute(value, axis, [(i, (i + step) % count) for i in range(count)])  19.4 us
    ppermute x10, starting transfers between devices, shifted(): lax.ppermute(value, axis, [(i, (i + step) % count) for i in range(count)])  17.7 us
    dot_general x2, matrix products, project(): jnp.dot(x, w, preferred_element_type=jnp.float32).astype(jnp.bfloat16)  5.81 us
  transfers between devices with their start and end apart: 10, of which 5 were waited for; matrix products, arithmetic and copies ran while one was open for 8% of the time, Pallas kernels for 48%

profile of v3, /device:TPU:7, one launch (start us, length us, event | category | flops | bytes accessed | tf_op | source)
XLA Modules:
  0.0 97.9 jit_solution(13402021295148770694)
XLA Ops:
  0.6 0.0 copy-start
  0.7 1.2 %fusion.25 = (bf16[7,16,1152]{2,1,0:T(8,128)(2,1)S(1)}, bf16[7,16,1152]{2,1,0:T(8,128)(2,1)S(1)}) fusion(bf16[16,16,1152]{2,1,0:T(8,128)(2,1)} %param.6), kind=kLoop, calls=%fused_computation.76 | loop fusion | bytes 1032192 | tf_op jit(solution)/shard_map/slice | solution.py:29
  1.9 6.5 %collective-permute-start.1 = (bf16[7,16,1152]{2,1,0:T(8,128)(2,1)S(1)}, bf16[7,16,1152]{2,1,0:T(8,128)(2,1)S(1)}, u32[]{:S(2)}, u32[]{:S(2)}) collective-permute-start(bf16[7,16,1152]{2,1,0:T(8,128)(2,1)S(1)} %get-tuple-element.60), channel_id=1, source_target_pairs={{0,112},{16,0},{32,16},{48,32},{64,48},{80,64},{96,80},{112,96},{1... | collective-permute-start | bytes 774152 | tf_op jit(solution)/shard_map/ppermute | solution.py:25
  8.3 0.0 collective-permute-start
  8.5 0.0 copy-start.2
  8.5 0.0 copy-start.3
  8.5 2.9 %convolution_convert_fusion.2.queries = bf16[256,1152]{1,0:T(8,128)(2,1)S(1)} fusion(bf16[256,1152]{1,0:T(8,128)(2,1)S(1)} %bitcast.24, bf16[1152,3456]{1,0:T(8,128)(2,1)} %w_ref.3), kind=kOutput, calls=%fused_computation.2 | convolution fusion | flops 679772160 | bytes 3833856 | tf_op jit(solution)/shard_map/dot_general | solution.py:385
  11.4 0.0 slice-start
  11.4 2.9 %convolution_convert_fusion.1.queries = bf16[256,1152]{1,0:T(8,128)(2,1)S(1)} fusion(bf16[256,1152]{1,0:T(8,128)(2,1)S(1)} %bitcast.26, bf16[1152,3456]{1,0:T(8,128)(2,1)} %w_ref.3), kind=kOutput, calls=%fused_computation.1 | convolution fusion | flops 679772160 | bytes 3833856 | tf_op jit(solution)/shard_map/dot_general | solution.py:385
  14.4 0.7 and_select_fusion.bias
  15.1 0.0 slice-start.1
  15.1 1.1 %convolution_convert_fusion.cotangents = bf16[256,1152]{1,0:T(8,128)(2,1)S(1)} fusion(bf16[256,1152]{1,0:T(8,128)(2,1)S(1)} %bitcast.18, bf16[1152,1152]{1,0:T(8,128)(2,1)S(1)} %copy-done.3), kind=kOutput, calls=%fused_computation | convolution fusion | flops 679772160 | bytes 3833856 | tf_op jit(solution)/shard_map/dot_general | solution.py:398
  16.2 0.0 collective-permute-done.1
  16.2 3.5 %collective-permute-done = bf16[7,16,1152]{2,1,0:T(8,128)(2,1)S(1)} collective-permute-done((bf16[7,16,1152]{2,1,0:T(8,128)(2,1)S(1)}, bf16[7,16,1152]{2,1,0:T(8,128)(2,1)S(1)}, u32[]{:S(2)}, u32[]{:S(2)}) %collective-permute-start) | collective-permute-done | bytes 258080 | tf_op jit(solution)/shard_map/ppermute | solution.py:25
  19.8 0.2 pad_maximum_fusion.2
  20.0 2.5 %collective-permute-start.2 = (bf16[32,8,1152]{2,1,0:T(8,128)(2,1)S(1)}, bf16[32,8,1152]{2,1,0:T(8,128)(2,1)S(1)}, u32[]{:S(2)}, u32[]{:S(2)}) collective-permute-start(bf16[32,8,1152]{2,1,0:T(8,128)(2,1)S(1)} %get-tuple-element.23), channel_id=1, source_target_pairs={{0,1},{1,2},{2,3},{3,4},{4,5},{5,6},{6,7},{7,8},{8,9},{9,10},{10,1... | collective-permute-start | bytes 1769480 | tf_op jit(solution)/shard_map/ppermute | solution.py:25
  22.5 0.0 collective-permute-start.3
  22.5 2.5 %collective-permute-start.5 = (bf16[7,16,1152]{2,1,0:T(8,128)(2,1)S(1)}, bf16[7,16,1152]{2,1,0:T(8,128)(2,1)S(1)}, u32[]{:S(2)}, u32[]{:S(2)}) collective-permute-start(bf16[7,16,1152]{2,1,0:T(8,128)(2,1)S(1)} %get-tuple-element.56), channel_id=1, source_target_pairs={{0,112},{16,0},{32,16},{48,32},{64,48},{80,64},{96,80},{112,96},{1... | collective-permute-start | bytes 774152 | tf_op jit(solution)/shard_map/ppermute | solution.py:25
  25.1 0.5 collective-permute-start.4
  25.6 3.2 %own_keys.2.kv_own = bf16[512,2304]{1,0:T(8,128)(2,1)S(1)} custom-call(bf16[112,1152]{1,0:T(8,128)(2,1)S(1)} %bitcast.32, bf16[256,1152]{1,0:T(8,128)(2,1)S(1)} %bitcast.25, bf16[112,1152]{1,0:T(8,128)(2,1)S(1)} %bitcast.31, bf16[1152,3456]{1,0:T(8,128)(2,1)S(1)} %bitcast.20), custom_call_target="tpu_custom_call" | custom-call | flops 2717908992 | bytes 16777216 | tf_op jit(solution)/shard_map/own_keys/pallas_call | solution.py:307
  28.8 0.5 collective-permute-done.2
  29.4 4.9 %collective-permute-done.3 = bf16[32,8,1152]{2,1,0:T(8,128)(2,1)S(1)} collective-permute-done((bf16[32,8,1152]{2,1,0:T(8,128)(2,1)S(1)}, bf16[32,8,1152]{2,1,0:T(8,128)(2,1)S(1)}, u32[]{:S(2)}, u32[]{:S(2)}) %collective-permute-start.3) | collective-permute-done | bytes 589856 | tf_op jit(solution)/shard_map/ppermute | solution.py:25
  34.3 0.1 pad_maximum_fusion
  34.3 0.0 slice-start.2
  34.4 0.0 slice-start.3
  34.4 22.4 %attention_backward.1 = (bf16[2304,512]{1,0:T(8,128)(2,1)S(1)}, bf16[256,1152]{1,0:T(8,128)(2,1)S(1)}, bf16[512,1152]{1,0:T(8,128)(2,1)S(1)}) custom-call(bf16[512,2304]{1,0:T(8,128)(2,1)S(1)} %own_keys.2.kv_own, bf16[512,1152]{1,0:T(8,128)(2,1)S(1)} %bitcast.29, bf16[1152,3456]{1,0:T(8,128)(2,1)} %w_ref.3, ...), custom_call_target="tpu_custom_call" | custom-call | flops 16173236224 | bytes 16777216 | tf_op jit(solution)/shard_map/attention_backward/pallas_call | solution.py:307
  56.7 0.1 slice_dynamic-update-slice_fusion
  56.8 0.0 collective-permute-done.5
  56.8 0.0 collective-permute-done.4
  56.9 0.1 slice_dynamic-update-slice_fusion.2
  57.0 0.1 collective-permute-start.6
  57.1 0.5 collective-permute-start.7
  57.6 3.8 %own_gradient.1 = f32[512,1152]{1,0:T(8,128)S(1)} custom-call(bf16[2304,512]{1,0:T(8,128)(2,1)S(1)} %get-tuple-element.39.dkv, bf16[256,1152]{1,0:T(8,128)(2,1)S(1)} %get-tuple-element.40.dq, bf16[1152,3456]{1,0:T(8,128)(2,1)S(1)} %bitcast.22), custom_call_target="tpu_custom_call" | custom-call | flops 2717908992 | bytes 16777216 | tf_op jit(solution)/shard_map/own_gradient/pallas_call | solution.py:307
  61.4 3.3 %own_keys.3.kv_own = bf16[512,2304]{1,0:T(8,128)(2,1)S(1)} custom-call(bf16[112,1152]{1,0:T(8,128)(2,1)S(1)} %bitcast.34, bf16[256,1152]{1,0:T(8,128)(2,1)S(1)} %bitcast.27, bf16[112,1152]{1,0:T(8,128)(2,1)S(1)} %bitcast.33, bf16[1152,3456]{1,0:T(8,128)(2,1)S(1)} %bitcast.22), custom_call_target="tpu_custom_call" | custom-call | flops 2717908992 | bytes 16777216 | tf_op jit(solution)/shard_map/own_keys/pallas_call | solution.py:307
  64.7 5.6 %collective-permute-done.6 = bf16[64,8,1152]{2,1,0:T(8,128)(2,1)S(1)} collective-permute-done((bf16[64,8,1152]{2,1,0:T(8,128)(2,1)S(1)}, bf16[64,8,1152]{2,1,0:T(8,128)(2,1)S(1)}, u32[]{:S(2)}, u32[]{:S(2)}) %collective-permute-start.6) | collective-permute-done | bytes 1179680 | tf_op jit(solution)/shard_map/ppermute | solution.py:25
  70.3 4.9 %collective-permute-done.7 = bf16[64,8,1152]{2,1,0:T(8,128)(2,1)S(1)} collective-permute-done((bf16[64,8,1152]{2,1,0:T(8,128)(2,1)S(1)}, bf16[64,8,1152]{2,1,0:T(8,128)(2,1)S(1)}, u32[]{:S(2)}, u32[]{:S(2)}) %collective-permute-start.7) | collective-permute-done | bytes 1179680 | tf_op jit(solution)/shard_map/ppermute | solution.py:25
  75.2 0.1 fusion.21
  75.3 0.1 fusion.22
  75.4 0.3 fusion.19
  75.7 2.6 %collective-permute-start.8 = (bf16[7,16,1152]{2,1,0:T(8,128)(2,1)S(1)}, bf16[7,16,1152]{2,1,0:T(8,128)(2,1)S(1)}, u32[]{:S(2)}, u32[]{:S(2)}) collective-permute-start(bf16[7,16,1152]{2,1,0:T(8,128)(2,1)S(1)} %get-tuple-element.46), channel_id=1, source_target_pairs={{0,16},{16,32},{32,48},{48,64},{64,80},{80,96},{96,112},{112,0},{1... | collective-permute-start | bytes 774152 | tf_op jit(solution)/shard_map/ppermute | solution.py:25
  78.4 2.5 %collective-permute-start.9 = (bf16[7,16,1152]{2,1,0:T(8,128)(2,1)S(1)}, bf16[7,16,1152]{2,1,0:T(8,128)(2,1)S(1)}, u32[]{:S(2)}, u32[]{:S(2)}) collective-permute-start(bf16[7,16,1152]{2,1,0:T(8,128)(2,1)S(1)} %get-tuple-element.47), channel_id=1, source_target_pairs={{0,112},{16,0},{32,16},{48,32},{64,48},{80,64},{96,80},{112,96},{1... | collective-permute-start | bytes 774152 | tf_op jit(solution)/shard_map/ppermute | solution.py:25
  80.9 0.1 slice.112
  81.0 0.1 pad_maximum_fusion.1
  81.1 1.6 %copy-done.4 = bf16[1152,1152]{1,0:T(8,128)(2,1)S(1)} copy-done((bf16[1152,1152]{1,0:T(8,128)(2,1)S(1)}, bf16[1152,1152]{1,0:T(8,128)(2,1)}, u32[]{:S(2)}) %copy-start.4) | copy-done | bytes 2654232
  82.6 14.3 %attention_forward.1 = bf16[256,1152]{1,0:T(8,128)(2,1)} custom-call(bf16[512,2304]{1,0:T(8,128)(2,1)S(1)} %own_keys.3.kv_own, bf16[512,1152]{1,0:T(8,128)(2,1)S(1)} %bitcast.30, bf16[1152,3456]{1,0:T(8,128)(2,1)} %w_ref.3, bf16[1152,1152]{1,0:T(8,128)(2,1)S(1)} %copy-done.4, bf16[256,1152]{1,0:T(8,128)(2,1)S(1)} %convolution_convert_fusion.1.queries, ...), custom_call_target="tpu_custom_call" | custom-call | flops 7012876288 | bytes 16777216 | tf_op jit(solution)/shard_map/attention_forward/pallas_call | solution.py:307
  96.9 0.0 collective-permute-done.8
  97.0 0.0 collective-permute-done.9
  97.0 0.9 add_convert_fusion
  (30 shorter events, 0.3 us)
Async XLA Ops:
  0.6 14.5 %copy-start = (bf16[16,16,1152]{2,1,0:T(8,128)(2,1)S(1)}, bf16[16,16,1152]{2,1,0:T(8,128)(2,1)}, u32[]{:S(2)}) copy-start(bf16[16,16,1152]{2,1,0:T(8,128)(2,1)} %param.7) | copy-start | bytes 1769476
  0.6 7.8 %copy-start.1 = (bf16[16,16,1152]{2,1,0:T(8,128)(2,1)S(1)}, bf16[16,16,1152]{2,1,0:T(8,128)(2,1)}, u32[]{:S(2)}) copy-start(bf16[16,16,1152]{2,1,0:T(8,128)(2,1)} %param.6) | copy-start | bytes 1769476
  1.9 14.3 %collective-permute-start.1 = (bf16[7,16,1152]{2,1,0:T(8,128)(2,1)S(1)}, bf16[7,16,1152]{2,1,0:T(8,128)(2,1)S(1)}, u32[]{:S(2)}, u32[]{:S(2)}) collective-permute-start(bf16[7,16,1152]{2,1,0:T(8,128)(2,1)S(1)} %get-tuple-element.60), channel_id=1, source_target_pairs={{0,112},{16,0},{32,16},{48,32},{64,48},{80,64},{96,80},{112,96},{1... | collective-permute-start | bytes 774152 | tf_op jit(solution)/shard_map/ppermute | solution.py:25
  8.3 11.4 %collective-permute-start = (bf16[7,16,1152]{2,1,0:T(8,128)(2,1)S(1)}, bf16[7,16,1152]{2,1,0:T(8,128)(2,1)S(1)}, u32[]{:S(2)}, u32[]{:S(2)}) collective-permute-start(bf16[7,16,1152]{2,1,0:T(8,128)(2,1)S(1)} %get-tuple-element.61), channel_id=1, source_target_pairs={{0,16},{16,32},{32,48},{48,64},{64,80},{80,96},{96,112},{112,0},{1... | collective-permute-start | bytes 774152 | tf_op jit(solution)/shard_map/ppermute | solution.py:25
  8.5 2.9 %copy-start.2 = (bf16[16,16,1152]{2,1,0:T(8,128)(2,1)S(1)}, bf16[16,16,1152]{2,1,0:T(8,128)(2,1)}, u32[]{:S(2)}) copy-start(bf16[16,16,1152]{2,1,0:T(8,128)(2,1)} %param.5) | copy-start | bytes 1769476
  8.5 6.6 %copy-start.3 = (bf16[1152,1152]{1,0:T(8,128)(2,1)S(1)}, bf16[1152,1152]{1,0:T(8,128)(2,1)}, u32[]{:S(2)}) copy-start(bf16[1152,1152]{1,0:T(8,128)(2,1)} %wo_ref.1) | copy-start | bytes 7962628
  11.4 14.2 %slice-start = ((s8[7962624]{0:T(1024)(128)(4,1)}), s8[4194304]{0:T(1024)(128)(4,1)S(1)}, s32[]{:S(2)}) async-start(s8[7962624]{0:T(1024)(128)(4,1)} %bitcast.19), calls=%async_computation | async-start | bytes 8388608
  15.1 10.5 %slice-start.1 = ((s8[7962624]{0:T(1024)(128)(4,1)}), s8[3768320]{0:T(1024)(128)(4,1)S(1)}, s32[]{:S(2)}) async-start(s8[7962624]{0:T(1024)(128)(4,1)} %bitcast.19), calls=%async_computation.1 | async-start | bytes 7536640
  20.0 9.4 %collective-permute-start.2 = (bf16[32,8,1152]{2,1,0:T(8,128)(2,1)S(1)}, bf16[32,8,1152]{2,1,0:T(8,128)(2,1)S(1)}, u32[]{:S(2)}, u32[]{:S(2)}) collective-permute-start(bf16[32,8,1152]{2,1,0:T(8,128)(2,1)S(1)} %get-tuple-element.23), channel_id=1, source_target_pairs={{0,1},{1,2},{2,3},{3,4},{4,5},{5,6},{6,7},{7,8},{8,9},{9,10},{10,1... | collective-permute-start | bytes 1769480 | tf_op jit(solution)/shard_map/ppermute | solution.py:25
  22.5 11.8 %collective-permute-start.3 = (bf16[32,8,1152]{2,1,0:T(8,128)(2,1)S(1)}, bf16[32,8,1152]{2,1,0:T(8,128)(2,1)S(1)}, u32[]{:S(2)}, u32[]{:S(2)}) collective-permute-start(bf16[32,8,1152]{2,1,0:T(8,128)(2,1)S(1)} %get-tuple-element.24), channel_id=1, source_target_pairs={{0,15},{1,0},{2,1},{3,2},{4,3},{5,4},{6,5},{7,6},{8,7},{9,8},{10,9... | collective-permute-start | bytes 1769480 | tf_op jit(solution)/shard_map/ppermute | solution.py:25
  22.5 34.3 %collective-permute-start.5 = (bf16[7,16,1152]{2,1,0:T(8,128)(2,1)S(1)}, bf16[7,16,1152]{2,1,0:T(8,128)(2,1)S(1)}, u32[]{:S(2)}, u32[]{:S(2)}) collective-permute-start(bf16[7,16,1152]{2,1,0:T(8,128)(2,1)S(1)} %get-tuple-element.56), channel_id=1, source_target_pairs={{0,112},{16,0},{32,16},{48,32},{64,48},{80,64},{96,80},{112,96},{1... | collective-permute-start | bytes 774152 | tf_op jit(solution)/shard_map/ppermute | solution.py:25
  25.1 31.8 %collective-permute-start.4 = (bf16[7,16,1152]{2,1,0:T(8,128)(2,1)S(1)}, bf16[7,16,1152]{2,1,0:T(8,128)(2,1)S(1)}, u32[]{:S(2)}, u32[]{:S(2)}) collective-permute-start(bf16[7,16,1152]{2,1,0:T(8,128)(2,1)S(1)} %get-tuple-element.57), channel_id=1, source_target_pairs={{0,16},{16,32},{32,48},{48,64},{64,80},{80,96},{96,112},{112,0},{1... | collective-permute-start | bytes 774152 | tf_op jit(solution)/shard_map/ppermute | solution.py:25
  34.3 23.3 %slice-start.2 = ((s8[7962624]{0:T(1024)(128)(4,1)}), s8[4194304]{0:T(1024)(128)(4,1)S(1)}, s32[]{:S(2)}) async-start(s8[7962624]{0:T(1024)(128)(4,1)} %bitcast.21), calls=%async_computation.2 | async-start | bytes 8388608
  34.4 23.3 %slice-start.3 = ((s8[7962624]{0:T(1024)(128)(4,1)}), s8[3768320]{0:T(1024)(128)(4,1)S(1)}, s32[]{:S(2)}) async-start(s8[7962624]{0:T(1024)(128)(4,1)} %bitcast.21), calls=%async_computation.3 | async-start | bytes 7536640
  57.0 13.2 %collective-permute-start.6 = (bf16[64,8,1152]{2,1,0:T(8,128)(2,1)S(1)}, bf16[64,8,1152]{2,1,0:T(8,128)(2,1)S(1)}, u32[]{:S(2)}, u32[]{:S(2)}) collective-permute-start(bf16[64,8,1152]{2,1,0:T(8,128)(2,1)S(1)} %constant_dynamic-update-slice_fusion), channel_id=1, source_target_pairs={{0,1},{1,2},{2,3},{3,4},{4,5},{5,6},{6,7},{7,8},{8,9},{9,10},{10,1... | collective-permute-start | bytes 3538952 | tf_op jit(solution)/shard_map/ppermute | solution.py:25
  57.1 18.1 %collective-permute-start.7 = (bf16[64,8,1152]{2,1,0:T(8,128)(2,1)S(1)}, bf16[64,8,1152]{2,1,0:T(8,128)(2,1)S(1)}, u32[]{:S(2)}, u32[]{:S(2)}) collective-permute-start(bf16[64,8,1152]{2,1,0:T(8,128)(2,1)S(1)} %constant_dynamic-update-slice_fusion.1), channel_id=1, source_target_pairs={{0,15},{1,0},{2,1},{3,2},{4,3},{5,4},{6,5},{7,6},{8,7},{9,8},{10,9... | collective-permute-start | bytes 3538952 | tf_op jit(solution)/shard_map/ppermute | solution.py:25
  75.7 21.2 %collective-permute-start.8 = (bf16[7,16,1152]{2,1,0:T(8,128)(2,1)S(1)}, bf16[7,16,1152]{2,1,0:T(8,128)(2,1)S(1)}, u32[]{:S(2)}, u32[]{:S(2)}) collective-permute-start(bf16[7,16,1152]{2,1,0:T(8,128)(2,1)S(1)} %get-tuple-element.46), channel_id=1, source_target_pairs={{0,16},{16,32},{32,48},{48,64},{64,80},{80,96},{96,112},{112,0},{1... | collective-permute-start | bytes 774152 | tf_op jit(solution)/shard_map/ppermute | solution.py:25
  78.4 18.6 %collective-permute-start.9 = (bf16[7,16,1152]{2,1,0:T(8,128)(2,1)S(1)}, bf16[7,16,1152]{2,1,0:T(8,128)(2,1)S(1)}, u32[]{:S(2)}, u32[]{:S(2)}) collective-permute-start(bf16[7,16,1152]{2,1,0:T(8,128)(2,1)S(1)} %get-tuple-element.47), channel_id=1, source_target_pairs={{0,112},{16,0},{32,16},{48,32},{64,48},{80,64},{96,80},{112,96},{1... | collective-permute-start | bytes 774152 | tf_op jit(solution)/shard_map/ppermute | solution.py:25
  80.9 1.7 %copy-start.4 = (bf16[1152,1152]{1,0:T(8,128)(2,1)S(1)}, bf16[1152,1152]{1,0:T(8,128)(2,1)}, u32[]{:S(2)}) copy-start(bf16[1152,1152]{1,0:T(8,128)(2,1)} %wo_ref.1) | copy-start | bytes 7962628

commit v4 on v2

--- a/solution.py
+++ b/solution.py
@@ -402,10 +402,10 @@
         (column_sends(parts_backward), q_backward, q_forward, grad_heads, bias)
     )
     side_backward = flat(side_columns(sends_backward))
-    x_forward, _ = lax.optimization_barrier((x_forward, sends_backward))
-    parts_forward = row_halos(x_forward)
     parts_backward, _ = lax.optimization_barrier((parts_backward, sends_backward))
     own_backward = own_keys([flat(part) for part in parts_backward], w_qkv)
+    x_forward, _ = lax.optimization_barrier((x_forward, own_backward))
+    parts_forward = row_halos(x_forward)
 
     dkv_own, dq, dx_side = attention_backward(
         own_backward, side_backward, w_qkv, q_backward, grad_heads, bias, heads

time: 95.6 us -> 95.1 us (level)
  no operation moved by 1% of the time
where the time goes in v4:
time: 95.1 us; the launch traced here: 95 us
  Pallas kernels  47.5 us (50%)
  starting transfers between devices  25 us (26%)
  waiting for transfers between devices  7.36 us (8%)
  matrix products  7.04 us (7%)
  local copies, waits for them, and re-layouts  4.34 us (5%)
  other arithmetic  2.64 us (3%)
  between operations  1.05 us (1%)
    pallas_call x5, Pallas kernels, call_kernel(): pl.pallas_call(kernel, in_specs=[pl.BlockSpec(memory_space=space) for spa...  47.5 us
    ppermute x12, starting transfers between devices, shifted(): lax.ppermute(value, axis, [(i, (i + step) % count) for i in range(count)])  25 us
    ppermute x12, waiting for transfers between devices, shifted(): lax.ppermute(value, axis, [(i, (i + step) % count) for i in range(count)])  7.36 us
    dot_general x2, matrix products, project(): jnp.dot(x, w, preferred_element_type=jnp.float32).astype(jnp.bfloat16)  5.99 us
  transfers between devices with their start and end apart: 12, of which 3 were waited for; matrix products, arithmetic and copies ran while one was open for 11% of the time, Pallas kernels for 50%

profile of v4, /device:TPU:7, one launch (start us, length us, event | category | flops | bytes accessed | tf_op | source)
XLA Modules:
  0.0 95.0 jit_solution(4801589262962707171)
XLA Ops:
  0.6 0.0 copy-start
  0.6 1.2 %fusion.25 = (bf16[7,16,1152]{2,1,0:T(8,128)(2,1)S(1)}, bf16[7,16,1152]{2,1,0:T(8,128)(2,1)S(1)}) fusion(bf16[16,16,1152]{2,1,0:T(8,128)(2,1)} %param.6), kind=kLoop, calls=%fused_computation.68 | loop fusion | bytes 1032192 | tf_op jit(solution)/shard_map/slice | solution.py:29
  1.8 6.5 %collective-permute-start.1 = (bf16[7,16,1152]{2,1,0:T(8,128)(2,1)S(1)}, bf16[7,16,1152]{2,1,0:T(8,128)(2,1)S(1)}, u32[]{:S(2)}, u32[]{:S(2)}) collective-permute-start(bf16[7,16,1152]{2,1,0:T(8,128)(2,1)S(1)} %get-tuple-element.62), channel_id=1, source_target_pairs={{0,112},{16,0},{32,16},{48,32},{64,48},{80,64},{96,80},{112,96},{1... | collective-permute-start | bytes 774152 | tf_op jit(solution)/shard_map/ppermute | solution.py:25
  8.3 0.0 collective-permute-start
  8.4 1.1 %fusion.24 = (bf16[16,8,1152]{2,1,0:T(8,128)(2,1)S(1)}, bf16[16,8,1152]{2,1,0:T(8,128)(2,1)S(1)}) fusion(bf16[16,16,1152]{2,1,0:T(8,128)(2,1)} %param.6), kind=kLoop, calls=%fused_computation.67 | loop fusion | bytes 1179648 | tf_op jit(solution)/shard_map/slice | solution.py:34
  9.5 0.0 copy-start.2
  9.5 0.0 copy-start.3
  9.5 0.0 slice-start
  9.5 3.1 %convolution_convert_fusion.2.queries = bf16[256,1152]{1,0:T(8,128)(2,1)S(1)} fusion(bf16[256,1152]{1,0:T(8,128)(2,1)} %bitcast.24, bf16[1152,3456]{1,0:T(8,128)(2,1)} %w_ref.3), kind=kOutput, calls=%fused_computation.2 | convolution fusion | flops 679772160 | bytes 3833856 | tf_op jit(solution)/shard_map/dot_general | solution.py:385
  12.6 0.0 slice-start.1
  12.6 2.9 %convolution_convert_fusion.1.queries = bf16[256,1152]{1,0:T(8,128)(2,1)S(1)} fusion(bf16[256,1152]{1,0:T(8,128)(2,1)S(1)} %bitcast.26, bf16[1152,3456]{1,0:T(8,128)(2,1)} %w_ref.3), kind=kOutput, calls=%fused_computation.1 | convolution fusion | flops 679772160 | bytes 3833856 | tf_op jit(solution)/shard_map/dot_general | solution.py:385
  15.6 0.1 pad.25.clone
  15.6 0.7 and_select_fusion.bias
  16.4 1.1 %convolution_convert_fusion.cotangents = bf16[256,1152]{1,0:T(8,128)(2,1)S(1)} fusion(bf16[256,1152]{1,0:T(8,128)(2,1)S(1)} %bitcast.18, bf16[1152,1152]{1,0:T(8,128)(2,1)S(1)} %copy-done.3), kind=kOutput, calls=%fused_computation | convolution fusion | flops 679772160 | bytes 3833856 | tf_op jit(solution)/shard_map/dot_general | solution.py:398
  17.5 0.0 copy-start.1
  17.5 0.0 collective-permute-done.1
  17.5 2.2 %collective-permute-done = bf16[7,16,1152]{2,1,0:T(8,128)(2,1)S(1)} collective-permute-done((bf16[7,16,1152]{2,1,0:T(8,128)(2,1)S(1)}, bf16[7,16,1152]{2,1,0:T(8,128)(2,1)S(1)}, u32[]{:S(2)}, u32[]{:S(2)}) %collective-permute-start) | collective-permute-done | bytes 258080 | tf_op jit(solution)/shard_map/ppermute | solution.py:25
  19.7 0.2 maximum_maximum_fusion.1
  19.9 2.5 %collective-permute-start.2 = (bf16[32,8,1152]{2,1,0:T(8,128)(2,1)S(1)}, bf16[32,8,1152]{2,1,0:T(8,128)(2,1)S(1)}, u32[]{:S(2)}, u32[]{:S(2)}) collective-permute-start(bf16[32,8,1152]{2,1,0:T(8,128)(2,1)S(1)} %get-tuple-element.26), channel_id=1, source_target_pairs={{0,1},{1,2},{2,3},{3,4},{4,5},{5,6},{6,7},{7,8},{8,9},{9,10},{10,1... | collective-permute-start | bytes 1769480 | tf_op jit(solution)/shard_map/ppermute | solution.py:25
  22.5 0.0 collective-permute-start.3
  22.5 3.2 %own_keys.2.kv_own = bf16[512,2304]{1,0:T(8,128)(2,1)S(1)} custom-call(bf16[112,1152]{1,0:T(8,128)(2,1)S(1)} %bitcast.32, bf16[256,1152]{1,0:T(8,128)(2,1)S(1)} %bitcast.25, bf16[112,1152]{1,0:T(8,128)(2,1)S(1)} %bitcast.31, bf16[1152,3456]{1,0:T(8,128)(2,1)S(1)} %bitcast.20), custom_call_target="tpu_custom_call" | custom-call | flops 2717908992 | bytes 16777216 | tf_op jit(solution)/shard_map/own_keys/pallas_call | solution.py:307
  25.8 2.6 %collective-permute-start.7 = (bf16[7,16,1152]{2,1,0:T(8,128)(2,1)S(1)}, bf16[7,16,1152]{2,1,0:T(8,128)(2,1)S(1)}, u32[]{:S(2)}, u32[]{:S(2)}) collective-permute-start(bf16[7,16,1152]{2,1,0:T(8,128)(2,1)S(1)} %get-tuple-element.58), channel_id=1, source_target_pairs={{0,112},{16,0},{32,16},{48,32},{64,48},{80,64},{96,80},{112,96},{1... | collective-permute-start | bytes 774152 | tf_op jit(solution)/shard_map/ppermute | solution.py:25
  28.3 0.5 collective-permute-start.6
  28.8 0.5 collective-permute-done.2
  29.3 4.7 %collective-permute-done.3 = bf16[32,8,1152]{2,1,0:T(8,128)(2,1)S(1)} collective-permute-done((bf16[32,8,1152]{2,1,0:T(8,128)(2,1)S(1)}, bf16[32,8,1152]{2,1,0:T(8,128)(2,1)S(1)}, u32[]{:S(2)}, u32[]{:S(2)}) %collective-permute-start.3) | collective-permute-done | bytes 589856 | tf_op jit(solution)/shard_map/ppermute | solution.py:25
  34.0 0.1 pad_maximum_fusion
  34.1 0.0 slice-start.2
  34.1 0.0 slice-start.3
  34.1 22.6 %attention_backward.1 = (bf16[2304,512]{1,0:T(8,128)(2,1)S(1)}, bf16[256,1152]{1,0:T(8,128)(2,1)S(1)}, bf16[512,1152]{1,0:T(8,128)(2,1)S(1)}) custom-call(bf16[512,2304]{1,0:T(8,128)(2,1)S(1)} %own_keys.2.kv_own, bf16[512,1152]{1,0:T(8,128)(2,1)S(1)} %bitcast.29, bf16[1152,3456]{1,0:T(8,128)(2,1)} %w_ref.3, ...), custom_call_target="tpu_custom_call" | custom-call | flops 16173236224 | bytes 16777216 | tf_op jit(solution)/shard_map/attention_backward/pallas_call | solution.py:307
  56.7 0.1 fusion.21
  56.8 0.1 collective-permute-start.5
  56.9 3.8 %collective-permute-start.4 = (bf16[32,8,1152]{2,1,0:T(8,128)(2,1)S(1)}, bf16[32,8,1152]{2,1,0:T(8,128)(2,1)S(1)}, u32[]{:S(2)}, u32[]{:S(2)}) collective-permute-start(bf16[32,8,1152]{2,1,0:T(8,128)(2,1)S(1)} %get-tuple-element.55), channel_id=1, source_target_pairs={{0,1},{1,2},{2,3},{3,4},{4,5},{5,6},{6,7},{7,8},{8,9},{9,10},{10,1... | collective-permute-start | bytes 1769480 | tf_op jit(solution)/shard_map/ppermute | solution.py:25
  60.7 3.8 %own_gradient.1 = f32[512,1152]{1,0:T(8,128)S(1)} custom-call(bf16[2304,512]{1,0:T(8,128)(2,1)S(1)} %get-tuple-element.36.dkv, bf16[256,1152]{1,0:T(8,128)(2,1)S(1)} %get-tuple-element.37.dq, bf16[1152,3456]{1,0:T(8,128)(2,1)S(1)} %bitcast.22), custom_call_target="tpu_custom_call" | custom-call | flops 2717908992 | bytes 16777216 | tf_op jit(solution)/shard_map/own_gradient/pallas_call | solution.py:307
  64.5 0.0 collective-permute-done.7
  64.6 0.2 maximum_maximum_fusion.3
  64.8 0.1 collective-permute-start.9
  64.9 3.8 %collective-permute-start.8 = (bf16[32,8,1152]{2,1,0:T(8,128)(2,1)S(1)}, bf16[32,8,1152]{2,1,0:T(8,128)(2,1)S(1)}, u32[]{:S(2)}, u32[]{:S(2)}) collective-permute-start(bf16[32,8,1152]{2,1,0:T(8,128)(2,1)S(1)} %get-tuple-element.73), channel_id=1, source_target_pairs={{0,1},{1,2},{2,3},{3,4},{4,5},{5,6},{6,7},{7,8},{8,9},{9,10},{10,1... | collective-permute-start | bytes 1769480 | tf_op jit(solution)/shard_map/ppermute | solution.py:25
  68.8 3.3 %own_keys.3.kv_own = bf16[512,2304]{1,0:T(8,128)(2,1)S(1)} custom-call(bf16[112,1152]{1,0:T(8,128)(2,1)S(1)} %bitcast.34, bf16[256,1152]{1,0:T(8,128)(2,1)S(1)} %bitcast.27, bf16[112,1152]{1,0:T(8,128)(2,1)S(1)} %bitcast.33, bf16[1152,3456]{1,0:T(8,128)(2,1)S(1)} %bitcast.22), custom_call_target="tpu_custom_call" | custom-call | flops 2717908992 | bytes 16777216 | tf_op jit(solution)/shard_map/own_keys/pallas_call | solution.py:307
  72.1 0.0 collective-permute-done.4
  72.1 0.3 fusion.19
  72.4 2.8 %collective-permute-start.10 = (bf16[7,16,1152]{2,1,0:T(8,128)(2,1)S(1)}, bf16[7,16,1152]{2,1,0:T(8,128)(2,1)S(1)}, u32[]{:S(2)}, u32[]{:S(2)}) collective-permute-start(bf16[7,16,1152]{2,1,0:T(8,128)(2,1)S(1)} %get-tuple-element.52), channel_id=1, source_target_pairs={{0,16},{16,32},{32,48},{48,64},{64,80},{80,96},{96,112},{112,0},{1... | collective-permute-start | bytes 774152 | tf_op jit(solution)/shard_map/ppermute | solution.py:25
  75.2 2.4 %collective-permute-start.11 = (bf16[7,16,1152]{2,1,0:T(8,128)(2,1)S(1)}, bf16[7,16,1152]{2,1,0:T(8,128)(2,1)S(1)}, u32[]{:S(2)}, u32[]{:S(2)}) collective-permute-start(bf16[7,16,1152]{2,1,0:T(8,128)(2,1)S(1)} %get-tuple-element.53), channel_id=1, source_target_pairs={{0,112},{16,0},{32,16},{48,32},{64,48},{80,64},{96,80},{112,96},{1... | collective-permute-start | bytes 774152 | tf_op jit(solution)/shard_map/ppermute | solution.py:25
  77.6 0.1 slice.96
  77.7 0.1 pad_maximum_fusion.1
  77.8 1.5 %copy-done.4 = bf16[1152,1152]{1,0:T(8,128)(2,1)S(1)} copy-done((bf16[1152,1152]{1,0:T(8,128)(2,1)S(1)}, bf16[1152,1152]{1,0:T(8,128)(2,1)}, u32[]{:S(2)}) %copy-start.4) | copy-done | bytes 2654232
  79.3 14.7 %attention_forward.1 = bf16[256,1152]{1,0:T(8,128)(2,1)} custom-call(bf16[512,2304]{1,0:T(8,128)(2,1)S(1)} %own_keys.3.kv_own, bf16[512,1152]{1,0:T(8,128)(2,1)S(1)} %bitcast.30, bf16[1152,3456]{1,0:T(8,128)(2,1)} %w_ref.3, bf16[1152,1152]{1,0:T(8,128)(2,1)S(1)} %copy-done.4, bf16[256,1152]{1,0:T(8,128)(2,1)S(1)} %convolution_convert_fusion.1.queries, ...), custom_call_target="tpu_custom_call" | custom-call | flops 7012876288 | bytes 16777216 | tf_op jit(solution)/shard_map/attention_forward/pallas_call | solution.py:307
  94.0 0.0 collective-permute-done.10
  94.0 0.9 add_convert_fusion
  (32 shorter events, 0.3 us)
Async XLA Ops:
  0.6 15.7 %copy-start = (bf16[16,16,1152]{2,1,0:T(8,128)(2,1)S(1)}, bf16[16,16,1152]{2,1,0:T(8,128)(2,1)}, u32[]{:S(2)}) copy-start(bf16[16,16,1152]{2,1,0:T(8,128)(2,1)} %param.7) | copy-start | bytes 1769476
  1.8 15.6 %collective-permute-start.1 = (bf16[7,16,1152]{2,1,0:T(8,128)(2,1)S(1)}, bf16[7,16,1152]{2,1,0:T(8,128)(2,1)S(1)}, u32[]{:S(2)}, u32[]{:S(2)}) collective-permute-start(bf16[7,16,1152]{2,1,0:T(8,128)(2,1)S(1)} %get-tuple-element.62), channel_id=1, source_target_pairs={{0,112},{16,0},{32,16},{48,32},{64,48},{80,64},{96,80},{112,96},{1... | collective-permute-start | bytes 774152 | tf_op jit(solution)/shard_map/ppermute | solution.py:25
  8.3 11.4 %collective-permute-start = (bf16[7,16,1152]{2,1,0:T(8,128)(2,1)S(1)}, bf16[7,16,1152]{2,1,0:T(8,128)(2,1)S(1)}, u32[]{:S(2)}, u32[]{:S(2)}) collective-permute-start(bf16[7,16,1152]{2,1,0:T(8,128)(2,1)S(1)} %get-tuple-element.63), channel_id=1, source_target_pairs={{0,16},{16,32},{32,48},{48,64},{64,80},{80,96},{96,112},{112,0},{1... | collective-permute-start | bytes 774152 | tf_op jit(solution)/shard_map/ppermute | solution.py:25
  9.5 3.1 %copy-start.2 = (bf16[16,16,1152]{2,1,0:T(8,128)(2,1)S(1)}, bf16[16,16,1152]{2,1,0:T(8,128)(2,1)}, u32[]{:S(2)}) copy-start(bf16[16,16,1152]{2,1,0:T(8,128)(2,1)} %param.5) | copy-start | bytes 1769476
  9.5 6.9 %copy-start.3 = (bf16[1152,1152]{1,0:T(8,128)(2,1)S(1)}, bf16[1152,1152]{1,0:T(8,128)(2,1)}, u32[]{:S(2)}) copy-start(bf16[1152,1152]{1,0:T(8,128)(2,1)} %wo_ref.1) | copy-start | bytes 7962628
  9.5 13.0 %slice-start = ((s8[7962624]{0:T(1024)(128)(4,1)}), s8[4194304]{0:T(1024)(128)(4,1)S(1)}, s32[]{:S(2)}) async-start(s8[7962624]{0:T(1024)(128)(4,1)} %bitcast.19), calls=%async_computation | async-start | bytes 8388608
  12.6 9.9 %slice-start.1 = ((s8[7962624]{0:T(1024)(128)(4,1)}), s8[3768320]{0:T(1024)(128)(4,1)S(1)}, s32[]{:S(2)}) async-start(s8[7962624]{0:T(1024)(128)(4,1)} %bitcast.19), calls=%async_computation.1 | async-start | bytes 7536640
  17.5 5.0 %copy-start.1 = (bf16[16,16,1152]{2,1,0:T(8,128)(2,1)S(1)}, bf16[16,16,1152]{2,1,0:T(8,128)(2,1)}, u32[]{:S(2)}) copy-start(bf16[16,16,1152]{2,1,0:T(8,128)(2,1)} %param.6) | copy-start | bytes 1769476
  19.9 9.4 %collective-permute-start.2 = (bf16[32,8,1152]{2,1,0:T(8,128)(2,1)S(1)}, bf16[32,8,1152]{2,1,0:T(8,128)(2,1)S(1)}, u32[]{:S(2)}, u32[]{:S(2)}) collective-permute-start(bf16[32,8,1152]{2,1,0:T(8,128)(2,1)S(1)} %get-tuple-element.26), channel_id=1, source_target_pairs={{0,1},{1,2},{2,3},{3,4},{4,5},{5,6},{6,7},{7,8},{8,9},{9,10},{10,1... | collective-permute-start | bytes 1769480 | tf_op jit(solution)/shard_map/ppermute | solution.py:25
  22.5 11.5 %collective-permute-start.3 = (bf16[32,8,1152]{2,1,0:T(8,128)(2,1)S(1)}, bf16[32,8,1152]{2,1,0:T(8,128)(2,1)S(1)}, u32[]{:S(2)}, u32[]{:S(2)}) collective-permute-start(bf16[32,8,1152]{2,1,0:T(8,128)(2,1)S(1)} %get-tuple-element.27), channel_id=1, source_target_pairs={{0,15},{1,0},{2,1},{3,2},{4,3},{5,4},{6,5},{7,6},{8,7},{9,8},{10,9... | collective-permute-start | bytes 1769480 | tf_op jit(solution)/shard_map/ppermute | solution.py:25
  25.8 38.7 %collective-permute-start.7 = (bf16[7,16,1152]{2,1,0:T(8,128)(2,1)S(1)}, bf16[7,16,1152]{2,1,0:T(8,128)(2,1)S(1)}, u32[]{:S(2)}, u32[]{:S(2)}) collective-permute-start(bf16[7,16,1152]{2,1,0:T(8,128)(2,1)S(1)} %get-tuple-element.58), channel_id=1, source_target_pairs={{0,112},{16,0},{32,16},{48,32},{64,48},{80,64},{96,80},{112,96},{1... | collective-permute-start | bytes 774152 | tf_op jit(solution)/shard_map/ppermute | solution.py:25
  28.3 36.1 %collective-permute-start.6 = (bf16[7,16,1152]{2,1,0:T(8,128)(2,1)S(1)}, bf16[7,16,1152]{2,1,0:T(8,128)(2,1)S(1)}, u32[]{:S(2)}, u32[]{:S(2)}) collective-permute-start(bf16[7,16,1152]{2,1,0:T(8,128)(2,1)S(1)} %get-tuple-element.59), channel_id=1, source_target_pairs={{0,16},{16,32},{32,48},{48,64},{64,80},{80,96},{96,112},{112,0},{1... | collective-permute-start | bytes 774152 | tf_op jit(solution)/shard_map/ppermute | solution.py:25
  34.1 26.6 %slice-start.2 = ((s8[7962624]{0:T(1024)(128)(4,1)}), s8[4194304]{0:T(1024)(128)(4,1)S(1)}, s32[]{:S(2)}) async-start(s8[7962624]{0:T(1024)(128)(4,1)} %bitcast.21), calls=%async_computation.2 | async-start | bytes 8388608
  34.1 26.6 %slice-start.3 = ((s8[7962624]{0:T(1024)(128)(4,1)}), s8[3768320]{0:T(1024)(128)(4,1)S(1)}, s32[]{:S(2)}) async-start(s8[7962624]{0:T(1024)(128)(4,1)} %bitcast.21), calls=%async_computation.3 | async-start | bytes 7536640
  56.8 15.3 %collective-permute-start.5 = (bf16[32,8,1152]{2,1,0:T(8,128)(2,1)S(1)}, bf16[32,8,1152]{2,1,0:T(8,128)(2,1)S(1)}, u32[]{:S(2)}, u32[]{:S(2)}) collective-permute-start(bf16[32,8,1152]{2,1,0:T(8,128)(2,1)S(1)} %get-tuple-element.54), channel_id=1, source_target_pairs={{0,15},{1,0},{2,1},{3,2},{4,3},{5,4},{6,5},{7,6},{8,7},{9,8},{10,9... | collective-permute-start | bytes 1769480 | tf_op jit(solution)/shard_map/ppermute | solution.py:25
  56.9 15.2 %collective-permute-start.4 = (bf16[32,8,1152]{2,1,0:T(8,128)(2,1)S(1)}, bf16[32,8,1152]{2,1,0:T(8,128)(2,1)S(1)}, u32[]{:S(2)}, u32[]{:S(2)}) collective-permute-start(bf16[32,8,1152]{2,1,0:T(8,128)(2,1)S(1)} %get-tuple-element.55), channel_id=1, source_target_pairs={{0,1},{1,2},{2,3},{3,4},{4,5},{5,6},{6,7},{7,8},{8,9},{9,10},{10,1... | collective-permute-start | bytes 1769480 | tf_op jit(solution)/shard_map/ppermute | solution.py:25
  64.8 12.8 %collective-permute-start.9 = (bf16[32,8,1152]{2,1,0:T(8,128)(2,1)S(1)}, bf16[32,8,1152]{2,1,0:T(8,128)(2,1)S(1)}, u32[]{:S(2)}, u32[]{:S(2)}) collective-permute-start(bf16[32,8,1152]{2,1,0:T(8,128)(2,1)S(1)} %get-tuple-element.72), channel_id=1, source_target_pairs={{0,15},{1,0},{2,1},{3,2},{4,3},{5,4},{6,5},{7,6},{8,7},{9,8},{10,9... | collective-permute-start | bytes 1769480 | tf_op jit(solution)/shard_map/ppermute | solution.py:25
  64.9 12.8 %collective-permute-start.8 = (bf16[32,8,1152]{2,1,0:T(8,128)(2,1)S(1)}, bf16[32,8,1152]{2,1,0:T(8,128)(2,1)S(1)}, u32[]{:S(2)}, u32[]{:S(2)}) collective-permute-start(bf16[32,8,1152]{2,1,0:T(8,128)(2,1)S(1)} %get-tuple-element.73), channel_id=1, source_target_pairs={{0,1},{1,2},{2,3},{3,4},{4,5},{5,6},{6,7},{7,8},{8,9},{9,10},{10,1... | collective-permute-start | bytes 1769480 | tf_op jit(solution)/shard_map/ppermute | solution.py:25
  72.4 21.6 %collective-permute-start.10 = (bf16[7,16,1152]{2,1,0:T(8,128)(2,1)S(1)}, bf16[7,16,1152]{2,1,0:T(8,128)(2,1)S(1)}, u32[]{:S(2)}, u32[]{:S(2)}) collective-permute-start(bf16[7,16,1152]{2,1,0:T(8,128)(2,1)S(1)} %get-tuple-element.52), channel_id=1, source_target_pairs={{0,16},{16,32},{32,48},{48,64},{64,80},{80,96},{96,112},{112,0},{1... | collective-permute-start | bytes 774152 | tf_op jit(solution)/shard_map/ppermute | solution.py:25
  75.2 18.8 %collective-permute-start.11 = (bf16[7,16,1152]{2,1,0:T(8,128)(2,1)S(1)}, bf16[7,16,1152]{2,1,0:T(8,128)(2,1)S(1)}, u32[]{:S(2)}, u32[]{:S(2)}) collective-permute-start(bf16[7,16,1152]{2,1,0:T(8,128)(2,1)S(1)} %get-tuple-element.53), channel_id=1, source_target_pairs={{0,112},{16,0},{32,16},{48,32},{64,48},{80,64},{96,80},{112,96},{1... | collective-permute-start | bytes 774152 | tf_op jit(solution)/shard_map/ppermute | solution.py:25
  77.6 1.7 %copy-start.4 = (bf16[1152,1152]{1,0:T(8,128)(2,1)S(1)}, bf16[1152,1152]{1,0:T(8,128)(2,1)}, u32[]{:S(2)}) copy-start(bf16[1152,1152]{1,0:T(8,128)(2,1)} %wo_ref.1) | copy-start | bytes 7962628

commit v5 on v4

--- a/solution.py
+++ b/solution.py
@@ -230,8 +230,8 @@
 
 
 def backward_kernel(
-    head_dim, kv_own, x_side, w_ref, queries, cotangents, bias, down_ref, dq_ref, dside_ref,
-    w_kv, queries_t, cotangents_t, kv, dkv, acc,
+    head_dim, kv_own, x_side, w_ref, queries, cotangents, queries_t, cotangents_t, bias,
+    down_ref, dq_ref, dside_ref, w_kv, kv, dkv, acc,
     scores0, scores1, grads0, grads1, probs0, probs1, dscores0, dscores1, sems
 ):
     width = queries.shape[1]
@@ -241,8 +241,6 @@
     probs, dscores = (probs0, probs1), (dscores0, dscores1)
     copies = fetch(key_weights(w_ref, w_kv), sems)
     acc[...] = jnp.zeros_like(acc)
-    turned(queries, queries_t)
-    turned(cotangents, cotangents_t)
     fill_keys(kv_own, x_side, w_kv, copies, kv)
 
     def scored(pair, u):
@@ -313,6 +311,17 @@
         cost_estimate=pl.CostEstimate(flops=flops, bytes_accessed=16 * 2**20, transcendentals=2**22),
         name=name,
     )(*args)
+
+
+def both_turned_kernel(queries, cotangents, queries_t, cotangents_t):
+    turned(queries, queries_t)
+    turned(cotangents, cotangents_t)
+
+
+def both_turned(queries, cotangents, heads):
+    tokens, width = queries.shape
+    out_shape = [jax.ShapeDtypeStruct((heads, width // heads, tokens), jnp.bfloat16)] * 2
+    return call_kernel(both_turned_kernel, [queries, cotangents], out_shape, [], 0, "both_turned")
 
 
 def own_keys(x_parts, w_qkv):
@@ -350,16 +359,13 @@
     )
 
 
-def attention_backward(kv_own, x_side, w_qkv, queries, cotangents, bias, heads):
+def attention_backward(kv_own, x_side, w_qkv, queries, cotangents, flipped, bias, heads):
     tokens, width = queries.shape
     head_dim = width // heads
     square = (2 * tokens, SPAN)
     half, full = jnp.bfloat16, jnp.float32
-    by_head = (heads, head_dim, tokens)
     scratch = [
         pltpu.VMEM((width, 2 * width), half),
-        pltpu.VMEM(by_head, half),
-        pltpu.VMEM(by_head, half),
         pltpu.VMEM((KEYS, 2 * width), half),
         pltpu.VMEM((2 * width, KEYS // 2), half),
         pltpu.VMEM((tokens, width), full),
@@ -368,7 +374,7 @@
     scratch += [pltpu.SemaphoreType.DMA((2 * width // SPAN,))]
     return call_kernel(
         functools.partial(backward_kernel, head_dim),
-        [kv_own, x_side, w_qkv, queries, cotangents, bias],
+        [kv_own, x_side, w_qkv, queries, cotangents, *flipped, bias],
         [
             jax.ShapeDtypeStruct((2 * width, KEYS // 2), half),
             jax.ShapeDtypeStruct(queries.shape, half),
@@ -398,8 +404,9 @@
     grad_heads = lax.dot_general(
         flat(grad_out), w_out, (((1,), (1,)), ((), ())), preferred_element_type=jnp.float32
     ).astype(jnp.bfloat16)
-    sends_backward, q_backward, q_forward, grad_heads, bias = lax.optimization_barrier(
-        (column_sends(parts_backward), q_backward, q_forward, grad_heads, bias)
+    flipped = both_turned(q_backward, grad_heads, heads)
+    sends_backward, q_backward, q_forward, grad_heads, flipped, bias = lax.optimization_barrier(
+        (column_sends(parts_backward), q_backward, q_forward, grad_heads, flipped, bias)
     )
     side_backward = flat(side_columns(sends_backward))
     parts_backward, _ = lax.optimization_barrier((parts_backward, sends_backward))
@@ -408,7 +415,7 @@
     parts_forward = row_halos(x_forward)
 
     dkv_own, dq, dx_side = attention_backward(
-        own_backward, side_backward, w_qkv, q_backward, grad_heads, bias, heads
+        own_backward, side_backward, w_qkv, q_backward, grad_heads, flipped, bias, heads
     )
     dx_side = dx_side.reshape(2 * SIDE, SIDE, width)
     from_right = shifted(dx_side[:, :8], "heads", -1)

time: 95.1 us -> 94.4 us (level)
    dot_general x2, matrix products: 5.99 us -> 3.91 us  [project(): jnp.dot(x, w, preferred_element_type=jnp.float32).astype(jnp.bfloat16)]
    dot_general x1, matrix products: 1.05 us -> 2.93 us  [body(): lax.dot_general(flat(grad_out), w_out, (((1,), (1,)), ((), ())), preferre...]
    pallas_call x5 -> x6, Pallas kernels: 47.5 us -> 47.3 us  [call_kernel(): pl.pallas_call(kernel, in_specs=[pl.BlockSpec(memory_space=space) for spa...]
  transfers between devices with their start and end apart: 12 -> 12, of which waited for: 3 -> 3; matrix products, arithmetic and copies ran while one was open for 11% -> 10% of each run, Pallas kernels for 50% -> 50%
where the time goes in v5:
time: 94.4 us; the launch traced here: 94.3 us
  Pallas kernels  47.3 us (50%)
  starting transfers between devices  25 us (26%)
  waiting for transfers between devices  7.12 us (8%)
  matrix products  6.84 us (7%)
  local copies, waits for them, and re-layouts  4.33 us (5%)
  other arithmetic  2.65 us (3%)
  between operations  1.04 us (1%)
    pallas_call x6, Pallas kernels, call_kernel(): pl.pallas_call(kernel, in_specs=[pl.BlockSpec(memory_space=space) for spa...  47.3 us
    ppermute x12, starting transfers between devices, shifted(): lax.ppermute(value, axis, [(i, (i + step) % count) for i in range(count)])  25 us
    ppermute x12, waiting for transfers between devices, shifted(): lax.ppermute(value, axis, [(i, (i + step) % count) for i in range(count)])  7.12 us
    dot_general x2, matrix products, project(): jnp.dot(x, w, preferred_element_type=jnp.float32).astype(jnp.bfloat16)  3.91 us
    dot_general x1, matrix products, body(): lax.dot_general(flat(grad_out), w_out, (((1,), (1,)), ((), ())), preferre...  2.93 us
  transfers between devices with their start and end apart: 12, of which 3 were waited for; matrix products, arithmetic and copies ran while one was open for 10% of the time, Pallas kernels for 50%

profile of v5, /device:TPU:7, one launch (start us, length us, event | category | flops | bytes accessed | tf_op | source)
XLA Modules:
  0.0 94.3 jit_solution(2427048692135416968)
XLA Ops:
  0.6 0.0 copy-start
  0.6 1.2 %fusion.25 = (bf16[7,16,1152]{2,1,0:T(8,128)(2,1)S(1)}, bf16[7,16,1152]{2,1,0:T(8,128)(2,1)S(1)}) fusion(bf16[16,16,1152]{2,1,0:T(8,128)(2,1)} %param.6), kind=kLoop, calls=%fused_computation.68 | loop fusion | bytes 1032192 | tf_op jit(solution)/shard_map/slice | solution.py:29
  1.8 6.5 %collective-permute-start.1 = (bf16[7,16,1152]{2,1,0:T(8,128)(2,1)S(1)}, bf16[7,16,1152]{2,1,0:T(8,128)(2,1)S(1)}, u32[]{:S(2)}, u32[]{:S(2)}) collective-permute-start(bf16[7,16,1152]{2,1,0:T(8,128)(2,1)S(1)} %get-tuple-element.70), channel_id=1, source_target_pairs={{0,112},{16,0},{32,16},{48,32},{64,48},{80,64},{96,80},{112,96},{1... | collective-permute-start | bytes 774152 | tf_op jit(solution)/shard_map/ppermute | solution.py:25
  8.3 0.0 collective-permute-start
  8.4 1.1 %fusion.24 = (bf16[16,8,1152]{2,1,0:T(8,128)(2,1)S(1)}, bf16[16,8,1152]{2,1,0:T(8,128)(2,1)S(1)}) fusion(bf16[16,16,1152]{2,1,0:T(8,128)(2,1)} %param.6), kind=kLoop, calls=%fused_computation.67 | loop fusion | bytes 1179648 | tf_op jit(solution)/shard_map/slice | solution.py:34
  9.5 0.0 copy-start.1
  9.5 0.1 pad.25.clone
  9.6 2.9 %convolution_convert_fusion.cotangents = bf16[256,1152]{1,0:T(8,128)(2,1)S(1)} fusion(bf16[256,1152]{1,0:T(8,128)(2,1)S(1)} %bitcast.18, bf16[1152,1152]{1,0:T(8,128)(2,1)} %wo_ref.1), kind=kOutput, calls=%fused_computation | convolution fusion | flops 679772160 | bytes 3833856 | tf_op jit(solution)/shard_map/dot_general | solution.py:404
  12.5 0.0 slice-start.1
  12.5 2.9 %convolution_convert_fusion.2.queries = bf16[256,1152]{1,0:T(8,128)(2,1)S(1)} fusion(bf16[256,1152]{1,0:T(8,128)(2,1)S(1)} %bitcast.24, bf16[1152,3456]{1,0:T(8,128)(2,1)} %w_ref.3), kind=kOutput, calls=%fused_computation.2 | convolution fusion | flops 679772160 | bytes 3833856 | tf_op jit(solution)/shard_map/dot_general | solution.py:391
  15.5 0.0 copy-start.2
  15.5 0.4 both_turned.1
  15.9 0.7 and_select_fusion.bias
  16.7 1.0 %convolution_convert_fusion.1.queries = bf16[256,1152]{1,0:T(8,128)(2,1)S(1)} fusion(bf16[256,1152]{1,0:T(8,128)(2,1)S(1)} %bitcast.26, bf16[1152,3456]{1,0:T(8,128)(2,1)S(1)} %bitcast.20), kind=kOutput, calls=%fused_computation.1 | convolution fusion | flops 679772160 | bytes 3833856 | tf_op jit(solution)/shard_map/dot_general | solution.py:391
  17.7 0.0 collective-permute-done.1
  17.7 2.0 %collective-permute-done = bf16[7,16,1152]{2,1,0:T(8,128)(2,1)S(1)} collective-permute-done((bf16[7,16,1152]{2,1,0:T(8,128)(2,1)S(1)}, bf16[7,16,1152]{2,1,0:T(8,128)(2,1)S(1)}, u32[]{:S(2)}, u32[]{:S(2)}) %collective-permute-start) | collective-permute-done | bytes 258080 | tf_op jit(solution)/shard_map/ppermute | solution.py:25
  19.7 0.2 maximum_maximum_fusion.1
  19.9 2.5 %collective-permute-start.2 = (bf16[32,8,1152]{2,1,0:T(8,128)(2,1)S(1)}, bf16[32,8,1152]{2,1,0:T(8,128)(2,1)S(1)}, u32[]{:S(2)}, u32[]{:S(2)}) collective-permute-start(bf16[32,8,1152]{2,1,0:T(8,128)(2,1)S(1)} %get-tuple-element.32), channel_id=1, source_target_pairs={{0,1},{1,2},{2,3},{3,4},{4,5},{5,6},{6,7},{7,8},{8,9},{9,10},{10,1... | collective-permute-start | bytes 1769480 | tf_op jit(solution)/shard_map/ppermute | solution.py:25
  22.5 0.0 collective-permute-start.3
  22.5 3.3 %own_keys.2.kv_own = bf16[512,2304]{1,0:T(8,128)(2,1)S(1)} custom-call(bf16[112,1152]{1,0:T(8,128)(2,1)S(1)} %bitcast.32, bf16[256,1152]{1,0:T(8,128)(2,1)S(1)} %bitcast.25, bf16[112,1152]{1,0:T(8,128)(2,1)S(1)} %bitcast.31, bf16[1152,3456]{1,0:T(8,128)(2,1)S(1)} %bitcast.20), custom_call_target="tpu_custom_call" | custom-call | flops 2717908992 | bytes 16777216 | tf_op jit(solution)/shard_map/own_keys/pallas_call | solution.py:305
  25.8 2.8 %collective-permute-start.7 = (bf16[7,16,1152]{2,1,0:T(8,128)(2,1)S(1)}, bf16[7,16,1152]{2,1,0:T(8,128)(2,1)S(1)}, u32[]{:S(2)}, u32[]{:S(2)}) collective-permute-start(bf16[7,16,1152]{2,1,0:T(8,128)(2,1)S(1)} %get-tuple-element.66), channel_id=1, source_target_pairs={{0,112},{16,0},{32,16},{48,32},{64,48},{80,64},{96,80},{112,96},{1... | collective-permute-start | bytes 774152 | tf_op jit(solution)/shard_map/ppermute | solution.py:25
  28.6 0.3 collective-permute-start.6
  28.9 0.4 collective-permute-done.2
  29.3 4.7 %collective-permute-done.3 = bf16[32,8,1152]{2,1,0:T(8,128)(2,1)S(1)} collective-permute-done((bf16[32,8,1152]{2,1,0:T(8,128)(2,1)S(1)}, bf16[32,8,1152]{2,1,0:T(8,128)(2,1)S(1)}, u32[]{:S(2)}, u32[]{:S(2)}) %collective-permute-start.3) | collective-permute-done | bytes 589856 | tf_op jit(solution)/shard_map/ppermute | solution.py:25
  34.0 0.1 pad_maximum_fusion
  34.1 0.0 slice-start.2
  34.1 0.0 slice-start.3
  34.1 22.2 %attention_backward.1 = (bf16[2304,512]{1,0:T(8,128)(2,1)S(1)}, bf16[256,1152]{1,0:T(8,128)(2,1)S(1)}, bf16[512,1152]{1,0:T(8,128)(2,1)S(1)}) custom-call(bf16[512,2304]{1,0:T(8,128)(2,1)S(1)} %own_keys.2.kv_own, bf16[512,1152]{1,0:T(8,128)(2,1)S(1)} %bitcast.29, bf16[1152,3456]{1,0:T(8,128)(2,1)} %w_ref.3, ...), custom_call_target="tpu_custom_call" | custom-call | flops 16173236224 | bytes 16777216 | tf_op jit(solution)/shard_map/attention_backward/pallas_call | solution.py:305
  56.3 0.1 fusion.21
  56.4 0.1 collective-permute-start.5
  56.5 3.8 %collective-permute-start.4 = (bf16[32,8,1152]{2,1,0:T(8,128)(2,1)S(1)}, bf16[32,8,1152]{2,1,0:T(8,128)(2,1)S(1)}, u32[]{:S(2)}, u32[]{:S(2)}) collective-permute-start(bf16[32,8,1152]{2,1,0:T(8,128)(2,1)S(1)} %get-tuple-element.63), channel_id=1, source_target_pairs={{0,1},{1,2},{2,3},{3,4},{4,5},{5,6},{6,7},{7,8},{8,9},{9,10},{10,1... | collective-permute-start | bytes 1769480 | tf_op jit(solution)/shard_map/ppermute | solution.py:25
  60.3 3.8 %own_gradient.1 = f32[512,1152]{1,0:T(8,128)S(1)} custom-call(bf16[2304,512]{1,0:T(8,128)(2,1)S(1)} %get-tuple-element.44.dkv, bf16[256,1152]{1,0:T(8,128)(2,1)S(1)} %get-tuple-element.45.dq, bf16[1152,3456]{1,0:T(8,128)(2,1)S(1)} %bitcast.22), custom_call_target="tpu_custom_call" | custom-call | flops 2717908992 | bytes 16777216 | tf_op jit(solution)/shard_map/own_gradient/pallas_call | solution.py:305
  64.2 0.0 collective-permute-done.7
  64.2 0.0 collective-permute-done.6
  64.3 0.2 maximum_maximum_fusion.3
  64.5 0.1 collective-permute-start.9
  64.6 3.8 %collective-permute-start.8 = (bf16[32,8,1152]{2,1,0:T(8,128)(2,1)S(1)}, bf16[32,8,1152]{2,1,0:T(8,128)(2,1)S(1)}, u32[]{:S(2)}, u32[]{:S(2)}) collective-permute-start(bf16[32,8,1152]{2,1,0:T(8,128)(2,1)S(1)} %get-tuple-element.81), channel_id=1, source_target_pairs={{0,1},{1,2},{2,3},{3,4},{4,5},{5,6},{6,7},{7,8},{8,9},{9,10},{10,1... | collective-permute-start | bytes 1769480 | tf_op jit(solution)/shard_map/ppermute | solution.py:25
  68.5 3.3 %own_keys.3.kv_own = bf16[512,2304]{1,0:T(8,128)(2,1)S(1)} custom-call(bf16[112,1152]{1,0:T(8,128)(2,1)S(1)} %bitcast.34, bf16[256,1152]{1,0:T(8,128)(2,1)S(1)} %bitcast.27, bf16[112,1152]{1,0:T(8,128)(2,1)S(1)} %bitcast.33, bf16[1152,3456]{1,0:T(8,128)(2,1)S(1)} %bitcast.22), custom_call_target="tpu_custom_call" | custom-call | flops 2717908992 | bytes 16777216 | tf_op jit(solution)/shard_map/own_keys/pallas_call | solution.py:305
  71.8 0.0 collective-permute-done.4
  71.8 0.3 fusion.19
  72.1 2.8 %collective-permute-start.10 = (bf16[7,16,1152]{2,1,0:T(8,128)(2,1)S(1)}, bf16[7,16,1152]{2,1,0:T(8,128)(2,1)S(1)}, u32[]{:S(2)}, u32[]{:S(2)}) collective-permute-start(bf16[7,16,1152]{2,1,0:T(8,128)(2,1)S(1)} %get-tuple-element.60), channel_id=1, source_target_pairs={{0,16},{16,32},{32,48},{48,64},{64,80},{80,96},{96,112},{112,0},{1... | collective-permute-start | bytes 774152 | tf_op jit(solution)/shard_map/ppermute | solution.py:25
  74.9 2.4 %collective-permute-start.11 = (bf16[7,16,1152]{2,1,0:T(8,128)(2,1)S(1)}, bf16[7,16,1152]{2,1,0:T(8,128)(2,1)S(1)}, u32[]{:S(2)}, u32[]{:S(2)}) collective-permute-start(bf16[7,16,1152]{2,1,0:T(8,128)(2,1)S(1)} %get-tuple-element.61), channel_id=1, source_target_pairs={{0,112},{16,0},{32,16},{48,32},{64,48},{80,64},{96,80},{112,96},{1... | collective-permute-start | bytes 774152 | tf_op jit(solution)/shard_map/ppermute | solution.py:25
  77.3 0.1 slice.96
  77.4 0.0 collective-permute-done.8
  77.4 0.1 pad_maximum_fusion.1
  77.5 1.5 %copy-done.3 = bf16[1152,1152]{1,0:T(8,128)(2,1)S(1)} copy-done((bf16[1152,1152]{1,0:T(8,128)(2,1)S(1)}, bf16[1152,1152]{1,0:T(8,128)(2,1)}, u32[]{:S(2)}) %copy-start.3) | copy-done | bytes 2654232
  79.0 14.3 %attention_forward.1 = bf16[256,1152]{1,0:T(8,128)(2,1)} custom-call(bf16[512,2304]{1,0:T(8,128)(2,1)S(1)} %own_keys.3.kv_own, bf16[512,1152]{1,0:T(8,128)(2,1)S(1)} %bitcast.30, bf16[1152,3456]{1,0:T(8,128)(2,1)} %w_ref.3, bf16[1152,1152]{1,0:T(8,128)(2,1)S(1)} %copy-done.3, bf16[256,1152]{1,0:T(8,128)(2,1)S(1)} %convolution_convert_fusion.1.queries, ...), custom_call_target="tpu_custom_call" | custom-call | flops 7012876288 | bytes 16777216 | tf_op jit(solution)/shard_map/attention_forward/pallas_call | solution.py:305
  93.4 0.9 add_convert_fusion
  (31 shorter events, 0.3 us)
Async XLA Ops:
  0.6 9.0 %copy-start = (bf16[16,16,1152]{2,1,0:T(8,128)(2,1)S(1)}, bf16[16,16,1152]{2,1,0:T(8,128)(2,1)}, u32[]{:S(2)}) copy-start(bf16[16,16,1152]{2,1,0:T(8,128)(2,1)} %param.7) | copy-start | bytes 1769476
  1.8 15.8 %collective-permute-start.1 = (bf16[7,16,1152]{2,1,0:T(8,128)(2,1)S(1)}, bf16[7,16,1152]{2,1,0:T(8,128)(2,1)S(1)}, u32[]{:S(2)}, u32[]{:S(2)}) collective-permute-start(bf16[7,16,1152]{2,1,0:T(8,128)(2,1)S(1)} %get-tuple-element.70), channel_id=1, source_target_pairs={{0,112},{16,0},{32,16},{48,32},{64,48},{80,64},{96,80},{112,96},{1... | collective-permute-start | bytes 774152 | tf_op jit(solution)/shard_map/ppermute | solution.py:25
  8.3 11.4 %collective-permute-start = (bf16[7,16,1152]{2,1,0:T(8,128)(2,1)S(1)}, bf16[7,16,1152]{2,1,0:T(8,128)(2,1)S(1)}, u32[]{:S(2)}, u32[]{:S(2)}) collective-permute-start(bf16[7,16,1152]{2,1,0:T(8,128)(2,1)S(1)} %get-tuple-element.71), channel_id=1, source_target_pairs={{0,16},{16,32},{32,48},{48,64},{64,80},{80,96},{96,112},{112,0},{1... | collective-permute-start | bytes 774152 | tf_op jit(solution)/shard_map/ppermute | solution.py:25
  9.5 3.0 %copy-start.1 = (bf16[16,16,1152]{2,1,0:T(8,128)(2,1)S(1)}, bf16[16,16,1152]{2,1,0:T(8,128)(2,1)}, u32[]{:S(2)}) copy-start(bf16[16,16,1152]{2,1,0:T(8,128)(2,1)} %param.6) | copy-start | bytes 1769476
  9.6 7.0 %slice-start = ((s8[7962624]{0:T(1024)(128)(4,1)}), s8[4194304]{0:T(1024)(128)(4,1)S(1)}, s32[]{:S(2)}) async-start(s8[7962624]{0:T(1024)(128)(4,1)} %bitcast.19), calls=%async_computation | async-start | bytes 8388608
  12.5 4.1 %slice-start.1 = ((s8[7962624]{0:T(1024)(128)(4,1)}), s8[3768320]{0:T(1024)(128)(4,1)S(1)}, s32[]{:S(2)}) async-start(s8[7962624]{0:T(1024)(128)(4,1)} %bitcast.19), calls=%async_computation.1 | async-start | bytes 7536640
  15.5 1.2 %copy-start.2 = (bf16[16,16,1152]{2,1,0:T(8,128)(2,1)S(1)}, bf16[16,16,1152]{2,1,0:T(8,128)(2,1)}, u32[]{:S(2)}) copy-start(bf16[16,16,1152]{2,1,0:T(8,128)(2,1)} %param.5) | copy-start | bytes 1769476
  19.9 9.4 %collective-permute-start.2 = (bf16[32,8,1152]{2,1,0:T(8,128)(2,1)S(1)}, bf16[32,8,1152]{2,1,0:T(8,128)(2,1)S(1)}, u32[]{:S(2)}, u32[]{:S(2)}) collective-permute-start(bf16[32,8,1152]{2,1,0:T(8,128)(2,1)S(1)} %get-tuple-element.32), channel_id=1, source_target_pairs={{0,1},{1,2},{2,3},{3,4},{4,5},{5,6},{6,7},{7,8},{8,9},{9,10},{10,1... | collective-permute-start | bytes 1769480 | tf_op jit(solution)/shard_map/ppermute | solution.py:25
  22.5 11.5 %collective-permute-start.3 = (bf16[32,8,1152]{2,1,0:T(8,128)(2,1)S(1)}, bf16[32,8,1152]{2,1,0:T(8,128)(2,1)S(1)}, u32[]{:S(2)}, u32[]{:S(2)}) collective-permute-start(bf16[32,8,1152]{2,1,0:T(8,128)(2,1)S(1)} %get-tuple-element.33), channel_id=1, source_target_pairs={{0,15},{1,0},{2,1},{3,2},{4,3},{5,4},{6,5},{7,6},{8,7},{9,8},{10,9... | collective-permute-start | bytes 1769480 | tf_op jit(solution)/shard_map/ppermute | solution.py:25
  25.8 38.4 %collective-permute-start.7 = (bf16[7,16,1152]{2,1,0:T(8,128)(2,1)S(1)}, bf16[7,16,1152]{2,1,0:T(8,128)(2,1)S(1)}, u32[]{:S(2)}, u32[]{:S(2)}) collective-permute-start(bf16[7,16,1152]{2,1,0:T(8,128)(2,1)S(1)} %get-tuple-element.66), channel_id=1, source_target_pairs={{0,112},{16,0},{32,16},{48,32},{64,48},{80,64},{96,80},{112,96},{1... | collective-permute-start | bytes 774152 | tf_op jit(solution)/shard_map/ppermute | solution.py:25
  28.6 35.6 %collective-permute-start.6 = (bf16[7,16,1152]{2,1,0:T(8,128)(2,1)S(1)}, bf16[7,16,1152]{2,1,0:T(8,128)(2,1)S(1)}, u32[]{:S(2)}, u32[]{:S(2)}) collective-permute-start(bf16[7,16,1152]{2,1,0:T(8,128)(2,1)S(1)} %get-tuple-element.67), channel_id=1, source_target_pairs={{0,16},{16,32},{32,48},{48,64},{64,80},{80,96},{96,112},{112,0},{1... | collective-permute-start | bytes 774152 | tf_op jit(solution)/shard_map/ppermute | solution.py:25
  34.1 26.3 %slice-start.2 = ((s8[7962624]{0:T(1024)(128)(4,1)}), s8[4194304]{0:T(1024)(128)(4,1)S(1)}, s32[]{:S(2)}) async-start(s8[7962624]{0:T(1024)(128)(4,1)} %bitcast.21), calls=%async_computation.2 | async-start | bytes 8388608
  34.1 26.3 %slice-start.3 = ((s8[7962624]{0:T(1024)(128)(4,1)}), s8[3768320]{0:T(1024)(128)(4,1)S(1)}, s32[]{:S(2)}) async-start(s8[7962624]{0:T(1024)(128)(4,1)} %bitcast.21), calls=%async_computation.3 | async-start | bytes 7536640
  56.4 15.3 %collective-permute-start.5 = (bf16[32,8,1152]{2,1,0:T(8,128)(2,1)S(1)}, bf16[32,8,1152]{2,1,0:T(8,128)(2,1)S(1)}, u32[]{:S(2)}, u32[]{:S(2)}) collective-permute-start(bf16[32,8,1152]{2,1,0:T(8,128)(2,1)S(1)} %get-tuple-element.62), channel_id=1, source_target_pairs={{0,15},{1,0},{2,1},{3,2},{4,3},{5,4},{6,5},{7,6},{8,7},{9,8},{10,9... | collective-permute-start | bytes 1769480 | tf_op jit(solution)/shard_map/ppermute | solution.py:25
  56.5 15.3 %collective-permute-start.4 = (bf16[32,8,1152]{2,1,0:T(8,128)(2,1)S(1)}, bf16[32,8,1152]{2,1,0:T(8,128)(2,1)S(1)}, u32[]{:S(2)}, u32[]{:S(2)}) collective-permute-start(bf16[32,8,1152]{2,1,0:T(8,128)(2,1)S(1)} %get-tuple-element.63), channel_id=1, source_target_pairs={{0,1},{1,2},{2,3},{3,4},{4,5},{5,6},{6,7},{7,8},{8,9},{9,10},{10,1... | collective-permute-start | bytes 1769480 | tf_op jit(solution)/shard_map/ppermute | solution.py:25
  64.5 12.8 %collective-permute-start.9 = (bf16[32,8,1152]{2,1,0:T(8,128)(2,1)S(1)}, bf16[32,8,1152]{2,1,0:T(8,128)(2,1)S(1)}, u32[]{:S(2)}, u32[]{:S(2)}) collective-permute-start(bf16[32,8,1152]{2,1,0:T(8,128)(2,1)S(1)} %get-tuple-element.80), channel_id=1, source_target_pairs={{0,15},{1,0},{2,1},{3,2},{4,3},{5,4},{6,5},{7,6},{8,7},{9,8},{10,9... | collective-permute-start | bytes 1769480 | tf_op jit(solution)/shard_map/ppermute | solution.py:25
  64.6 12.8 %collective-permute-start.8 = (bf16[32,8,1152]{2,1,0:T(8,128)(2,1)S(1)}, bf16[32,8,1152]{2,1,0:T(8,128)(2,1)S(1)}, u32[]{:S(2)}, u32[]{:S(2)}) collective-permute-start(bf16[32,8,1152]{2,1,0:T(8,128)(2,1)S(1)} %get-tuple-element.81), channel_id=1, source_target_pairs={{0,1},{1,2},{2,3},{3,4},{4,5},{5,6},{6,7},{7,8},{8,9},{9,10},{10,1... | collective-permute-start | bytes 1769480 | tf_op jit(solution)/shard_map/ppermute | solution.py:25
  72.1 21.2 %collective-permute-start.10 = (bf16[7,16,1152]{2,1,0:T(8,128)(2,1)S(1)}, bf16[7,16,1152]{2,1,0:T(8,128)(2,1)S(1)}, u32[]{:S(2)}, u32[]{:S(2)}) collective-permute-start(bf16[7,16,1152]{2,1,0:T(8,128)(2,1)S(1)} %get-tuple-element.60), channel_id=1, source_target_pairs={{0,16},{16,32},{32,48},{48,64},{64,80},{80,96},{96,112},{112,0},{1... | collective-permute-start | bytes 774152 | tf_op jit(solution)/shard_map/ppermute | solution.py:25
  74.9 18.5 %collective-permute-start.11 = (bf16[7,16,1152]{2,1,0:T(8,128)(2,1)S(1)}, bf16[7,16,1152]{2,1,0:T(8,128)(2,1)S(1)}, u32[]{:S(2)}, u32[]{:S(2)}) collective-permute-start(bf16[7,16,1152]{2,1,0:T(8,128)(2,1)S(1)} %get-tuple-element.61), channel_id=1, source_target_pairs={{0,112},{16,0},{32,16},{48,32},{64,48},{80,64},{96,80},{112,96},{1... | collective-permute-start | bytes 774152 | tf_op jit(solution)/shard_map/ppermute | solution.py:25
  77.3 1.7 %copy-start.3 = (bf16[1152,1152]{1,0:T(8,128)(2,1)S(1)}, bf16[1152,1152]{1,0:T(8,128)(2,1)}, u32[]{:S(2)}) copy-start(bf16[1152,1152]{1,0:T(8,128)(2,1)} %wo_ref.1) | copy-start | bytes 7962628
